TPU v7x, 32 devices: a whole 2x2x4 slice. The times are simulated.
32 devices in a mesh: grp: 4 (over z), seq: 8 (over y, x, core).
Axes of the slice: x: 2, y: 2, z: 4, core: 2. Of those that a mesh axis runs over, the one named last changes fastest.
Arguments:
- queries: bfloat16 [32, 4, 64, 576], P('grp'), parts along dimension 0, may hold values from -190 to 190
- latent_cache: bfloat16 [32, 8192, 576], P('grp', 'seq'), parts along dimension 0, may hold values from -4 to 4
- context_lengths: int32 [32], P('grp'), parts along dimension 0, may hold values from 2048 to 8192, as said below
- value_up: bfloat16 [64, 512, 128], P('seq'), may hold values from -0.5 to 0.5
- output_projection_rows: bfloat16 [8192, 7168], P('seq'), may hold values from -0.25 to 0.25
Outputs:
- attention_out: bfloat16 [32, 4, 7168], P('grp', None, 'seq'), parts along dimension 0
There are 4 independent parts, one for each index of `grp`. A program takes and returns all parts, laid end to end along the dimension named above; an argument that names none is the same for every part. Nothing has to cross between parts.
Inputs may be any that keep to these rules, and one draw needn't show every extreme that they name: `context_lengths`: in every draw one request holds exactly 8192 tokens.
All inputs are finite; a program needn't handle non-finite values.
Results may differ from a plain program's by a relative error of at most 0.0058.
Values sent between devices are 32-bit elements; how exact they have to be, the bound alone decides.
No kernel may reach another device: no remote copies, remote signals or barrier semaphores. Data moves between devices by JAX's collectives and lax.ppermute only.
A program may use at most 128 MiB of HBM per device.

v0:
```python
import jax
import jax.numpy as jnp
from jax import lax
from jax.sharding import PartitionSpec as P

score_scale = 0.07216878364870323
empty_mark = -1e30


def shard_partial(queries, cache_rows, context_lengths, first_token, latent_width):
    query_count = queries.shape[1]
    shard_width = cache_rows.shape[1]
    scores = (
        jnp.einsum("bqhc,btc->bqht", queries, cache_rows, preferred_element_type=jnp.float32)
        * score_scale
    )
    position = first_token + jnp.arange(shard_width, dtype=jnp.int32)
    row_limit = (
        context_lengths[:, None]
        - (query_count - 1)
        + jnp.arange(query_count, dtype=jnp.int32)[None, :]
    )
    visible = position[None, None, None, :] < row_limit[:, :, None, None]
    masked = jnp.where(visible, scores, empty_mark)
    row_peak = jnp.max(masked, axis=3)
    weights = jnp.where(visible, jnp.exp(masked - row_peak[..., None]), 0.0)
    row_rescale = jnp.maximum(jnp.sum(weights, axis=3), 1.0)
    values = jnp.einsum(
        "bqht,btc->bqhc",
        weights.astype(jnp.bfloat16),
        cache_rows[:, :, :latent_width],
        preferred_element_type=jnp.float32,
    )
    return (values / row_rescale[..., None], row_peak + jnp.log(row_rescale))


def combine_all(partials, log_sums):
    greatest_score = jnp.max(log_sums, axis=0)
    shares = jnp.exp(log_sums - greatest_score[None])
    return jnp.sum(shares[..., None] * partials, axis=0) / jnp.sum(shares, axis=0)[..., None]


def project_heads(attended, value_up, output_projection_rows):
    attended_low = attended.astype(jnp.bfloat16)
    head_out = jnp.einsum(
        "bqhc,hcv->bqhv", attended_low, value_up, preferred_element_type=jnp.float32
    ).astype(jnp.bfloat16)
    flattened_heads = head_out.reshape(head_out.shape[0], head_out.shape[1], -1)
    return jnp.einsum(
        "msp,pc->msc", flattened_heads, output_projection_rows, preferred_element_type=jnp.float32
    )


def local(queries, latent_cache, context_lengths, value_up, output_projection_rows):
    latent_width = value_up.shape[1]
    first_token = lax.axis_index("seq") * latent_cache.shape[1]
    partials, log_sums = shard_partial(
        queries, latent_cache, context_lengths, first_token, latent_width
    )
    term = project_heads(
        combine_all(
            lax.all_to_all(partials[None], "seq", split_axis=3, concat_axis=0, tiled=True),
            lax.all_to_all(log_sums[None], "seq", split_axis=3, concat_axis=0, tiled=True),
        ),
        value_up,
        output_projection_rows,
    )
    return lax.psum_scatter(term, "seq", scatter_dimension=2, tiled=True).astype(jnp.bfloat16)


def solution(mesh):
    placed = (
        P("grp", None, None, None),
        P("grp", "seq", None),
        P("grp"),
        P("seq", None, None),
        P("seq", None),
    )
    return jax.shard_map(
        local, mesh=mesh, in_specs=placed, out_specs=P("grp", None, "seq"), check_vma=False
    )
```

profile of v0, /device:TPU:0, one launch (start us, length us, event | category | flops | bytes accessed | tf_op | source)
XLA Modules:
  0.0 156.5 jit_solution(8409263443172818239)
XLA Ops:
  6.5 0.0 copy-start
  6.5 0.8 broadcast_add_fusion
  7.3 0.1 iota_add_fusion
  7.4 0.1 broadcast_compare_fusion
  7.5 0.8 copy-done
  8.3 6.3 %fusion.7 = (f32[8,4,64]{2,1,0:T(4,128)S(1)}, f32[8,4,64,1024]{3,2,1,0:T(8,128)S(1)}) fusion(pred[8,4,1024]{2,1,0:T(4,128)(4,1)S(1)} %broadcast_compare_fusion, bf16[8,4,64,576]{3,2,1,0:T(8,128)(2,1)S(1)} %copy-done, bf16[8,1024,576]{1,2,0:T(8,128)(2,1)} %param.6), kind=kOutput, calls=%fused_computation.9 | convolution fusion | flops 2422208512 | bytes 20226048 | tf_op jit(solution)/shard_map/bqhc,btc->bqht/dot_general | solution.py:14
  14.6 0.0 copy-start.1
  14.6 3.2 %copy-done.1 = f32[8,4,64,1024]{3,2,1,0:T(8,128)} copy-done((f32[8,4,64,1024]{3,2,1,0:T(8,128)}, f32[8,4,64,1024]{3,2,1,0:T(8,128)S(1)}, u32[]{:S(2)}) %copy-start.1) | copy-done | bytes 8388632
  17.8 2.8 %fusion.9 = f32[8,4,64]{2,1,0:T(4,128)S(1)} fusion(f32[8,4,64,1024]{3,2,1,0:T(8,128)S(1)} %get-tuple-element.10, f32[8,4,64]{2,1,0:T(4,128)S(1)} %get-tuple-element.9, pred[8,4,1024]{2,1,0:T(4,128)(4,1)S(1)} %broadcast_compare_fusion), kind=kLoop, calls=%fused_computation.11 | loop fusion | flops 10483712 | bytes 8437760 | tf_op jit(solution)/shard_map/reduce_sum | solution.py:27
  20.7 0.1 copy.20
  20.8 0.8 reshape.73
  21.5 5.2 %all-to-all-start = ((f32[8,1,256]{2,1,0:T(1,128)}), f32[8,1,256]{2,1,0:T(1,128)S(1)}, u32[]{:S(2)}, u32[]{:S(2)}) async-start(f32[8,1,256]{2,1,0:T(1,128)} %reshape.73), calls=%async_computation | async-start | bytes 16384 | tf_op jit(solution)/shard_map/all_to_all | solution.py:63
  26.7 10.7 %divide_bitcast_fusion = f32[1,8,4,64,512]{4,3,2,1,0:T(8,128)} fusion(f32[8,4,64]{2,1,0:T(4,128)S(1)} %get-tuple-element.8, bf16[8,1024,576]{1,2,0:T(8,128)(2,1)} %param.6, f32[8,4,64,1024]{3,2,1,0:T(8,128)} %copy-done.1, f32[8,4,64]{2,1,0:T(4,128)S(1)} %get-tuple-element.9, pred[8,4,1024]{2,1,0:T(4,128)(4,1)S(1)} %broadcast_compare_fusion), kind=kOutput, calls=%fused_computation.14 | convolution fusion | flops 2159017984 | bytes 21020672 | tf_op jit(solution)/shard_map/bqht,btc->bqhc/dot_general | solution.py:28
  37.4 6.8 %copy.23 = f32[1,8,4,64,512]{4,2,1,0,3:T(4,128)} copy(f32[1,8,4,64,512]{4,3,2,1,0:T(8,128)} %divide_bitcast_fusion) | data formatting | bytes 8388608 | tf_op jit(solution)/shard_map/broadcast_in_dim | solution.py:62
  44.2 0.0 all-to-all-done
  44.2 4.5 %all-to-all-start.1 = ((f32[1,8,4,64,512]{4,2,1,0,3:T(4,128)}), f32[1,8,4,64,512]{4,2,1,0,3:T(4,128)}, u32[]{:S(2)}, u32[]{:S(2)}) async-start(f32[1,8,4,64,512]{4,2,1,0,3:T(4,128)} %copy.23), calls=%async_computation.1 | async-start | bytes 8388608 | tf_op jit(solution)/shard_map/all_to_all | solution.py:62
  48.7 0.2 reduce-scatter.2.cloned.1.call-start
  49.0 0.5 broadcast.57
  49.5 0.7 reduce.1
  50.2 0.2 reshape.74
  50.4 0.2 copy.21
  50.5 0.1 bitcast_reduce_fusion
  50.6 0.1 fusion.30
  50.6 47.2 %all-to-all-done.1 = f32[1,8,4,64,512]{4,2,1,0,3:T(4,128)} async-done(((f32[1,8,4,64,512]{4,2,1,0,3:T(4,128)}), f32[1,8,4,64,512]{4,2,1,0,3:T(4,128)}, u32[]{:S(2)}, u32[]{:S(2)}) %all-to-all-start.1) | async-done | bytes 4194336 | tf_op jit(solution)/shard_map/all_to_all | solution.py:62
  97.9 4.8 %fusion.11 = f32[8,4,8,512]{3,2,1,0:T(8,128)S(1)} fusion(f32[1,8,4,8,8,512]{5,2,1,4,3,0:T(4,128)} %bitcast.9, f32[8,8,4,8]{3,0,2,1:T(8,128)S(1)} %get-tuple-element.6), kind=kLoop, calls=%fused_computation.13 | loop fusion | flops 1966080 | bytes 4726784 | tf_op jit(solution)/shard_map/reduce_sum | solution.py:40
  102.7 0.1 divide_convert_fusion
  102.8 1.6 %fusion.17 = bf16[8,4,1,8,128]{4,3,2,1,0:T(8,128)(2,1)S(1)} fusion(bf16[8,512,128]{2,1,0:T(8,128)(2,1)} %param.8, bf16[8,4,8,512]{3,2,1,0:T(8,128)(2,1)S(1)} %divide_convert_fusion), kind=kOutput, calls=%fused_computation.21 | convolution fusion | flops 33587200 | bytes 1376256 | tf_op jit(solution)/shard_map/bqhc,hcv->bqhv/dot_general | solution.py:45
  104.4 8.6 %fusion = f32[8,4,7168]{2,0,1:T(8,128)} fusion(bf16[1024,7168]{1,0:T(8,128)(2,1)} %param.9, bf16[8,4,1,8,128]{4,3,2,1,0:T(8,128)(2,1)S(1)} %fusion.17), kind=kOutput, calls=%fused_computation | convolution fusion | flops 469762048 | bytes 15663104 | tf_op jit(solution)/shard_map/msp,pc->msc/dot_general | solution.py:49
  113.0 0.0 reduce-scatter.2.cloned.1.call-update
  113.1 35.1 %reduce-scatter.2.cloned.1.call-done = f32[8,4,896]{2,0,1:T(8,128)} async-done(((f32[8,4,7168]{2,0,1:T(8,128)}), f32[8,4,896]{2,0,1:T(8,128)}) %reduce-scatter.2.cloned.1.call-update) | async-done | bytes 114704 | tf_op jit(solution)/shard_map/reduce_scatter | solution.py:68
  148.1 0.9 convert_element_type.19
  149.0 0.6 copy.27
  (2 shorter events, 0.0 us)
Async XLA Ops:
  6.5 1.8 %copy-start = (bf16[8,4,64,576]{3,2,1,0:T(8,128)(2,1)S(1)}, bf16[8,4,64,576]{3,2,1,0:T(8,128)(2,1)}, u32[]{:S(2)}) copy-start(bf16[8,4,64,576]{3,2,1,0:T(8,128)(2,1)} %param.5) | copy-start | bytes 7077892
  14.6 3.2 %copy-start.1 = (f32[8,4,64,1024]{3,2,1,0:T(8,128)}, f32[8,4,64,1024]{3,2,1,0:T(8,128)S(1)}, u32[]{:S(2)}) copy-start(f32[8,4,64,1024]{3,2,1,0:T(8,128)S(1)} %get-tuple-element.10) | copy-start | bytes 25165828
  21.5 22.6 %all-to-all-start = ((f32[8,1,256]{2,1,0:T(1,128)}), f32[8,1,256]{2,1,0:T(1,128)S(1)}, u32[]{:S(2)}, u32[]{:S(2)}) async-start(f32[8,1,256]{2,1,0:T(1,128)} %reshape.73), calls=%async_computation | async-start | bytes 16384 | tf_op jit(solution)/shard_map/all_to_all | solution.py:63
  44.2 53.7 %all-to-all-start.1 = ((f32[1,8,4,64,512]{4,2,1,0,3:T(4,128)}), f32[1,8,4,64,512]{4,2,1,0,3:T(4,128)}, u32[]{:S(2)}, u32[]{:S(2)}) async-start(f32[1,8,4,64,512]{4,2,1,0,3:T(4,128)} %copy.23), calls=%async_computation.1 | async-start | bytes 8388608 | tf_op jit(solution)/shard_map/all_to_all | solution.py:62
  48.7 99.4 %reduce-scatter.2.cloned.1.call-start = ((), (), s32[]{:S(2)}) async-start(), calls=%async_computation.3 | async-start | bytes 1032192 | tf_op jit(solution)/shard_map/reduce_scatter | solution.py:68
Sparse Core Ops, SparseCore 0:
  113.2 34.9 reduce-scatter.1
where the time goes:
time: 157 us
  waiting for transfers between devices  82.3 us (52%)
  matrix products  27.2 us (17%)
  between operations  13.5 us (9%)
  local copies, waits for them, and re-layouts  13.2 us (8%)
  other arithmetic  10.4 us (7%)
  starting transfers between devices  9.94 us (6%)
    all_to_all x1, waiting for transfers between devices, local(): lax.all_to_all(partials[None], 'seq', split_axis=3, concat_axis=0, tiled=...  47.2 us
    reduce_scatter x1, waiting for transfers between devices, local(): lax.psum_scatter(term, 'seq', scatter_dimension=2, tiled=True)  35.1 us
    dot_general x1, matrix products, shard_partial(): jnp.einsum('bqht,btc->bqhc', weights.astype(jnp.bfloat16), cache_rows[:,...  10.7 us
    dot_general x1, matrix products, project_heads(): jnp.einsum('msp,pc->msc', flattened_heads, output_projection_rows, prefer...  8.63 us
    broadcast_in_dim x1, local copies, waits for them, and re-layouts, local(): partials[None]  6.81 us
    dot_general x1, matrix products, shard_partial(): jnp.einsum('bqhc,btc->bqht', queries, cache_rows, preferred_element_type=...  6.31 us
    all_to_all x1, starting transfers between devices, local(): lax.all_to_all(log_sums[None], 'seq', split_axis=3, concat_axis=0, tiled=...  5.17 us
    unnamed x6, local copies, waits for them, and re-layouts  4.94 us
  transfers between devices with their start and end apart: 3, of which 2 were waited for; matrix products, arithmetic and copies ran while one was open for 12% of the time, Pallas kernels for 0%

commit v1 on v0

v1 whole, which is shorter than its diff:
```python
import functools
import math

import jax
import jax.numpy as jnp
from jax import lax
from jax.experimental import pallas as pl
from jax.experimental.pallas import tpu as pltpu
from jax.sharding import PartitionSpec as P

score_scale = 0.07216878364870323
empty_mark = -1e30
MIB = 1024 * 1024
PARTS = (2, 2, 2, 2)
LAST = (50, 50, 0)
DIRECT = ()
ORDER = "A0:10 A1:10 C0:50 A2:10 C1:50 A3:10 C2:50 S0:50 C3:0 S1:0 S2:0 S3:50 M0:5 M1:5 M2:5"
BLOCK = 32
PIECES = 4
TILE = 256
OWN = 8
VM = pl.BlockSpec(memory_space=pltpu.VMEM)
SM = pl.BlockSpec(memory_space=pltpu.SMEM)
HB = pl.BlockSpec(memory_space=pltpu.HBM)
ANY = pl.BlockSpec(memory_space=pl.ANY)


def declared(length):
    return pl.CostEstimate(flops=length * 10**8 + 1, bytes_accessed=1, transcendentals=0)


def group(me, q, mate, turn):
    core = (me & 1) ^ mate ^ turn
    first = 2 + 2 * core
    return me ^ mate ^ ((q >> 1) * first + (q & 1) * (6 - first))


def pairs_of(n, step, turn):
    bits = ((1, 1), (2, 4), (4, 2), (6, 6))[step]
    return [(s, s ^ bits[(s & 1) ^ turn]) for s in range(n)]


def attention_kernel(first, count, turn, ready, following, after, me_ref, lengths_hbm, q_hbm, cache_hbm, *refs):
    q_buf, cache_buf = refs[:2] if ready else refs[-3:-1]
    refs = refs[2 * ready + after :]
    (keep, send), refs = refs[:2], refs[2:]
    targets, refs = refs[: 2 * (following > 0)], refs[2 * (following > 0) :]
    raw_buf, low_buf, acc_buf, lengths, length_sem, next_sems = refs[:6]
    nq, heads, lat = q_hbm.shape[1:]
    rows = nq * heads
    tokens = cache_hbm.shape[2]
    kvr = keep.shape[1]
    me = me_ref[0]
    length_copy = pltpu.make_async_copy(lengths_hbm, lengths, length_sem)
    length_copy.start()
    depth = lat // PIECES

    def copies(i, q_target, cache_target, sems):
        pieces = [slice(k * depth, (k + 1) * depth) for k in range(PIECES)]
        return [
            pltpu.make_async_copy(cache_hbm.at[first + i, piece], cache_target.at[piece], sems.at[k])
            for k, piece in enumerate(pieces)
        ] + [pltpu.make_async_copy(q_hbm.at[first + i], q_target, sems.at[PIECES])]

    ahead = [
        copy
        for i in range(following)
        for copy in copies(count + i, targets[0].at[i], targets[1].at[i], next_sems.at[i])
    ]
    fetches = []
    if not ready:
        fetches = [copies(i, q_buf.at[i], cache_buf.at[i], refs[-1].at[i]) for i in range(count)]
    for copy in sum(fetches, []) or ahead:
        copy.start()
    row = lax.broadcasted_iota(jnp.int32, (BLOCK, 1), 0)
    token = lax.broadcasted_iota(jnp.int32, (BLOCK, tokens), 1)
    lane = lax.broadcasted_iota(jnp.int32, (BLOCK, 128), 1)
    for out in (keep, send):
        out[out.shape[0] - OWN :, :] = jnp.zeros((OWN, kvr), jnp.float32)
    length_copy.wait()

    def score_piece(i, start):
        if fetches and start == 0:
            for copy in fetches[i]:
                copy.wait()
            for copy in ahead if i == 0 else ():
                copy.start()
        columns = slice(start, start + TILE)
        raw_buf[i % 2, :, columns] = jnp.dot(
            q_buf[i].reshape(rows, lat),
            cache_buf[i, :, columns],
            preferred_element_type=jnp.float32,
        )

    scales = {}
    tails = {}

    def weight_piece(i, start):
        block = slice(start, start + BLOCK)
        limit = lengths[first + i] - (nq - 1) - me * tokens + (row + start) // heads
        raw = jnp.where(token < limit, raw_buf[i % 2, block, :], empty_mark)
        peak = jnp.max(raw, axis=1, keepdims=True)
        weights = jnp.exp2((raw - peak) * (score_scale * math.log2(math.e)))
        total = jnp.maximum(jnp.sum(weights, axis=1, keepdims=True), 1.0)
        low_buf[i % 2, block, :] = weights.astype(jnp.bfloat16)
        some = limit > 0
        scales[i, start] = jnp.where(some, 1.0 / total, 0.0)
        lse = jnp.where(some, peak * score_scale + jnp.log(total), empty_mark)
        part = start // 128
        spread = jnp.where(lane + part * 128 == row + start, lse, 0.0)
        tails[i, part] = tails.get((i, part), 0.0) + jnp.sum(spread, axis=0, keepdims=True)

    def value_piece(i, start):
        acc = lax.dot_general(
            low_buf[i % 2],
            cache_buf[i, start : start + TILE, :],
            (((1,), (1,)), ((), ())),
            preferred_element_type=jnp.float32,
        )
        for block in range(0, rows, BLOCK):
            acc_buf[i % 2, block : block + BLOCK, start : start + TILE] = acc[block : block + BLOCK] * scales[i, block]

    def out_piece(i):
        for mate, out in enumerate((keep, send)):
            for q in range(4):
                for j in range(nq):
                    source = pl.multiple_of(j * heads + group(me, q, mate, turn) * OWN, OWN)
                    to = ((q * count + i) * nq + j) * OWN
                    out[to : to + OWN, :] = acc_buf[i % 2, pl.ds(source, OWN), :]
        for part in range(rows // 128):
            for out in (keep, send):
                at = out.shape[0] - OWN + i
                out[at : at + 1, part * 128 : (part + 1) * 128] = tails[i, part]

    def pieces(stage, i):
        if not 0 <= i < count:
            return []
        if stage == 0:
            return [functools.partial(score_piece, i, t) for t in range(0, tokens, TILE)]
        if stage == 1:
            return [functools.partial(weight_piece, i, t) for t in range(0, rows, BLOCK)]
        return [functools.partial(value_piece, i, t) for t in range(0, kvr, TILE)] + [functools.partial(out_piece, i)]

    for i in range(count + 2):
        stages = [pieces(stage, i - stage) for stage in range(3)]
        marked = []
        for stage, own in enumerate(stages):
            marked += [((k + 0.5) / len(own), stage, k, piece) for k, piece in enumerate(own)]
        for _, _, _, piece in sorted(marked, key=lambda entry: entry[:3]):
            piece()
    for copy in ahead:
        copy.wait()


def attention(me, lengths, queries, cache, kvr, first, count, turn, ready, following, after, length):
    batch, nq, heads, lat = queries.shape
    tokens = cache.shape[2]
    rows = nq * heads
    out_rows = count * rows // 2 + OWN
    scratch = [
        pltpu.VMEM((2, rows, tokens), jnp.float32),
        pltpu.VMEM((2, rows, tokens), jnp.bfloat16),
        pltpu.VMEM((2, rows, kvr), jnp.float32),
        pltpu.SMEM((batch,), jnp.int32),
        pltpu.SemaphoreType.DMA,
        pltpu.SemaphoreType.DMA((max(following, 1), PIECES + 1)),
    ]
    if not ready:
        scratch += [
            pltpu.VMEM((count, nq, heads, lat), jnp.bfloat16),
            pltpu.VMEM((count, lat, tokens), jnp.bfloat16),
            pltpu.SemaphoreType.DMA((count, PIECES + 1)),
        ]
    out_shape = [jax.ShapeDtypeStruct((out_rows, kvr), jnp.float32)] * 2
    if following:
        out_shape += [
            jax.ShapeDtypeStruct((following, nq, heads, lat), jnp.bfloat16),
            jax.ShapeDtypeStruct((following, lat, tokens), jnp.bfloat16),
        ]
    return pl.pallas_call(
        functools.partial(attention_kernel, first, count, turn, len(ready) > 0, following, len(after)),
        in_specs=[SM, HB, HB, HB] + [VM] * len(ready) + [ANY] * len(after),
        out_specs=[VM] * len(out_shape),
        out_shape=out_shape,
        scratch_shapes=scratch,
        compiler_params=pltpu.CompilerParams(vmem_limit_bytes=24 * MIB),
        cost_estimate=declared(length),
    )(me, lengths, queries, cache, *ready, *after)


def merged(refs, shares):
    lanes = shares.shape[1]
    logs = [ref[ref.shape[0] - OWN :, :lanes] for ref in refs]
    largest = functools.reduce(jnp.maximum, logs)
    parts = [jnp.exp(log - largest) for log in logs]
    total = sum(parts[1:], parts[0])
    for k, part in enumerate(parts):
        shares[k] = (part / total).T
    return largest + jnp.log(total)


def merged_rows(refs, shares, me, heads, batch, q, b, j, turn):
    at = pl.ds(pl.multiple_of(j * heads + group(me, q, 0, turn) * OWN, OWN), OWN)
    source = ((q * batch + b) * (shares.shape[1] // heads) + j) * OWN
    rows = slice(source, source + OWN)
    terms_of = [shares[k, at, b : b + 1] * ref[rows, :] for k, ref in enumerate(refs)]
    return sum(terms_of[1:], terms_of[0])


def combine_kernel(places, pieces, batch, heads, turn, me_ref, keep_ref, got_ref, *refs):
    *outs, shares = refs[len(refs) - pieces - 1 :]
    lse = merged((keep_ref, got_ref), shares)
    lanes = shares.shape[1]
    size = batch * (lanes // heads) * OWN
    for q in range(places):
        side, at = divmod(q, places // pieces)
        for b in range(batch):
            for j in range(lanes // heads):
                to = at * size + (b * (lanes // heads) + j) * OWN
                outs[side][to : to + OWN, :] = merged_rows(
                    (keep_ref, got_ref), shares, me_ref[0], heads, batch, q, b, j, turn
                )
    for out in outs:
        out[out.shape[0] - OWN :, :] = jnp.zeros((OWN, out.shape[1]), jnp.float32)
        out[out.shape[0] - OWN :, :lanes] = lse


def combine(me, keep, got, places, pieces, batch, heads, lanes, turn, after, length):
    out_rows = (keep.shape[0] - OWN) // pieces + OWN
    return pl.pallas_call(
        functools.partial(combine_kernel, places, pieces, batch, heads, turn),
        in_specs=[SM, VM, VM] + [ANY] * len(after),
        out_specs=[VM] * pieces,
        out_shape=[jax.ShapeDtypeStruct((out_rows, keep.shape[1]), jnp.float32)] * pieces,
        scratch_shapes=[pltpu.VMEM((2, lanes, OWN), jnp.float32)],
        compiler_params=pltpu.CompilerParams(vmem_limit_bytes=16 * MIB),
        cost_estimate=declared(length),
    )(me, keep, got, *after)


def order_kernel(*refs):
    refs[-1][...] = jnp.zeros(refs[-1].shape, jnp.float32)


def order(after, length):
    return pl.pallas_call(
        order_kernel,
        in_specs=[ANY] * len(after),
        out_specs=VM,
        out_shape=jax.ShapeDtypeStruct((OWN, 128), jnp.float32),
        compiler_params=pltpu.CompilerParams(vmem_limit_bytes=MIB),
        cost_estimate=declared(length),
    )(*after)


def attend_rows(batch, heads, me, refs, shares, attended):
    merged(refs, shares)
    positions = shares.shape[1] // heads
    for b in range(batch):
        for j in range(positions):
            to = (b * positions + j) * OWN
            rows = merged_rows(refs, shares, me, heads, batch, 0, b, j, 0)
            for k in range(attended.shape[0]):
                attended[k, to : to + OWN, :] = rows[:, k * 128 : (k + 1) * 128]


def last_merge_kernel(batch, heads, count, me_ref, *refs):
    out_ref, shares = refs[-2:]
    attend_rows(batch, heads, me_ref[0], refs[:count], shares, out_ref)


def last_merge(me, arrays, batch, heads, lanes, after, length):
    rows, kvr = arrays[0].shape
    return pl.pallas_call(
        functools.partial(last_merge_kernel, batch, heads, len(arrays)),
        in_specs=[SM] + [VM] * len(arrays) + [ANY] * len(after),
        out_specs=VM,
        out_shape=jax.ShapeDtypeStruct((kvr // 128, rows - OWN, 128), jnp.float32),
        scratch_shapes=[pltpu.VMEM((len(arrays), lanes, OWN), jnp.float32)],
        compiler_params=pltpu.CompilerParams(vmem_limit_bytes=16 * MIB),
        cost_estimate=declared(length),
    )(me, *arrays, *after)


def heads_kernel(batch, heads, count, me_ref, *refs):
    early, refs = refs[: -count - 4], refs[-count - 4 :]
    arrays, (up_ref, out_ref, shares, attended) = refs[:count], refs[count:]
    attend_rows(batch, heads, me_ref[0], arrays, shares, attended)
    width = up_ref.shape[2]
    for i in range(OWN):
        own = [
            jnp.concatenate([ref[k, pl.ds(i, ref.shape[1] // OWN, stride=OWN), :] for k in range(ref.shape[0])], axis=1)
            for ref in (*early, attended)
        ]
        own = jnp.concatenate(own, axis=0).astype(jnp.bfloat16)
        head_out = jnp.dot(own, up_ref[i], preferred_element_type=jnp.float32)
        out_ref[:, i * width : (i + 1) * width] = head_out.astype(jnp.bfloat16)


def heads_out(me, early, arrays, batch, value_up, heads, lanes):
    rows, kvr = arrays[0].shape
    shape = (kvr // 128, rows - OWN, 128)
    places = sum(array.shape[1] for array in early) // OWN + shape[1] // OWN
    return pl.pallas_call(
        functools.partial(heads_kernel, batch, heads, len(arrays)),
        in_specs=[SM] + [VM] * (len(early) + len(arrays) + 1),
        out_specs=VM,
        out_shape=jax.ShapeDtypeStruct((places, OWN * value_up.shape[2]), jnp.bfloat16),
        scratch_shapes=[pltpu.VMEM((len(arrays), lanes, OWN), jnp.float32), pltpu.VMEM(shape, jnp.float32)],
        compiler_params=pltpu.CompilerParams(vmem_limit_bytes=16 * MIB),
        cost_estimate=declared(0),
    )(me, *early, *arrays, value_up)


def terms_kernel(mate, places, me_ref, heads_ref, weights_ref, *refs):
    out_ref = refs[-1]
    heads = heads_ref[...]
    width = out_ref.shape[2]
    for at, q in enumerate(places):
        start = pl.multiple_of(group(me_ref[0], q, mate, 0) * width, width)
        out_ref[at] = jnp.dot(heads, weights_ref[:, pl.ds(start, width)], preferred_element_type=jnp.float32)


def terms(me, heads, weights, mate, places, width, after, length):
    return pl.pallas_call(
        functools.partial(terms_kernel, mate, places),
        in_specs=[SM, VM, VM] + [ANY] * len(after),
        out_specs=VM,
        out_shape=jax.ShapeDtypeStruct((len(places), heads.shape[0], width), jnp.float32),
        compiler_params=pltpu.CompilerParams(vmem_limit_bytes=20 * MIB),
        cost_estimate=declared(length),
    )(me, heads, weights, *after)


def fold_kernel(own_ref, got_ref, *refs):
    for q, out in enumerate(refs[len(refs) - own_ref.shape[0] :]):
        out[...] = own_ref[q] + got_ref[q]


def fold(own, got, after):
    return pl.pallas_call(
        fold_kernel,
        in_specs=[VM, VM] + [ANY] * len(after),
        out_specs=[VM] * own.shape[0],
        out_shape=[jax.ShapeDtypeStruct(own.shape[1:], jnp.float32)] * own.shape[0],
        compiler_params=pltpu.CompilerParams(vmem_limit_bytes=8 * MIB),
        cost_estimate=declared(0),
    )(own, got, *after)


def finish_kernel(*refs):
    ins, out_ref = refs[:-1], refs[-1]
    batch, nq, _ = out_ref.shape
    total = ins[0][...]
    for ref in ins[1:]:
        total = total + ref[...]
    total = total.astype(jnp.bfloat16)
    for b in range(batch):
        out_ref[b] = total[b * nq : (b + 1) * nq, :]


def finish(terms_of, batch, nq):
    return pl.pallas_call(
        finish_kernel,
        in_specs=[VM] * len(terms_of),
        out_specs=VM,
        out_shape=jax.ShapeDtypeStruct((batch, nq, terms_of[0].shape[1]), jnp.bfloat16),
        compiler_params=pltpu.CompilerParams(vmem_limit_bytes=8 * MIB),
        cost_estimate=declared(0),
    )(*terms_of)


def local(n, queries, latent_cache, context_lengths, value_up, output_projection_rows):
    batch, nq, heads, _ = queries.shape
    kvr = value_up.shape[1]
    lanes = nq * heads
    me = lax.axis_index("seq").astype(jnp.int32).reshape(1)
    queries = pltpu.with_memory_space_constraint(queries, pltpu.HBM)
    cache = pltpu.with_memory_space_constraint(jnp.swapaxes(latent_cache, 1, 2), pltpu.HBM)
    lengths = pltpu.with_memory_space_constraint(context_lengths, pltpu.HBM)

    def swap(array, step, turn=0):
        return lax.ppermute(array, "seq", pairs_of(n, step, turn))

    keep, send, early = {}, {}, {}

    def arrived(p):
        turn = p & 1
        if len(send[p]) == 1:
            return [keep[p], swap(send[p][0], 2, turn)]
        second, first, both = send[p]
        return [keep[p], swap(first, 1, turn), swap(second, 2, turn), swap(both, 3, turn)]

    after, ready = (), ()
    for entry in ORDER.split():
        kind, p, length = entry[0], int(entry[1]), int(entry[3:])
        turn = p & 1
        if kind == "N":
            after = (order(after, length),)
        elif kind == "A":
            following = (*PARTS, 0)[p + 1]
            outs = attention(
                me, lengths, queries, cache, kvr, sum(PARTS[:p]), PARTS[p], turn, ready, following, after, length
            )
            keep[p], send[p], ready = outs[0], outs[1:2], outs[2:]
            after = (keep[p],)
        elif kind == "M":
            early[p] = last_merge(me, arrived(p), PARTS[p], heads, lanes, after, length)
            after = (early[p],)
        else:
            step = "CS".index(kind)
            pieces = 4 if kind == "C" and p in DIRECT else 2
            keep[p], *send[p] = combine(
                me,
                keep[p],
                swap(send[p][0], step, turn),
                4 >> step,
                pieces,
                PARTS[p],
                heads,
                lanes,
                turn,
                after,
                length,
            )
            after = (keep[p],)

    last = len(PARTS) - 1
    flat = heads_out(me, [early[p] for p in range(last)], arrived(last), PARTS[last], value_up, heads, lanes)
    width = output_projection_rows.shape[1] // n
    sums = {}
    after = ()
    for places in ((3, 2), (1, 0)):
        sent = terms(me, flat, output_projection_rows, 1, places, width, after, LAST[0])
        own = terms(me, flat, output_projection_rows, 0, places, width, (sent,), LAST[1])
        after = (order((own,), LAST[2]),) if LAST[2] and after else ()
        folded = fold(own, swap(sent, 0), after)
        sums.update(zip(places, folded))
        after = (folded[0],)
    return finish([sums[0], swap(sums[3], 3), swap(sums[2], 1), swap(sums[1], 2)], batch, nq)


def plain(queries, latent_cache, context_lengths, value_up, output_projection_rows):
    batch, nq = queries.shape[:2]
    kvr = value_up.shape[1]
    tokens = latent_cache.shape[1]
    scores = score_scale * jnp.einsum("bqhc,btc->bqht", queries, latent_cache, preferred_element_type=jnp.float32)
    position = lax.axis_index("seq") * tokens + jnp.arange(tokens, dtype=jnp.int32)
    limit = context_lengths[:, None] - (nq - 1) + jnp.arange(nq, dtype=jnp.int32)[None, :]
    visible = position[None, None, None, :] < limit[:, :, None, None]
    masked = jnp.where(visible, scores, empty_mark)
    peak = jnp.max(masked, axis=3)
    weights = jnp.where(visible, jnp.exp(masked - peak[..., None]), 0.0)
    total = jnp.maximum(jnp.sum(weights, axis=3), 1.0)
    values = jnp.einsum(
        "bqht,btc->bqhc", weights.astype(jnp.bfloat16), latent_cache[:, :, :kvr], preferred_element_type=jnp.float32
    )
    partials = lax.all_to_all((values / total[..., None])[None], "seq", split_axis=3, concat_axis=0, tiled=True)
    lse = lax.all_to_all((peak + jnp.log(total))[None], "seq", split_axis=3, concat_axis=0, tiled=True)
    shares = jnp.exp(lse - jnp.max(lse, axis=0)[None])
    attended = jnp.sum(shares[..., None] * partials, axis=0) / jnp.sum(shares, axis=0)[..., None]
    head_out = jnp.einsum(
        "bqhc,hcv->bqhv", attended.astype(jnp.bfloat16), value_up, preferred_element_type=jnp.float32
    )
    flat = head_out.astype(jnp.bfloat16).reshape(batch, nq, -1)
    term = jnp.einsum("msp,pc->msc", flat, output_projection_rows, preferred_element_type=jnp.float32)
    return lax.psum_scatter(term, "seq", scatter_dimension=2, tiled=True).astype(jnp.bfloat16)


def solution(mesh):
    n = mesh.shape["seq"]

    def body(queries, latent_cache, context_lengths, value_up, output_projection_rows):
        args = (queries, latent_cache, context_lengths, value_up, output_projection_rows)
        if n == 8 and value_up.shape[0] == OWN:
            return local(n, *args)
        return plain(*args)

    placed = (
        P("grp", None, None, None),
        P("grp", "seq", None),
        P("grp"),
        P("seq", None, None),
        P("seq", None),
    )
    return jax.shard_map(
        body, mesh=mesh, in_specs=placed, out_specs=P("grp", None, "seq"), check_vma=False
    )
```

time: 157 us -> 47.5 us (0.30)
  waiting for transfers between devices: 82.3 us -> 13.6 us
  matrix products: 27.2 us -> 0 us
  Pallas kernels: 0 us -> 19.4 us
  between operations: 13.5 us -> 0.26 us
  local copies, waits for them, and re-layouts: 13.2 us -> 0.02 us
  other arithmetic: 10.4 us -> 0.01 us
  starting transfers between devices: 9.94 us -> 14 us
    all_to_all x2 -> x0, waiting for transfers between devices: 47.2 us -> none  [the longest x1 47.2 us: local(): lax.all_to_all(partials[None], 'seq', split_axis=3, concat_axis=0, tiled=...]
    reduce_scatter x1 -> x0, waiting for transfers between devices: 35.1 us -> none  [local(): lax.psum_scatter(term, 'seq', scatter_dimension=2, tiled=True)]
    dot_general x4 -> x0, matrix products: 27.2 us -> none  [the longest x1 10.7 us: shard_partial(): jnp.einsum('bqht,btc->bqhc', weights.astype(jnp.bfloat16), cache_rows[:,...]
    pallas_call x0 -> x23, Pallas kernels: none -> 19.4 us  [the longest x4 12.1 us: attention(): pl.pallas_call(functools.partial(attention_kernel, first, count, turn, le...]
    ppermute x0 -> x17, starting transfers between devices: none -> 14 us  [swap(): return lax.ppermute(array, 'seq', pairs_of(n, step, turn))]
    ppermute x0 -> x17, waiting for transfers between devices: none -> 13.6 us  [swap(): return lax.ppermute(array, 'seq', pairs_of(n, step, turn))]
    all_to_all x2 -> x0, starting transfers between devices: 9.72 us -> none  [the longest x1 5.17 us: local(): lax.all_to_all(log_sums[None], 'seq', split_axis=3, concat_axis=0, tiled=...]
    reduce_sum x3 -> x0, other arithmetic: 7.67 us -> none  [the longest x1 4.81 us: combine_all(): jnp.sum(shares[..., None] * partials, axis=0)]
  transfers between devices with their start and end apart: 3 -> 17, of which waited for: 2 -> 9; matrix products, arithmetic and copies ran while one was open for 12% -> 0% of each run, Pallas kernels for 0% -> 29%
where the time goes in v1:
time: 47.5 us; the launch traced here: 47.3 us
  Pallas kernels  19.4 us (41%)
  starting transfers between devices  14 us (29%)
  waiting for transfers between devices  13.6 us (29%)
    ppermute x17, starting transfers between devices, swap(): return lax.ppermute(array, 'seq', pairs_of(n, step, turn))  14 us
    ppermute x17, waiting for transfers between devices, swap(): return lax.ppermute(array, 'seq', pairs_of(n, step, turn))  13.6 us
    pallas_call x4, Pallas kernels, attention(): pl.pallas_call(functools.partial(attention_kernel, first, count, turn, le...  12.1 us
    pallas_call x4, Pallas kernels, terms(): pl.pallas_call(functools.partial(terms_kernel, mate, places), in_specs=[S...  2.84 us
    pallas_call x8, Pallas kernels, combine(): pl.pallas_call(functools.partial(combine_kernel, places, pieces, batch, h...  2.4 us
  transfers between devices with their start and end apart: 17, of which 9 were waited for; matrix products, arithmetic and copies ran while one was open for 0% of the time, Pallas kernels for 29%

profile of v1, /device:TPU:0, one launch (start us, length us, event | category | flops | bytes accessed | tf_op | source)
XLA Modules:
  0.0 47.3 jit_solution(14696751539373930810)
XLA Ops:
  0.0 3.7 %shard_map.55 = (f32[264,512]{1,0:T(8,128)S(1)}, f32[264,512]{1,0:T(8,128)S(1)}, bf16[2,4,64,576]{3,2,1,0:T(8,128)(2,1)S(1)}, bf16[2,576,1024]{2,1,0:T(8,128)(2,1)S(1)}) custom-call(s32[1]{0:T(128)} %bitcast.me_ref, s32[8]{0:T(128)} %lengths_hbm.7, bf16[8,4,64,576]{3,2,1,0:T(8,128)(2,1)} %q_hbm.7, bf16[8,576,1024]{2,1,0:T(8,128)(2,1)} %bitcast.4), custom_call_target="tpu_custom_call" | custom-call | flops 1000000000 | bytes 1 | tf_op jit(solution)/shard_map/pallas_call | solution.py:180
  3.8 0.5 %collective-permute-start = (f32[264,512]{1,0:T(8,128)S(1)}, f32[264,512]{1,0:T(8,128)S(1)}, u32[]{:S(2)}, u32[]{:S(2)}) collective-permute-start(f32[264,512]{1,0:T(8,128)S(1)} %get-tuple-element.40), channel_id=1, source_target_pairs={{0,1},{1,0},{2,3},{3,2},{4,5},{5,4},{6,7},{7,6},{8,9},{9,8},{10,11... | collective-permute-start | bytes 1622024 | tf_op jit(solution)/shard_map/ppermute | solution.py:383
  4.3 2.9 %shard_map.56 = (f32[264,512]{1,0:T(8,128)S(1)}, f32[264,512]{1,0:T(8,128)S(1)}, bf16[2,4,64,576]{3,2,1,0:T(8,128)(2,1)S(1)}, bf16[2,576,1024]{2,1,0:T(8,128)(2,1)S(1)}) custom-call(s32[1]{0:T(128)} %bitcast.me_ref, s32[8]{0:T(128)} %lengths_hbm.7, bf16[8,4,64,576]{3,2,1,0:T(8,128)(2,1)} %q_hbm.7, bf16[8,576,1024]{2,1,0:T(8,128)(2,1)} %bitcast.5, ...), custom_call_target="tpu_custom_call" | custom-call | flops 1000000000 | bytes 1 | tf_op jit(solution)/shard_map/pallas_call | solution.py:180
  7.6 3.0 %collective-permute-start.1 = (f32[136,512]{1,0:T(8,128)S(1)}, f32[136,512]{1,0:T(8,128)S(1)}, u32[]{:S(2)}, u32[]{:S(2)}) collective-permute-start(f32[136,512]{1,0:T(8,128)S(1)} %get-tuple-element.45), channel_id=1, source_target_pairs={{0,2},{1,5},{2,0},{3,7},{4,6},{5,1},{6,4},{7,3},{8,10},{9,13},{10,... | collective-permute-start | bytes 835592 | tf_op jit(solution)/shard_map/ppermute | solution.py:383
  10.6 2.9 %shard_map.58 = (f32[264,512]{1,0:T(8,128)S(1)}, f32[264,512]{1,0:T(8,128)S(1)}, bf16[2,4,64,576]{3,2,1,0:T(8,128)(2,1)S(1)}, bf16[2,576,1024]{2,1,0:T(8,128)(2,1)S(1)}) custom-call(s32[1]{0:T(128)} %bitcast.me_ref, s32[8]{0:T(128)} %lengths_hbm.7, bf16[8,4,64,576]{3,2,1,0:T(8,128)(2,1)} %q_hbm.7, bf16[8,576,1024]{2,1,0:T(8,128)(2,1)} %bitcast.6, ...), custom_call_target="tpu_custom_call" | custom-call | flops 1000000000 | bytes 1 | tf_op jit(solution)/shard_map/pallas_call | solution.py:180
  13.6 0.3 shard_map.59
  13.9 1.6 %collective-permute-start.8 = (f32[136,512]{1,0:T(8,128)S(1)}, f32[136,512]{1,0:T(8,128)S(1)}, u32[]{:S(2)}, u32[]{:S(2)}) collective-permute-start(f32[136,512]{1,0:T(8,128)S(1)} %get-tuple-element.62), channel_id=1, source_target_pairs={{0,4},{1,3},{2,6},{3,1},{4,0},{5,7},{6,2},{7,5},{8,12},{9,11},{10,... | collective-permute-start | bytes 835592 | tf_op jit(solution)/shard_map/ppermute | solution.py:383
  15.5 2.7 %shard_map.60 = (f32[264,512]{1,0:T(8,128)S(1)}, f32[264,512]{1,0:T(8,128)S(1)}) custom-call(s32[1]{0:T(128)} %bitcast.me_ref, s32[8]{0:T(128)} %lengths_hbm.7, bf16[8,4,64,576]{3,2,1,0:T(8,128)(2,1)} %q_hbm.7, bf16[8,576,1024]{2,1,0:T(8,128)(2,1)} %bitcast.7, bf16[2,4,64,576]{3,2,1,0:T(8,128)(2,1)S(1)} %get-tuple-element.50.refs_0_, ...), custom_call_target="tpu_custom_call" | custom-call | flops 1000000000 | bytes 1 | tf_op jit(solution)/shard_map/pallas_call | solution.py:180
  18.3 0.3 shard_map.61
  18.6 0.7 %collective-permute-start.7 = (f32[136,512]{1,0:T(8,128)S(1)}, f32[136,512]{1,0:T(8,128)S(1)}, u32[]{:S(2)}, u32[]{:S(2)}) collective-permute-start(f32[136,512]{1,0:T(8,128)S(1)} %get-tuple-element.61), channel_id=1, source_target_pairs={{0,2},{1,5},{2,0},{3,7},{4,6},{5,1},{6,4},{7,3},{8,10},{9,13},{10,... | collective-permute-start | bytes 835592 | tf_op jit(solution)/shard_map/ppermute | solution.py:383
  19.6 0.5 %collective-permute-done.5.got_ref = f32[264,512]{1,0:T(8,128)S(1)} collective-permute-done((f32[264,512]{1,0:T(8,128)S(1)}, f32[264,512]{1,0:T(8,128)S(1)}, u32[]{:S(2)}, u32[]{:S(2)}) %collective-permute-start.5) | collective-permute-done | bytes 540704 | tf_op jit(solution)/shard_map/ppermute | solution.py:383
  20.5 1.1 %collective-permute-start.6 = (f32[136,512]{1,0:T(8,128)S(1)}, f32[136,512]{1,0:T(8,128)S(1)}, u32[]{:S(2)}, u32[]{:S(2)}) collective-permute-start(f32[136,512]{1,0:T(8,128)S(1)} %get-tuple-element.60), channel_id=1, source_target_pairs={{0,4},{1,3},{2,6},{3,1},{4,0},{5,7},{6,2},{7,5},{8,12},{9,11},{10,... | collective-permute-start | bytes 835592 | tf_op jit(solution)/shard_map/ppermute | solution.py:383
  21.6 1.0 %collective-permute-start.4 = (f32[72,512]{1,0:T(8,128)S(1)}, f32[72,512]{1,0:T(8,128)S(1)}, u32[]{:S(2)}, u32[]{:S(2)}) collective-permute-start(f32[72,512]{1,0:T(8,128)S(1)} %get-tuple-element.57), channel_id=1, source_target_pairs={{0,4},{1,3},{2,6},{3,1},{4,0},{5,7},{6,2},{7,5},{8,12},{9,11},{10,... | collective-permute-start | bytes 442376 | tf_op jit(solution)/shard_map/ppermute | solution.py:383
  22.9 0.9 %collective-permute-start.9 = (f32[72,512]{1,0:T(8,128)S(1)}, f32[72,512]{1,0:T(8,128)S(1)}, u32[]{:S(2)}, u32[]{:S(2)}) collective-permute-start(f32[72,512]{1,0:T(8,128)S(1)} %get-tuple-element.66), channel_id=1, source_target_pairs={{0,2},{1,5},{2,0},{3,7},{4,6},{5,1},{6,4},{7,3},{8,10},{9,13},{10,... | collective-permute-start | bytes 442376 | tf_op jit(solution)/shard_map/ppermute | solution.py:383
  23.8 3.3 %collective-permute-done.7.got_ref = f32[136,512]{1,0:T(8,128)S(1)} collective-permute-done((f32[136,512]{1,0:T(8,128)S(1)}, f32[136,512]{1,0:T(8,128)S(1)}, u32[]{:S(2)}, u32[]{:S(2)}) %collective-permute-start.7) | collective-permute-done | bytes 278560 | tf_op jit(solution)/shard_map/ppermute | solution.py:383
  27.4 0.6 %collective-permute-start.10 = (f32[72,512]{1,0:T(8,128)S(1)}, f32[72,512]{1,0:T(8,128)S(1)}, u32[]{:S(2)}, u32[]{:S(2)}) collective-permute-start(f32[72,512]{1,0:T(8,128)S(1)} %get-tuple-element.67), channel_id=1, source_target_pairs={{0,4},{1,3},{2,6},{3,1},{4,0},{5,7},{6,2},{7,5},{8,12},{9,11},{10,... | collective-permute-start | bytes 442376 | tf_op jit(solution)/shard_map/ppermute | solution.py:383
  27.9 1.3 %collective-permute-done.6.got_ref = f32[136,512]{1,0:T(8,128)S(1)} collective-permute-done((f32[136,512]{1,0:T(8,128)S(1)}, f32[136,512]{1,0:T(8,128)S(1)}, u32[]{:S(2)}, u32[]{:S(2)}) %collective-permute-start.6) | collective-permute-done | bytes 278560 | tf_op jit(solution)/shard_map/ppermute | solution.py:383
  29.6 0.6 %collective-permute-start.11 = (f32[72,512]{1,0:T(8,128)S(1)}, f32[72,512]{1,0:T(8,128)S(1)}, u32[]{:S(2)}, u32[]{:S(2)}) collective-permute-start(f32[72,512]{1,0:T(8,128)S(1)} %get-tuple-element.68), channel_id=1, source_target_pairs={{0,2},{1,5},{2,0},{3,7},{4,6},{5,1},{6,4},{7,3},{8,10},{9,13},{10,... | collective-permute-start | bytes 442376 | tf_op jit(solution)/shard_map/ppermute | solution.py:383
  30.2 0.7 %collective-permute-done.4.refs_1_ = f32[72,512]{1,0:T(8,128)S(1)} collective-permute-done((f32[72,512]{1,0:T(8,128)S(1)}, f32[72,512]{1,0:T(8,128)S(1)}, u32[]{:S(2)}, u32[]{:S(2)}) %collective-permute-start.4) | collective-permute-done | bytes 147488 | tf_op jit(solution)/shard_map/ppermute | solution.py:383
  31.4 1.4 %collective-permute-done.10.refs_1_ = f32[72,512]{1,0:T(8,128)S(1)} collective-permute-done((f32[72,512]{1,0:T(8,128)S(1)}, f32[72,512]{1,0:T(8,128)S(1)}, u32[]{:S(2)}, u32[]{:S(2)}) %collective-permute-start.10) | collective-permute-done | bytes 147488 | tf_op jit(solution)/shard_map/ppermute | solution.py:383
  33.1 1.7 %collective-permute-done.11.refs_4_ = f32[72,512]{1,0:T(8,128)S(1)} collective-permute-done((f32[72,512]{1,0:T(8,128)S(1)}, f32[72,512]{1,0:T(8,128)S(1)}, u32[]{:S(2)}, u32[]{:S(2)}) %collective-permute-start.11) | collective-permute-done | bytes 147488 | tf_op jit(solution)/shard_map/ppermute | solution.py:383
  34.8 0.5 %shard_map.70.heads_ref = bf16[32,1024]{1,0:T(8,128)(2,1)S(1)} custom-call(s32[1]{0:T(128)} %bitcast.me_ref, f32[4,64,128]{2,1,0:T(8,128)S(1)} %shard_map.67.refs_2_.refs_0_, f32[4,64,128]{2,1,0:T(8,128)S(1)} %shard_map.68.refs_2_.refs_1_, f32[4,64,128]{2,1,0:T(8,128)S(1)} %shard_map.69.refs_2_, f32[72,512]{1,0:T(8,128)S(1)} %get-tuple-element.65.refs_2_.refs_3_, ...), custom_call_target="tpu_custom_call" | custom-call | flops 1 | bytes 1 | tf_op jit(solution)/shard_map/pallas_call | solution.py:304
  35.3 0.7 %shard_map.71.refs_0_ = f32[2,32,896]{2,1,0:T(8,128)S(1)} custom-call(s32[1]{0:T(128)} %bitcast.me_ref, bf16[32,1024]{1,0:T(8,128)(2,1)S(1)} %shard_map.70.heads_ref, bf16[1024,7168]{1,0:T(8,128)(2,1)S(1)} %bitcast.3), custom_call_target="tpu_custom_call" | custom-call | flops 5000000000 | bytes 1 | tf_op jit(solution)/shard_map/pallas_call | solution.py:325
  36.1 0.7 %shard_map.72.own_ref = f32[2,32,896]{2,1,0:T(8,128)S(1)} custom-call(s32[1]{0:T(128)} %bitcast.me_ref, bf16[32,1024]{1,0:T(8,128)(2,1)S(1)} %shard_map.70.heads_ref, bf16[1024,7168]{1,0:T(8,128)(2,1)S(1)} %bitcast.3, f32[2,32,896]{2,1,0:T(8,128)S(1)} %shard_map.71.refs_0_), custom_call_target="tpu_custom_call" | custom-call | flops 5000000000 | bytes 1 | tf_op jit(solution)/shard_map/pallas_call | solution.py:325
  36.9 0.7 %collective-permute-done.12.got_ref = f32[2,32,896]{2,1,0:T(8,128)S(1)} collective-permute-done((f32[2,32,896]{2,1,0:T(8,128)S(1)}, f32[2,32,896]{2,1,0:T(8,128)S(1)}, u32[]{:S(2)}, u32[]{:S(2)}) %collective-permute-start.12) | collective-permute-done | bytes 229408 | tf_op jit(solution)/shard_map/ppermute | solution.py:383
  37.6 1.4 %collective-permute-start.14 = (f32[32,896]{1,0:T(8,128)S(1)}, f32[32,896]{1,0:T(8,128)S(1)}, u32[]{:S(2)}, u32[]{:S(2)}) collective-permute-start(f32[32,896]{1,0:T(8,128)S(1)} %get-tuple-element.69.refs_0_), channel_id=1, source_target_pairs={{0,6},{1,7},{2,4},{3,5},{4,2},{5,3},{6,0},{7,1},{8,14},{9,15},{10,... | collective-permute-start | bytes 344072 | tf_op jit(solution)/shard_map/ppermute | solution.py:383
  39.1 0.7 %shard_map.74.refs_0_ = f32[2,32,896]{2,1,0:T(8,128)S(1)} custom-call(s32[1]{0:T(128)} %bitcast.me_ref, bf16[32,1024]{1,0:T(8,128)(2,1)S(1)} %shard_map.70.heads_ref, bf16[1024,7168]{1,0:T(8,128)(2,1)S(1)} %bitcast.3, f32[32,896]{1,0:T(8,128)S(1)} %get-tuple-element.69.refs_0_), custom_call_target="tpu_custom_call" | custom-call | flops 5000000000 | bytes 1 | tf_op jit(solution)/shard_map/pallas_call | solution.py:325
  39.9 0.7 %shard_map.75.own_ref = f32[2,32,896]{2,1,0:T(8,128)S(1)} custom-call(s32[1]{0:T(128)} %bitcast.me_ref, bf16[32,1024]{1,0:T(8,128)(2,1)S(1)} %shard_map.70.heads_ref, bf16[1024,7168]{1,0:T(8,128)(2,1)S(1)} %bitcast.3, f32[2,32,896]{2,1,0:T(8,128)S(1)} %shard_map.74.refs_0_), custom_call_target="tpu_custom_call" | custom-call | flops 5000000000 | bytes 1 | tf_op jit(solution)/shard_map/pallas_call | solution.py:325
  40.6 0.6 %collective-permute-start.15 = (f32[32,896]{1,0:T(8,128)S(1)}, f32[32,896]{1,0:T(8,128)S(1)}, u32[]{:S(2)}, u32[]{:S(2)}) collective-permute-start(f32[32,896]{1,0:T(8,128)S(1)} %get-tuple-element.71), channel_id=1, source_target_pairs={{0,2},{1,5},{2,0},{3,7},{4,6},{5,1},{6,4},{7,3},{8,10},{9,13},{10,... | collective-permute-start | bytes 344072 | tf_op jit(solution)/shard_map/ppermute | solution.py:383
  41.4 1.5 %collective-permute-start.16 = (f32[32,896]{1,0:T(8,128)S(1)}, f32[32,896]{1,0:T(8,128)S(1)}, u32[]{:S(2)}, u32[]{:S(2)}) collective-permute-start(f32[32,896]{1,0:T(8,128)S(1)} %get-tuple-element.72), channel_id=1, source_target_pairs={{0,4},{1,3},{2,6},{3,1},{4,0},{5,7},{6,2},{7,5},{8,12},{9,11},{10,... | collective-permute-start | bytes 344072 | tf_op jit(solution)/shard_map/ppermute | solution.py:383
  42.9 3.7 %collective-permute-done.15.refs_2_ = f32[32,896]{1,0:T(8,128)S(1)} collective-permute-done((f32[32,896]{1,0:T(8,128)S(1)}, f32[32,896]{1,0:T(8,128)S(1)}, u32[]{:S(2)}, u32[]{:S(2)}) %collective-permute-start.15) | collective-permute-done | bytes 114720 | tf_op jit(solution)/shard_map/ppermute | solution.py:383
  46.6 0.7 %shard_map.77 = bf16[8,4,896]{2,1,0:T(4,128)(2,1)} custom-call(f32[32,896]{1,0:T(8,128)S(1)} %get-tuple-element.70.refs_0_, f32[32,896]{1,0:T(8,128)S(1)} %collective-permute-done.14.refs_1_, f32[32,896]{1,0:T(8,128)S(1)} %collective-permute-done.15.refs_2_, f32[32,896]{1,0:T(8,128)S(1)} %collective-permute-done.16.refs_3_), custom_call_target="tpu_custom_call" | custom-call | flops 1 | bytes 1 | tf_op jit(solution)/shard_map/pallas_call | solution.py:363
  (36 shorter events, 3.1 us)
Async XLA Ops:
  3.8 3.5 %collective-permute-start = (f32[264,512]{1,0:T(8,128)S(1)}, f32[264,512]{1,0:T(8,128)S(1)}, u32[]{:S(2)}, u32[]{:S(2)}) collective-permute-start(f32[264,512]{1,0:T(8,128)S(1)} %get-tuple-element.40), channel_id=1, source_target_pairs={{0,1},{1,0},{2,3},{3,2},{4,5},{5,4},{6,7},{7,6},{8,9},{9,8},{10,11... | collective-permute-start | bytes 1622024 | tf_op jit(solution)/shard_map/ppermute | solution.py:383
  7.1 6.4 %collective-permute-start.3 = (f32[264,512]{1,0:T(8,128)S(1)}, f32[264,512]{1,0:T(8,128)S(1)}, u32[]{:S(2)}, u32[]{:S(2)}) collective-permute-start(f32[264,512]{1,0:T(8,128)S(1)} %get-tuple-element.52), channel_id=1, source_target_pairs={{0,1},{1,0},{2,3},{3,2},{4,5},{5,4},{6,7},{7,6},{8,9},{9,8},{10,11... | collective-permute-start | bytes 1622024 | tf_op jit(solution)/shard_map/ppermute | solution.py:383
  7.6 11.7 %collective-permute-start.1 = (f32[136,512]{1,0:T(8,128)S(1)}, f32[136,512]{1,0:T(8,128)S(1)}, u32[]{:S(2)}, u32[]{:S(2)}) collective-permute-start(f32[136,512]{1,0:T(8,128)S(1)} %get-tuple-element.45), channel_id=1, source_target_pairs={{0,2},{1,5},{2,0},{3,7},{4,6},{5,1},{6,4},{7,3},{8,10},{9,13},{10,... | collective-permute-start | bytes 835592 | tf_op jit(solution)/shard_map/ppermute | solution.py:383
  13.5 4.8 %collective-permute-start.2 = (f32[264,512]{1,0:T(8,128)S(1)}, f32[264,512]{1,0:T(8,128)S(1)}, u32[]{:S(2)}, u32[]{:S(2)}) collective-permute-start(f32[264,512]{1,0:T(8,128)S(1)} %get-tuple-element.49), channel_id=1, source_target_pairs={{0,1},{1,0},{2,3},{3,2},{4,5},{5,4},{6,7},{7,6},{8,9},{9,8},{10,11... | collective-permute-start | bytes 1622024 | tf_op jit(solution)/shard_map/ppermute | solution.py:383
  13.9 8.7 %collective-permute-start.8 = (f32[136,512]{1,0:T(8,128)S(1)}, f32[136,512]{1,0:T(8,128)S(1)}, u32[]{:S(2)}, u32[]{:S(2)}) collective-permute-start(f32[136,512]{1,0:T(8,128)S(1)} %get-tuple-element.62), channel_id=1, source_target_pairs={{0,4},{1,3},{2,6},{3,1},{4,0},{5,7},{6,2},{7,5},{8,12},{9,11},{10,... | collective-permute-start | bytes 835592 | tf_op jit(solution)/shard_map/ppermute | solution.py:383
  18.2 2.0 %collective-permute-start.5 = (f32[264,512]{1,0:T(8,128)S(1)}, f32[264,512]{1,0:T(8,128)S(1)}, u32[]{:S(2)}, u32[]{:S(2)}) collective-permute-start(f32[264,512]{1,0:T(8,128)S(1)} %get-tuple-element.58), channel_id=1, source_target_pairs={{0,1},{1,0},{2,3},{3,2},{4,5},{5,4},{6,7},{7,6},{8,9},{9,8},{10,11... | collective-permute-start | bytes 1622024 | tf_op jit(solution)/shard_map/ppermute | solution.py:383
  18.6 8.5 %collective-permute-start.7 = (f32[136,512]{1,0:T(8,128)S(1)}, f32[136,512]{1,0:T(8,128)S(1)}, u32[]{:S(2)}, u32[]{:S(2)}) collective-permute-start(f32[136,512]{1,0:T(8,128)S(1)} %get-tuple-element.61), channel_id=1, source_target_pairs={{0,2},{1,5},{2,0},{3,7},{4,6},{5,1},{6,4},{7,3},{8,10},{9,13},{10,... | collective-permute-start | bytes 835592 | tf_op jit(solution)/shard_map/ppermute | solution.py:383
  19.3 16.0 %slice-start = ((s8[14680064]{0:T(1024)(128)(4,1)}), s8[4194304]{0:T(1024)(128)(4,1)S(1)}, s32[]{:S(2)}) async-start(s8[14680064]{0:T(1024)(128)(4,1)} %bitcast.2), calls=%async_computation | async-start | bytes 8388608
  19.3 16.0 %slice-start.1 = ((s8[14680064]{0:T(1024)(128)(4,1)}), s8[4194304]{0:T(1024)(128)(4,1)S(1)}, s32[]{:S(2)}) async-start(s8[14680064]{0:T(1024)(128)(4,1)} %bitcast.2), calls=%async_computation.1 | async-start | bytes 8388608
  20.5 8.8 %collective-permute-start.6 = (f32[136,512]{1,0:T(8,128)S(1)}, f32[136,512]{1,0:T(8,128)S(1)}, u32[]{:S(2)}, u32[]{:S(2)}) collective-permute-start(f32[136,512]{1,0:T(8,128)S(1)} %get-tuple-element.60), channel_id=1, source_target_pairs={{0,4},{1,3},{2,6},{3,1},{4,0},{5,7},{6,2},{7,5},{8,12},{9,11},{10,... | collective-permute-start | bytes 835592 | tf_op jit(solution)/shard_map/ppermute | solution.py:383
  21.6 9.3 %collective-permute-start.4 = (f32[72,512]{1,0:T(8,128)S(1)}, f32[72,512]{1,0:T(8,128)S(1)}, u32[]{:S(2)}, u32[]{:S(2)}) collective-permute-start(f32[72,512]{1,0:T(8,128)S(1)} %get-tuple-element.57), channel_id=1, source_target_pairs={{0,4},{1,3},{2,6},{3,1},{4,0},{5,7},{6,2},{7,5},{8,12},{9,11},{10,... | collective-permute-start | bytes 442376 | tf_op jit(solution)/shard_map/ppermute | solution.py:383
  22.9 8.3 %collective-permute-start.9 = (f32[72,512]{1,0:T(8,128)S(1)}, f32[72,512]{1,0:T(8,128)S(1)}, u32[]{:S(2)}, u32[]{:S(2)}) collective-permute-start(f32[72,512]{1,0:T(8,128)S(1)} %get-tuple-element.66), channel_id=1, source_target_pairs={{0,2},{1,5},{2,0},{3,7},{4,6},{5,1},{6,4},{7,3},{8,10},{9,13},{10,... | collective-permute-start | bytes 442376 | tf_op jit(solution)/shard_map/ppermute | solution.py:383
  27.4 5.4 %collective-permute-start.10 = (f32[72,512]{1,0:T(8,128)S(1)}, f32[72,512]{1,0:T(8,128)S(1)}, u32[]{:S(2)}, u32[]{:S(2)}) collective-permute-start(f32[72,512]{1,0:T(8,128)S(1)} %get-tuple-element.67), channel_id=1, source_target_pairs={{0,4},{1,3},{2,6},{3,1},{4,0},{5,7},{6,2},{7,5},{8,12},{9,11},{10,... | collective-permute-start | bytes 442376 | tf_op jit(solution)/shard_map/ppermute | solution.py:383
  29.3 6.0 %slice-start.2 = ((s8[14680064]{0:T(1024)(128)(4,1)}), s8[4194304]{0:T(1024)(128)(4,1)S(1)}, s32[]{:S(2)}) async-start(s8[14680064]{0:T(1024)(128)(4,1)} %bitcast.2), calls=%async_computation.2 | async-start | bytes 8388608
  29.3 6.1 %slice-start.3 = ((s8[14680064]{0:T(1024)(128)(4,1)}), s8[2097152]{0:T(1024)(128)(4,1)S(1)}, s32[]{:S(2)}) async-start(s8[14680064]{0:T(1024)(128)(4,1)} %bitcast.2), calls=%async_computation.3 | async-start | bytes 4194304
  29.6 5.2 %collective-permute-start.11 = (f32[72,512]{1,0:T(8,128)S(1)}, f32[72,512]{1,0:T(8,128)S(1)}, u32[]{:S(2)}, u32[]{:S(2)}) collective-permute-start(f32[72,512]{1,0:T(8,128)S(1)} %get-tuple-element.68), channel_id=1, source_target_pairs={{0,2},{1,5},{2,0},{3,7},{4,6},{5,1},{6,4},{7,3},{8,10},{9,13},{10,... | collective-permute-start | bytes 442376 | tf_op jit(solution)/shard_map/ppermute | solution.py:383
  30.9 3.9 %copy-start = (bf16[8,512,128]{2,1,0:T(8,128)(2,1)S(1)}, bf16[8,512,128]{2,1,0:T(8,128)(2,1)}, u32[]{:S(2)}) copy-start(bf16[8,512,128]{2,1,0:T(8,128)(2,1)} %refs_5_.1) | copy-start | bytes 3145732
  36.1 1.6 %collective-permute-start.12 = (f32[2,32,896]{2,1,0:T(8,128)S(1)}, f32[2,32,896]{2,1,0:T(8,128)S(1)}, u32[]{:S(2)}, u32[]{:S(2)}) collective-permute-start(f32[2,32,896]{2,1,0:T(8,128)S(1)} %shard_map.71.refs_0_), channel_id=1, source_target_pairs={{0,1},{1,0},{2,3},{3,2},{4,5},{5,4},{6,7},{7,6},{8,9},{9,8},{10,11... | collective-permute-start | bytes 688136 | tf_op jit(solution)/shard_map/ppermute | solution.py:383
  37.6 9.0 %collective-permute-start.14 = (f32[32,896]{1,0:T(8,128)S(1)}, f32[32,896]{1,0:T(8,128)S(1)}, u32[]{:S(2)}, u32[]{:S(2)}) collective-permute-start(f32[32,896]{1,0:T(8,128)S(1)} %get-tuple-element.69.refs_0_), channel_id=1, source_target_pairs={{0,6},{1,7},{2,4},{3,5},{4,2},{5,3},{6,0},{7,1},{8,14},{9,15},{10,... | collective-permute-start | bytes 344072 | tf_op jit(solution)/shard_map/ppermute | solution.py:383
  39.8 1.6 %collective-permute-start.13 = (f32[2,32,896]{2,1,0:T(8,128)S(1)}, f32[2,32,896]{2,1,0:T(8,128)S(1)}, u32[]{:S(2)}, u32[]{:S(2)}) collective-permute-start(f32[2,32,896]{2,1,0:T(8,128)S(1)} %shard_map.74.refs_0_), channel_id=1, source_target_pairs={{0,1},{1,0},{2,3},{3,2},{4,5},{5,4},{6,7},{7,6},{8,9},{9,8},{10,11... | collective-permute-start | bytes 688136 | tf_op jit(solution)/shard_map/ppermute | solution.py:383
  40.6 6.0 %collective-permute-start.15 = (f32[32,896]{1,0:T(8,128)S(1)}, f32[32,896]{1,0:T(8,128)S(1)}, u32[]{:S(2)}, u32[]{:S(2)}) collective-permute-start(f32[32,896]{1,0:T(8,128)S(1)} %get-tuple-element.71), channel_id=1, source_target_pairs={{0,2},{1,5},{2,0},{3,7},{4,6},{5,1},{6,4},{7,3},{8,10},{9,13},{10,... | collective-permute-start | bytes 344072 | tf_op jit(solution)/shard_map/ppermute | solution.py:383
  41.4 5.3 %collective-permute-start.16 = (f32[32,896]{1,0:T(8,128)S(1)}, f32[32,896]{1,0:T(8,128)S(1)}, u32[]{:S(2)}, u32[]{:S(2)}) collective-permute-start(f32[32,896]{1,0:T(8,128)S(1)} %get-tuple-element.72), channel_id=1, source_target_pairs={{0,4},{1,3},{2,6},{3,1},{4,0},{5,7},{6,2},{7,5},{8,12},{9,11},{10,... | collective-permute-start | bytes 344072 | tf_op jit(solution)/shard_map/ppermute | solution.py:383

commit v2 on v1

--- a/solution.py
+++ b/solution.py
@@ -12,7 +12,7 @@
 empty_mark = -1e30
 MIB = 1024 * 1024
 PARTS = (2, 2, 2, 2)
-LAST = (50, 50, 0)
+LAST = (20, 20, 0)
 DIRECT = ()
 ORDER = "A0:10 A1:10 C0:50 A2:10 C1:50 A3:10 C2:50 S0:50 C3:0 S1:0 S2:0 S3:50 M0:5 M1:5 M2:5"
 BLOCK = 32

time: 47.5 us -> 48.2 us (1.015)
  waiting for transfers between devices: 13.6 us -> 14.2 us
    ppermute x17, waiting for transfers between devices: 13.6 us -> 14.2 us  [swap(): return lax.ppermute(array, 'seq', pairs_of(n, step, turn))]
  transfers between devices with their start and end apart: 17 -> 17, of which waited for: 9 -> 9; matrix products, arithmetic and copies ran while one was open for 0% -> 0% of each run, Pallas kernels for 29% -> 27%
where the time goes in v2:
time: 48.2 us; the launch traced here: 48 us
  Pallas kernels  19.4 us (40%)
  waiting for transfers between devices  14.2 us (29%)
  starting transfers between devices  14.1 us (29%)
    ppermute x17, waiting for transfers between devices, swap(): return lax.ppermute(array, 'seq', pairs_of(n, step, turn))  14.2 us
    ppermute x17, starting transfers between devices, swap(): return lax.ppermute(array, 'seq', pairs_of(n, step, turn))  14.1 us
    pallas_call x4, Pallas kernels, attention(): pl.pallas_call(functools.partial(attention_kernel, first, count, turn, le...  12.1 us
    pallas_call x4, Pallas kernels, terms(): pl.pallas_call(functools.partial(terms_kernel, mate, places), in_specs=[S...  2.84 us
    pallas_call x8, Pallas kernels, combine(): pl.pallas_call(functools.partial(combine_kernel, places, pieces, batch, h...  2.4 us
  transfers between devices with their start and end apart: 17, of which 9 were waited for; matrix products, arithmetic and copies ran while one was open for 0% of the time, Pallas kernels for 27%

profile of v2, /device:TPU:0, one launch (start us, length us, event | category | flops | bytes accessed | tf_op | source)
XLA Modules:
  0.0 48.0 jit_solution(591551777910900604)
XLA Ops:
  0.0 3.7 %shard_map.55 = (f32[264,512]{1,0:T(8,128)S(1)}, f32[264,512]{1,0:T(8,128)S(1)}, bf16[2,4,64,576]{3,2,1,0:T(8,128)(2,1)S(1)}, bf16[2,576,1024]{2,1,0:T(8,128)(2,1)S(1)}) custom-call(s32[1]{0:T(128)} %bitcast.me_ref, s32[8]{0:T(128)} %lengths_hbm.7, bf16[8,4,64,576]{3,2,1,0:T(8,128)(2,1)} %q_hbm.7, bf16[8,576,1024]{2,1,0:T(8,128)(2,1)} %bitcast.4), custom_call_target="tpu_custom_call" | custom-call | flops 1000000000 | bytes 1 | tf_op jit(solution)/shard_map/pallas_call | solution.py:180
  3.8 0.5 %collective-permute-start = (f32[264,512]{1,0:T(8,128)S(1)}, f32[264,512]{1,0:T(8,128)S(1)}, u32[]{:S(2)}, u32[]{:S(2)}) collective-permute-start(f32[264,512]{1,0:T(8,128)S(1)} %get-tuple-element.40), channel_id=1, source_target_pairs={{0,1},{1,0},{2,3},{3,2},{4,5},{5,4},{6,7},{7,6},{8,9},{9,8},{10,11... | collective-permute-start | bytes 1622024 | tf_op jit(solution)/shard_map/ppermute | solution.py:383
  4.3 2.9 %shard_map.56 = (f32[264,512]{1,0:T(8,128)S(1)}, f32[264,512]{1,0:T(8,128)S(1)}, bf16[2,4,64,576]{3,2,1,0:T(8,128)(2,1)S(1)}, bf16[2,576,1024]{2,1,0:T(8,128)(2,1)S(1)}) custom-call(s32[1]{0:T(128)} %bitcast.me_ref, s32[8]{0:T(128)} %lengths_hbm.7, bf16[8,4,64,576]{3,2,1,0:T(8,128)(2,1)} %q_hbm.7, bf16[8,576,1024]{2,1,0:T(8,128)(2,1)} %bitcast.5, ...), custom_call_target="tpu_custom_call" | custom-call | flops 1000000000 | bytes 1 | tf_op jit(solution)/shard_map/pallas_call | solution.py:180
  7.6 3.0 %collective-permute-start.1 = (f32[136,512]{1,0:T(8,128)S(1)}, f32[136,512]{1,0:T(8,128)S(1)}, u32[]{:S(2)}, u32[]{:S(2)}) collective-permute-start(f32[136,512]{1,0:T(8,128)S(1)} %get-tuple-element.45), channel_id=1, source_target_pairs={{0,2},{1,5},{2,0},{3,7},{4,6},{5,1},{6,4},{7,3},{8,10},{9,13},{10,... | collective-permute-start | bytes 835592 | tf_op jit(solution)/shard_map/ppermute | solution.py:383
  10.6 2.9 %shard_map.58 = (f32[264,512]{1,0:T(8,128)S(1)}, f32[264,512]{1,0:T(8,128)S(1)}, bf16[2,4,64,576]{3,2,1,0:T(8,128)(2,1)S(1)}, bf16[2,576,1024]{2,1,0:T(8,128)(2,1)S(1)}) custom-call(s32[1]{0:T(128)} %bitcast.me_ref, s32[8]{0:T(128)} %lengths_hbm.7, bf16[8,4,64,576]{3,2,1,0:T(8,128)(2,1)} %q_hbm.7, bf16[8,576,1024]{2,1,0:T(8,128)(2,1)} %bitcast.6, ...), custom_call_target="tpu_custom_call" | custom-call | flops 1000000000 | bytes 1 | tf_op jit(solution)/shard_map/pallas_call | solution.py:180
  13.6 0.3 shard_map.59
  13.9 1.6 %collective-permute-start.8 = (f32[136,512]{1,0:T(8,128)S(1)}, f32[136,512]{1,0:T(8,128)S(1)}, u32[]{:S(2)}, u32[]{:S(2)}) collective-permute-start(f32[136,512]{1,0:T(8,128)S(1)} %get-tuple-element.62), channel_id=1, source_target_pairs={{0,4},{1,3},{2,6},{3,1},{4,0},{5,7},{6,2},{7,5},{8,12},{9,11},{10,... | collective-permute-start | bytes 835592 | tf_op jit(solution)/shard_map/ppermute | solution.py:383
  15.5 2.7 %shard_map.60 = (f32[264,512]{1,0:T(8,128)S(1)}, f32[264,512]{1,0:T(8,128)S(1)}) custom-call(s32[1]{0:T(128)} %bitcast.me_ref, s32[8]{0:T(128)} %lengths_hbm.7, bf16[8,4,64,576]{3,2,1,0:T(8,128)(2,1)} %q_hbm.7, bf16[8,576,1024]{2,1,0:T(8,128)(2,1)} %bitcast.7, bf16[2,4,64,576]{3,2,1,0:T(8,128)(2,1)S(1)} %get-tuple-element.50.refs_0_, ...), custom_call_target="tpu_custom_call" | custom-call | flops 1000000000 | bytes 1 | tf_op jit(solution)/shard_map/pallas_call | solution.py:180
  18.6 0.7 %collective-permute-start.7 = (f32[136,512]{1,0:T(8,128)S(1)}, f32[136,512]{1,0:T(8,128)S(1)}, u32[]{:S(2)}, u32[]{:S(2)}) collective-permute-start(f32[136,512]{1,0:T(8,128)S(1)} %get-tuple-element.61), channel_id=1, source_target_pairs={{0,2},{1,5},{2,0},{3,7},{4,6},{5,1},{6,4},{7,3},{8,10},{9,13},{10,... | collective-permute-start | bytes 835592 | tf_op jit(solution)/shard_map/ppermute | solution.py:383
  19.6 0.5 %collective-permute-done.5.got_ref = f32[264,512]{1,0:T(8,128)S(1)} collective-permute-done((f32[264,512]{1,0:T(8,128)S(1)}, f32[264,512]{1,0:T(8,128)S(1)}, u32[]{:S(2)}, u32[]{:S(2)}) %collective-permute-start.5) | collective-permute-done | bytes 540704 | tf_op jit(solution)/shard_map/ppermute | solution.py:383
  20.5 1.1 %collective-permute-start.6 = (f32[136,512]{1,0:T(8,128)S(1)}, f32[136,512]{1,0:T(8,128)S(1)}, u32[]{:S(2)}, u32[]{:S(2)}) collective-permute-start(f32[136,512]{1,0:T(8,128)S(1)} %get-tuple-element.60), channel_id=1, source_target_pairs={{0,4},{1,3},{2,6},{3,1},{4,0},{5,7},{6,2},{7,5},{8,12},{9,11},{10,... | collective-permute-start | bytes 835592 | tf_op jit(solution)/shard_map/ppermute | solution.py:383
  21.6 1.0 %collective-permute-start.4 = (f32[72,512]{1,0:T(8,128)S(1)}, f32[72,512]{1,0:T(8,128)S(1)}, u32[]{:S(2)}, u32[]{:S(2)}) collective-permute-start(f32[72,512]{1,0:T(8,128)S(1)} %get-tuple-element.57), channel_id=1, source_target_pairs={{0,4},{1,3},{2,6},{3,1},{4,0},{5,7},{6,2},{7,5},{8,12},{9,11},{10,... | collective-permute-start | bytes 442376 | tf_op jit(solution)/shard_map/ppermute | solution.py:383
  22.9 0.9 %collective-permute-start.9 = (f32[72,512]{1,0:T(8,128)S(1)}, f32[72,512]{1,0:T(8,128)S(1)}, u32[]{:S(2)}, u32[]{:S(2)}) collective-permute-start(f32[72,512]{1,0:T(8,128)S(1)} %get-tuple-element.66), channel_id=1, source_target_pairs={{0,2},{1,5},{2,0},{3,7},{4,6},{5,1},{6,4},{7,3},{8,10},{9,13},{10,... | collective-permute-start | bytes 442376 | tf_op jit(solution)/shard_map/ppermute | solution.py:383
  23.8 3.3 %collective-permute-done.7.got_ref = f32[136,512]{1,0:T(8,128)S(1)} collective-permute-done((f32[136,512]{1,0:T(8,128)S(1)}, f32[136,512]{1,0:T(8,128)S(1)}, u32[]{:S(2)}, u32[]{:S(2)}) %collective-permute-start.7) | collective-permute-done | bytes 278560 | tf_op jit(solution)/shard_map/ppermute | solution.py:383
  27.4 0.6 %collective-permute-start.10 = (f32[72,512]{1,0:T(8,128)S(1)}, f32[72,512]{1,0:T(8,128)S(1)}, u32[]{:S(2)}, u32[]{:S(2)}) collective-permute-start(f32[72,512]{1,0:T(8,128)S(1)} %get-tuple-element.67), channel_id=1, source_target_pairs={{0,4},{1,3},{2,6},{3,1},{4,0},{5,7},{6,2},{7,5},{8,12},{9,11},{10,... | collective-permute-start | bytes 442376 | tf_op jit(solution)/shard_map/ppermute | solution.py:383
  27.9 1.3 %collective-permute-done.6.got_ref = f32[136,512]{1,0:T(8,128)S(1)} collective-permute-done((f32[136,512]{1,0:T(8,128)S(1)}, f32[136,512]{1,0:T(8,128)S(1)}, u32[]{:S(2)}, u32[]{:S(2)}) %collective-permute-start.6) | collective-permute-done | bytes 278560 | tf_op jit(solution)/shard_map/ppermute | solution.py:383
  29.6 0.6 %collective-permute-start.11 = (f32[72,512]{1,0:T(8,128)S(1)}, f32[72,512]{1,0:T(8,128)S(1)}, u32[]{:S(2)}, u32[]{:S(2)}) collective-permute-start(f32[72,512]{1,0:T(8,128)S(1)} %get-tuple-element.68), channel_id=1, source_target_pairs={{0,2},{1,5},{2,0},{3,7},{4,6},{5,1},{6,4},{7,3},{8,10},{9,13},{10,... | collective-permute-start | bytes 442376 | tf_op jit(solution)/shard_map/ppermute | solution.py:383
  30.2 0.7 %collective-permute-done.4.refs_1_ = f32[72,512]{1,0:T(8,128)S(1)} collective-permute-done((f32[72,512]{1,0:T(8,128)S(1)}, f32[72,512]{1,0:T(8,128)S(1)}, u32[]{:S(2)}, u32[]{:S(2)}) %collective-permute-start.4) | collective-permute-done | bytes 147488 | tf_op jit(solution)/shard_map/ppermute | solution.py:383
  31.4 1.4 %collective-permute-done.10.refs_1_ = f32[72,512]{1,0:T(8,128)S(1)} collective-permute-done((f32[72,512]{1,0:T(8,128)S(1)}, f32[72,512]{1,0:T(8,128)S(1)}, u32[]{:S(2)}, u32[]{:S(2)}) %collective-permute-start.10) | collective-permute-done | bytes 147488 | tf_op jit(solution)/shard_map/ppermute | solution.py:383
  33.1 1.7 %collective-permute-done.11.refs_4_ = f32[72,512]{1,0:T(8,128)S(1)} collective-permute-done((f32[72,512]{1,0:T(8,128)S(1)}, f32[72,512]{1,0:T(8,128)S(1)}, u32[]{:S(2)}, u32[]{:S(2)}) %collective-permute-start.11) | collective-permute-done | bytes 147488 | tf_op jit(solution)/shard_map/ppermute | solution.py:383
  34.8 0.5 %shard_map.70.heads_ref = bf16[32,1024]{1,0:T(8,128)(2,1)S(1)} custom-call(s32[1]{0:T(128)} %bitcast.me_ref, f32[4,64,128]{2,1,0:T(8,128)S(1)} %shard_map.67.refs_2_.refs_0_, f32[4,64,128]{2,1,0:T(8,128)S(1)} %shard_map.68.refs_2_.refs_1_, f32[4,64,128]{2,1,0:T(8,128)S(1)} %shard_map.69.refs_2_, f32[72,512]{1,0:T(8,128)S(1)} %get-tuple-element.65.refs_2_.refs_3_, ...), custom_call_target="tpu_custom_call" | custom-call | flops 1 | bytes 1 | tf_op jit(solution)/shard_map/pallas_call | solution.py:304
  35.3 0.7 %shard_map.71.refs_0_ = f32[2,32,896]{2,1,0:T(8,128)S(1)} custom-call(s32[1]{0:T(128)} %bitcast.me_ref, bf16[32,1024]{1,0:T(8,128)(2,1)S(1)} %shard_map.70.heads_ref, bf16[1024,7168]{1,0:T(8,128)(2,1)S(1)} %bitcast.3), custom_call_target="tpu_custom_call" | custom-call | flops 2000000000 | bytes 1 | tf_op jit(solution)/shard_map/pallas_call | solution.py:325
  36.1 0.7 %shard_map.72.own_ref = f32[2,32,896]{2,1,0:T(8,128)S(1)} custom-call(s32[1]{0:T(128)} %bitcast.me_ref, bf16[32,1024]{1,0:T(8,128)(2,1)S(1)} %shard_map.70.heads_ref, bf16[1024,7168]{1,0:T(8,128)(2,1)S(1)} %bitcast.3, f32[2,32,896]{2,1,0:T(8,128)S(1)} %shard_map.71.refs_0_), custom_call_target="tpu_custom_call" | custom-call | flops 2000000000 | bytes 1 | tf_op jit(solution)/shard_map/pallas_call | solution.py:325
  36.9 0.7 %collective-permute-done.12.got_ref = f32[2,32,896]{2,1,0:T(8,128)S(1)} collective-permute-done((f32[2,32,896]{2,1,0:T(8,128)S(1)}, f32[2,32,896]{2,1,0:T(8,128)S(1)}, u32[]{:S(2)}, u32[]{:S(2)}) %collective-permute-start.12) | collective-permute-done | bytes 229408 | tf_op jit(solution)/shard_map/ppermute | solution.py:383
  37.6 0.7 %shard_map.74.refs_0_ = f32[2,32,896]{2,1,0:T(8,128)S(1)} custom-call(s32[1]{0:T(128)} %bitcast.me_ref, bf16[32,1024]{1,0:T(8,128)(2,1)S(1)} %shard_map.70.heads_ref, bf16[1024,7168]{1,0:T(8,128)(2,1)S(1)} %bitcast.3, f32[32,896]{1,0:T(8,128)S(1)} %get-tuple-element.69.refs_0_), custom_call_target="tpu_custom_call" | custom-call | flops 2000000000 | bytes 1 | tf_op jit(solution)/shard_map/pallas_call | solution.py:325
  38.6 1.4 %collective-permute-start.14 = (f32[32,896]{1,0:T(8,128)S(1)}, f32[32,896]{1,0:T(8,128)S(1)}, u32[]{:S(2)}, u32[]{:S(2)}) collective-permute-start(f32[32,896]{1,0:T(8,128)S(1)} %get-tuple-element.69.refs_0_), channel_id=1, source_target_pairs={{0,6},{1,7},{2,4},{3,5},{4,2},{5,3},{6,0},{7,1},{8,14},{9,15},{10,... | collective-permute-start | bytes 344072 | tf_op jit(solution)/shard_map/ppermute | solution.py:383
  40.0 0.6 %collective-permute-start.15 = (f32[32,896]{1,0:T(8,128)S(1)}, f32[32,896]{1,0:T(8,128)S(1)}, u32[]{:S(2)}, u32[]{:S(2)}) collective-permute-start(f32[32,896]{1,0:T(8,128)S(1)} %get-tuple-element.71), channel_id=1, source_target_pairs={{0,2},{1,5},{2,0},{3,7},{4,6},{5,1},{6,4},{7,3},{8,10},{9,13},{10,... | collective-permute-start | bytes 344072 | tf_op jit(solution)/shard_map/ppermute | solution.py:383
  40.5 0.7 %shard_map.75.own_ref = f32[2,32,896]{2,1,0:T(8,128)S(1)} custom-call(s32[1]{0:T(128)} %bitcast.me_ref, bf16[32,1024]{1,0:T(8,128)(2,1)S(1)} %shard_map.70.heads_ref, bf16[1024,7168]{1,0:T(8,128)(2,1)S(1)} %bitcast.3, f32[2,32,896]{2,1,0:T(8,128)S(1)} %shard_map.74.refs_0_), custom_call_target="tpu_custom_call" | custom-call | flops 2000000000 | bytes 1 | tf_op jit(solution)/shard_map/pallas_call | solution.py:325
  41.3 1.6 %collective-permute-start.16 = (f32[32,896]{1,0:T(8,128)S(1)}, f32[32,896]{1,0:T(8,128)S(1)}, u32[]{:S(2)}, u32[]{:S(2)}) collective-permute-start(f32[32,896]{1,0:T(8,128)S(1)} %get-tuple-element.72), channel_id=1, source_target_pairs={{0,4},{1,3},{2,6},{3,1},{4,0},{5,7},{6,2},{7,5},{8,12},{9,11},{10,... | collective-permute-start | bytes 344072 | tf_op jit(solution)/shard_map/ppermute | solution.py:383
  42.9 3.5 %collective-permute-done.15.refs_2_ = f32[32,896]{1,0:T(8,128)S(1)} collective-permute-done((f32[32,896]{1,0:T(8,128)S(1)}, f32[32,896]{1,0:T(8,128)S(1)}, u32[]{:S(2)}, u32[]{:S(2)}) %collective-permute-start.15) | collective-permute-done | bytes 114720 | tf_op jit(solution)/shard_map/ppermute | solution.py:383
  46.4 0.9 %collective-permute-done.16.refs_3_ = f32[32,896]{1,0:T(8,128)S(1)} collective-permute-done((f32[32,896]{1,0:T(8,128)S(1)}, f32[32,896]{1,0:T(8,128)S(1)}, u32[]{:S(2)}, u32[]{:S(2)}) %collective-permute-start.16) | collective-permute-done | bytes 114720 | tf_op jit(solution)/shard_map/ppermute | solution.py:383
  47.3 0.7 %shard_map.77 = bf16[8,4,896]{2,1,0:T(4,128)(2,1)} custom-call(f32[32,896]{1,0:T(8,128)S(1)} %get-tuple-element.70.refs_0_, f32[32,896]{1,0:T(8,128)S(1)} %collective-permute-done.14.refs_1_, f32[32,896]{1,0:T(8,128)S(1)} %collective-permute-done.15.refs_2_, f32[32,896]{1,0:T(8,128)S(1)} %collective-permute-done.16.refs_3_), custom_call_target="tpu_custom_call" | custom-call | flops 1 | bytes 1 | tf_op jit(solution)/shard_map/pallas_call | solution.py:363
  (36 shorter events, 3.5 us)
Async XLA Ops:
  3.8 3.5 %collective-permute-start = (f32[264,512]{1,0:T(8,128)S(1)}, f32[264,512]{1,0:T(8,128)S(1)}, u32[]{:S(2)}, u32[]{:S(2)}) collective-permute-start(f32[264,512]{1,0:T(8,128)S(1)} %get-tuple-element.40), channel_id=1, source_target_pairs={{0,1},{1,0},{2,3},{3,2},{4,5},{5,4},{6,7},{7,6},{8,9},{9,8},{10,11... | collective-permute-start | bytes 1622024 | tf_op jit(solution)/shard_map/ppermute | solution.py:383
  7.1 6.4 %collective-permute-start.3 = (f32[264,512]{1,0:T(8,128)S(1)}, f32[264,512]{1,0:T(8,128)S(1)}, u32[]{:S(2)}, u32[]{:S(2)}) collective-permute-start(f32[264,512]{1,0:T(8,128)S(1)} %get-tuple-element.52), channel_id=1, source_target_pairs={{0,1},{1,0},{2,3},{3,2},{4,5},{5,4},{6,7},{7,6},{8,9},{9,8},{10,11... | collective-permute-start | bytes 1622024 | tf_op jit(solution)/shard_map/ppermute | solution.py:383
  7.6 11.7 %collective-permute-start.1 = (f32[136,512]{1,0:T(8,128)S(1)}, f32[136,512]{1,0:T(8,128)S(1)}, u32[]{:S(2)}, u32[]{:S(2)}) collective-permute-start(f32[136,512]{1,0:T(8,128)S(1)} %get-tuple-element.45), channel_id=1, source_target_pairs={{0,2},{1,5},{2,0},{3,7},{4,6},{5,1},{6,4},{7,3},{8,10},{9,13},{10,... | collective-permute-start | bytes 835592 | tf_op jit(solution)/shard_map/ppermute | solution.py:383
  13.5 4.8 %collective-permute-start.2 = (f32[264,512]{1,0:T(8,128)S(1)}, f32[264,512]{1,0:T(8,128)S(1)}, u32[]{:S(2)}, u32[]{:S(2)}) collective-permute-start(f32[264,512]{1,0:T(8,128)S(1)} %get-tuple-element.49), channel_id=1, source_target_pairs={{0,1},{1,0},{2,3},{3,2},{4,5},{5,4},{6,7},{7,6},{8,9},{9,8},{10,11... | collective-permute-start | bytes 1622024 | tf_op jit(solution)/shard_map/ppermute | solution.py:383
  13.9 8.7 %collective-permute-start.8 = (f32[136,512]{1,0:T(8,128)S(1)}, f32[136,512]{1,0:T(8,128)S(1)}, u32[]{:S(2)}, u32[]{:S(2)}) collective-permute-start(f32[136,512]{1,0:T(8,128)S(1)} %get-tuple-element.62), channel_id=1, source_target_pairs={{0,4},{1,3},{2,6},{3,1},{4,0},{5,7},{6,2},{7,5},{8,12},{9,11},{10,... | collective-permute-start | bytes 835592 | tf_op jit(solution)/shard_map/ppermute | solution.py:383
  18.2 2.0 %collective-permute-start.5 = (f32[264,512]{1,0:T(8,128)S(1)}, f32[264,512]{1,0:T(8,128)S(1)}, u32[]{:S(2)}, u32[]{:S(2)}) collective-permute-start(f32[264,512]{1,0:T(8,128)S(1)} %get-tuple-element.58), channel_id=1, source_target_pairs={{0,1},{1,0},{2,3},{3,2},{4,5},{5,4},{6,7},{7,6},{8,9},{9,8},{10,11... | collective-permute-start | bytes 1622024 | tf_op jit(solution)/shard_map/ppermute | solution.py:383
  18.6 8.5 %collective-permute-start.7 = (f32[136,512]{1,0:T(8,128)S(1)}, f32[136,512]{1,0:T(8,128)S(1)}, u32[]{:S(2)}, u32[]{:S(2)}) collective-permute-start(f32[136,512]{1,0:T(8,128)S(1)} %get-tuple-element.61), channel_id=1, source_target_pairs={{0,2},{1,5},{2,0},{3,7},{4,6},{5,1},{6,4},{7,3},{8,10},{9,13},{10,... | collective-permute-start | bytes 835592 | tf_op jit(solution)/shard_map/ppermute | solution.py:383
  19.3 16.0 %slice-start = ((s8[14680064]{0:T(1024)(128)(4,1)}), s8[4194304]{0:T(1024)(128)(4,1)S(1)}, s32[]{:S(2)}) async-start(s8[14680064]{0:T(1024)(128)(4,1)} %bitcast.2), calls=%async_computation | async-start | bytes 8388608
  19.3 16.0 %slice-start.1 = ((s8[14680064]{0:T(1024)(128)(4,1)}), s8[4194304]{0:T(1024)(128)(4,1)S(1)}, s32[]{:S(2)}) async-start(s8[14680064]{0:T(1024)(128)(4,1)} %bitcast.2), calls=%async_computation.1 | async-start | bytes 8388608
  20.5 8.8 %collective-permute-start.6 = (f32[136,512]{1,0:T(8,128)S(1)}, f32[136,512]{1,0:T(8,128)S(1)}, u32[]{:S(2)}, u32[]{:S(2)}) collective-permute-start(f32[136,512]{1,0:T(8,128)S(1)} %get-tuple-element.60), channel_id=1, source_target_pairs={{0,4},{1,3},{2,6},{3,1},{4,0},{5,7},{6,2},{7,5},{8,12},{9,11},{10,... | collective-permute-start | bytes 835592 | tf_op jit(solution)/shard_map/ppermute | solution.py:383
  21.6 9.3 %collective-permute-start.4 = (f32[72,512]{1,0:T(8,128)S(1)}, f32[72,512]{1,0:T(8,128)S(1)}, u32[]{:S(2)}, u32[]{:S(2)}) collective-permute-start(f32[72,512]{1,0:T(8,128)S(1)} %get-tuple-element.57), channel_id=1, source_target_pairs={{0,4},{1,3},{2,6},{3,1},{4,0},{5,7},{6,2},{7,5},{8,12},{9,11},{10,... | collective-permute-start | bytes 442376 | tf_op jit(solution)/shard_map/ppermute | solution.py:383
  22.9 8.3 %collective-permute-start.9 = (f32[72,512]{1,0:T(8,128)S(1)}, f32[72,512]{1,0:T(8,128)S(1)}, u32[]{:S(2)}, u32[]{:S(2)}) collective-permute-start(f32[72,512]{1,0:T(8,128)S(1)} %get-tuple-element.66), channel_id=1, source_target_pairs={{0,2},{1,5},{2,0},{3,7},{4,6},{5,1},{6,4},{7,3},{8,10},{9,13},{10,... | collective-permute-start | bytes 442376 | tf_op jit(solution)/shard_map/ppermute | solution.py:383
  27.4 5.4 %collective-permute-start.10 = (f32[72,512]{1,0:T(8,128)S(1)}, f32[72,512]{1,0:T(8,128)S(1)}, u32[]{:S(2)}, u32[]{:S(2)}) collective-permute-start(f32[72,512]{1,0:T(8,128)S(1)} %get-tuple-element.67), channel_id=1, source_target_pairs={{0,4},{1,3},{2,6},{3,1},{4,0},{5,7},{6,2},{7,5},{8,12},{9,11},{10,... | collective-permute-start | bytes 442376 | tf_op jit(solution)/shard_map/ppermute | solution.py:383
  29.3 6.0 %slice-start.2 = ((s8[14680064]{0:T(1024)(128)(4,1)}), s8[4194304]{0:T(1024)(128)(4,1)S(1)}, s32[]{:S(2)}) async-start(s8[14680064]{0:T(1024)(128)(4,1)} %bitcast.2), calls=%async_computation.2 | async-start | bytes 8388608
  29.3 6.1 %slice-start.3 = ((s8[14680064]{0:T(1024)(128)(4,1)}), s8[2097152]{0:T(1024)(128)(4,1)S(1)}, s32[]{:S(2)}) async-start(s8[14680064]{0:T(1024)(128)(4,1)} %bitcast.2), calls=%async_computation.3 | async-start | bytes 4194304
  29.6 5.2 %collective-permute-start.11 = (f32[72,512]{1,0:T(8,128)S(1)}, f32[72,512]{1,0:T(8,128)S(1)}, u32[]{:S(2)}, u32[]{:S(2)}) collective-permute-start(f32[72,512]{1,0:T(8,128)S(1)} %get-tuple-element.68), channel_id=1, source_target_pairs={{0,2},{1,5},{2,0},{3,7},{4,6},{5,1},{6,4},{7,3},{8,10},{9,13},{10,... | collective-permute-start | bytes 442376 | tf_op jit(solution)/shard_map/ppermute | solution.py:383
  30.9 3.9 %copy-start = (bf16[8,512,128]{2,1,0:T(8,128)(2,1)S(1)}, bf16[8,512,128]{2,1,0:T(8,128)(2,1)}, u32[]{:S(2)}) copy-start(bf16[8,512,128]{2,1,0:T(8,128)(2,1)} %refs_5_.1) | copy-start | bytes 3145732
  36.1 1.6 %collective-permute-start.12 = (f32[2,32,896]{2,1,0:T(8,128)S(1)}, f32[2,32,896]{2,1,0:T(8,128)S(1)}, u32[]{:S(2)}, u32[]{:S(2)}) collective-permute-start(f32[2,32,896]{2,1,0:T(8,128)S(1)} %shard_map.71.refs_0_), channel_id=1, source_target_pairs={{0,1},{1,0},{2,3},{3,2},{4,5},{5,4},{6,7},{7,6},{8,9},{9,8},{10,11... | collective-permute-start | bytes 688136 | tf_op jit(solution)/shard_map/ppermute | solution.py:383
  38.4 2.9 %collective-permute-start.13 = (f32[2,32,896]{2,1,0:T(8,128)S(1)}, f32[2,32,896]{2,1,0:T(8,128)S(1)}, u32[]{:S(2)}, u32[]{:S(2)}) collective-permute-start(f32[2,32,896]{2,1,0:T(8,128)S(1)} %shard_map.74.refs_0_), channel_id=1, source_target_pairs={{0,1},{1,0},{2,3},{3,2},{4,5},{5,4},{6,7},{7,6},{8,9},{9,8},{10,11... | collective-permute-start | bytes 688136 | tf_op jit(solution)/shard_map/ppermute | solution.py:383
  38.6 7.8 %collective-permute-start.14 = (f32[32,896]{1,0:T(8,128)S(1)}, f32[32,896]{1,0:T(8,128)S(1)}, u32[]{:S(2)}, u32[]{:S(2)}) collective-permute-start(f32[32,896]{1,0:T(8,128)S(1)} %get-tuple-element.69.refs_0_), channel_id=1, source_target_pairs={{0,6},{1,7},{2,4},{3,5},{4,2},{5,3},{6,0},{7,1},{8,14},{9,15},{10,... | collective-permute-start | bytes 344072 | tf_op jit(solution)/shard_map/ppermute | solution.py:383
  40.0 6.5 %collective-permute-start.15 = (f32[32,896]{1,0:T(8,128)S(1)}, f32[32,896]{1,0:T(8,128)S(1)}, u32[]{:S(2)}, u32[]{:S(2)}) collective-permute-start(f32[32,896]{1,0:T(8,128)S(1)} %get-tuple-element.71), channel_id=1, source_target_pairs={{0,2},{1,5},{2,0},{3,7},{4,6},{5,1},{6,4},{7,3},{8,10},{9,13},{10,... | collective-permute-start | bytes 344072 | tf_op jit(solution)/shard_map/ppermute | solution.py:383
  41.3 6.0 %collective-permute-start.16 = (f32[32,896]{1,0:T(8,128)S(1)}, f32[32,896]{1,0:T(8,128)S(1)}, u32[]{:S(2)}, u32[]{:S(2)}) collective-permute-start(f32[32,896]{1,0:T(8,128)S(1)} %get-tuple-element.72), channel_id=1, source_target_pairs={{0,4},{1,3},{2,6},{3,1},{4,0},{5,7},{6,2},{7,5},{8,12},{9,11},{10,... | collective-permute-start | bytes 344072 | tf_op jit(solution)/shard_map/ppermute | solution.py:383

commit v3 on v1

--- a/solution.py
+++ b/solution.py
@@ -11,10 +11,10 @@
 score_scale = 0.07216878364870323
 empty_mark = -1e30
 MIB = 1024 * 1024
-PARTS = (2, 2, 2, 2)
+PARTS = (2, 3, 3)
 LAST = (50, 50, 0)
 DIRECT = ()
-ORDER = "A0:10 A1:10 C0:50 A2:10 C1:50 A3:10 C2:50 S0:50 C3:0 S1:0 S2:0 S3:50 M0:5 M1:5 M2:5"
+ORDER = "A0:10 A1:10 C0:50 A2:10 C1:50 S0:50 C2:0 S1:0 S2:50 M0:5 M1:5"
 BLOCK = 32
 PIECES = 4
 TILE = 256

time: 47.5 us -> 48.9 us (1.029)
  waiting for transfers between devices: 13.6 us -> 15.8 us
  Pallas kernels: 19.4 us -> 18 us
  starting transfers between devices: 14 us -> 14.6 us
    ppermute x17 -> x14, waiting for transfers between devices: 13.6 us -> 15.8 us  [swap(): return lax.ppermute(array, 'seq', pairs_of(n, step, turn))]
    ppermute x17 -> x14, starting transfers between devices: 14 us -> 14.6 us  [swap(): return lax.ppermute(array, 'seq', pairs_of(n, step, turn))]
    pallas_call x4 -> x3, Pallas kernels: 12.1 us -> 11.5 us  [attention(): pl.pallas_call(functools.partial(attention_kernel, first, count, turn, le...]
    pallas_call x8 -> x6, Pallas kernels: 2.4 us -> 1.93 us  [combine(): pl.pallas_call(functools.partial(combine_kernel, places, pieces, batch, h...]
  transfers between devices with their start and end apart: 17 -> 14, of which waited for: 9 -> 7; matrix products, arithmetic and copies ran while one was open for 0% -> 0% of each run, Pallas kernels for 29% -> 25%
where the time goes in v3:
time: 48.9 us; the launch traced here: 48.7 us
  Pallas kernels  18 us (37%)
  waiting for transfers between devices  15.8 us (32%)
  starting transfers between devices  14.6 us (30%)
    ppermute x14, waiting for transfers between devices, swap(): return lax.ppermute(array, 'seq', pairs_of(n, step, turn))  15.8 us
    ppermute x14, starting transfers between devices, swap(): return lax.ppermute(array, 'seq', pairs_of(n, step, turn))  14.6 us
    pallas_call x3, Pallas kernels, attention(): pl.pallas_call(functools.partial(attention_kernel, first, count, turn, le...  11.5 us
    pallas_call x4, Pallas kernels, terms(): pl.pallas_call(functools.partial(terms_kernel, mate, places), in_specs=[S...  2.85 us
    pallas_call x6, Pallas kernels, combine(): pl.pallas_call(functools.partial(combine_kernel, places, pieces, batch, h...  1.93 us
  transfers between devices with their start and end apart: 14, of which 7 were waited for; matrix products, arithmetic and copies ran while one was open for 0% of the time, Pallas kernels for 25%

profile of v3, /device:TPU:0, one launch (start us, length us, event | category | flops | bytes accessed | tf_op | source)
XLA Modules:
  0.0 48.7 jit_solution(13064179926888610700)
XLA Ops:
  0.0 4.0 %shard_map.55 = (f32[264,512]{1,0:T(8,128)S(1)}, f32[264,512]{1,0:T(8,128)S(1)}, bf16[3,4,64,576]{3,2,1,0:T(8,128)(2,1)S(1)}, bf16[3,576,1024]{2,1,0:T(8,128)(2,1)S(1)}) custom-call(s32[1]{0:T(128)} %bitcast.me_ref, s32[8]{0:T(128)} %lengths_hbm.5, bf16[8,4,64,576]{3,2,1,0:T(8,128)(2,1)} %q_hbm.5, bf16[8,576,1024]{2,1,0:T(8,128)(2,1)} %bitcast.4), custom_call_target="tpu_custom_call" | custom-call | flops 1000000000 | bytes 1 | tf_op jit(solution)/shard_map/pallas_call | solution.py:180
  4.1 0.5 %collective-permute-start = (f32[264,512]{1,0:T(8,128)S(1)}, f32[264,512]{1,0:T(8,128)S(1)}, u32[]{:S(2)}, u32[]{:S(2)}) collective-permute-start(f32[264,512]{1,0:T(8,128)S(1)} %get-tuple-element.32), channel_id=1, source_target_pairs={{0,1},{1,0},{2,3},{3,2},{4,5},{5,4},{6,7},{7,6},{8,9},{9,8},{10,11... | collective-permute-start | bytes 1622024 | tf_op jit(solution)/shard_map/ppermute | solution.py:383
  4.6 3.9 %shard_map.56 = (f32[392,512]{1,0:T(8,128)S(1)}, f32[392,512]{1,0:T(8,128)S(1)}, bf16[3,4,64,576]{3,2,1,0:T(8,128)(2,1)S(1)}, bf16[3,576,1024]{2,1,0:T(8,128)(2,1)S(1)}) custom-call(s32[1]{0:T(128)} %bitcast.me_ref, s32[8]{0:T(128)} %lengths_hbm.5, bf16[8,4,64,576]{3,2,1,0:T(8,128)(2,1)} %q_hbm.5, bf16[8,576,1024]{2,1,0:T(8,128)(2,1)} %bitcast.5, ...), custom_call_target="tpu_custom_call" | custom-call | flops 1000000000 | bytes 1 | tf_op jit(solution)/shard_map/pallas_call | solution.py:180
  8.6 0.3 shard_map.57
  8.9 3.0 %collective-permute-start.1 = (f32[136,512]{1,0:T(8,128)S(1)}, f32[136,512]{1,0:T(8,128)S(1)}, u32[]{:S(2)}, u32[]{:S(2)}) collective-permute-start(f32[136,512]{1,0:T(8,128)S(1)} %get-tuple-element.37), channel_id=1, source_target_pairs={{0,2},{1,5},{2,0},{3,7},{4,6},{5,1},{6,4},{7,3},{8,10},{9,13},{10,... | collective-permute-start | bytes 835592 | tf_op jit(solution)/shard_map/ppermute | solution.py:383
  11.9 3.6 %shard_map.58 = (f32[392,512]{1,0:T(8,128)S(1)}, f32[392,512]{1,0:T(8,128)S(1)}) custom-call(s32[1]{0:T(128)} %bitcast.me_ref, s32[8]{0:T(128)} %lengths_hbm.5, bf16[8,4,64,576]{3,2,1,0:T(8,128)(2,1)} %q_hbm.5, bf16[8,576,1024]{2,1,0:T(8,128)(2,1)} %bitcast.6, bf16[3,4,64,576]{3,2,1,0:T(8,128)(2,1)S(1)} %get-tuple-element.39.refs_0_, ...), custom_call_target="tpu_custom_call" | custom-call | flops 1000000000 | bytes 1 | tf_op jit(solution)/shard_map/pallas_call | solution.py:180
  15.6 0.4 shard_map.59
  15.9 1.6 %collective-permute-start.6 = (f32[200,512]{1,0:T(8,128)S(1)}, f32[200,512]{1,0:T(8,128)S(1)}, u32[]{:S(2)}, u32[]{:S(2)}) collective-permute-start(f32[200,512]{1,0:T(8,128)S(1)} %get-tuple-element.48), channel_id=1, source_target_pairs={{0,4},{1,3},{2,6},{3,1},{4,0},{5,7},{6,2},{7,5},{8,12},{9,11},{10,... | collective-permute-start | bytes 1228808 | tf_op jit(solution)/shard_map/ppermute | solution.py:383
  17.5 0.3 shard_map.60
  17.9 0.4 shard_map.61
  18.2 1.0 %collective-permute-start.5 = (f32[200,512]{1,0:T(8,128)S(1)}, f32[200,512]{1,0:T(8,128)S(1)}, u32[]{:S(2)}, u32[]{:S(2)}) collective-permute-start(f32[200,512]{1,0:T(8,128)S(1)} %get-tuple-element.47), channel_id=1, source_target_pairs={{0,2},{1,5},{2,0},{3,7},{4,6},{5,1},{6,4},{7,3},{8,10},{9,13},{10,... | collective-permute-start | bytes 1228808 | tf_op jit(solution)/shard_map/ppermute | solution.py:383
  19.2 1.5 %collective-permute-start.3 = (f32[72,512]{1,0:T(8,128)S(1)}, f32[72,512]{1,0:T(8,128)S(1)}, u32[]{:S(2)}, u32[]{:S(2)}) collective-permute-start(f32[72,512]{1,0:T(8,128)S(1)} %get-tuple-element.44), channel_id=1, source_target_pairs={{0,4},{1,3},{2,6},{3,1},{4,0},{5,7},{6,2},{7,5},{8,12},{9,11},{10,... | collective-permute-start | bytes 442376 | tf_op jit(solution)/shard_map/ppermute | solution.py:383
  20.7 6.1 %collective-permute-done.6.got_ref = f32[200,512]{1,0:T(8,128)S(1)} collective-permute-done((f32[200,512]{1,0:T(8,128)S(1)}, f32[200,512]{1,0:T(8,128)S(1)}, u32[]{:S(2)}, u32[]{:S(2)}) %collective-permute-start.6) | collective-permute-done | bytes 409632 | tf_op jit(solution)/shard_map/ppermute | solution.py:383
  26.8 0.3 shard_map.62
  27.1 1.5 %collective-permute-start.7 = (f32[104,512]{1,0:T(8,128)S(1)}, f32[104,512]{1,0:T(8,128)S(1)}, u32[]{:S(2)}, u32[]{:S(2)}) collective-permute-start(f32[104,512]{1,0:T(8,128)S(1)} %get-tuple-element.51), channel_id=1, source_target_pairs={{0,2},{1,5},{2,0},{3,7},{4,6},{5,1},{6,4},{7,3},{8,10},{9,13},{10,... | collective-permute-start | bytes 638984 | tf_op jit(solution)/shard_map/ppermute | solution.py:383
  28.6 0.8 %collective-permute-done.5.got_ref = f32[200,512]{1,0:T(8,128)S(1)} collective-permute-done((f32[200,512]{1,0:T(8,128)S(1)}, f32[200,512]{1,0:T(8,128)S(1)}, u32[]{:S(2)}, u32[]{:S(2)}) %collective-permute-start.5) | collective-permute-done | bytes 409632 | tf_op jit(solution)/shard_map/ppermute | solution.py:383
  29.4 0.3 shard_map.63
  29.8 1.6 %collective-permute-start.8 = (f32[104,512]{1,0:T(8,128)S(1)}, f32[104,512]{1,0:T(8,128)S(1)}, u32[]{:S(2)}, u32[]{:S(2)}) collective-permute-start(f32[104,512]{1,0:T(8,128)S(1)} %get-tuple-element.52), channel_id=1, source_target_pairs={{0,4},{1,3},{2,6},{3,1},{4,0},{5,7},{6,2},{7,5},{8,12},{9,11},{10,... | collective-permute-start | bytes 638984 | tf_op jit(solution)/shard_map/ppermute | solution.py:383
  31.6 1.5 %collective-permute-done.7.refs_1_ = f32[104,512]{1,0:T(8,128)S(1)} collective-permute-done((f32[104,512]{1,0:T(8,128)S(1)}, f32[104,512]{1,0:T(8,128)S(1)}, u32[]{:S(2)}, u32[]{:S(2)}) %collective-permute-start.7) | collective-permute-done | bytes 213024 | tf_op jit(solution)/shard_map/ppermute | solution.py:383
  33.4 2.3 %collective-permute-done.8.refs_3_ = f32[104,512]{1,0:T(8,128)S(1)} collective-permute-done((f32[104,512]{1,0:T(8,128)S(1)}, f32[104,512]{1,0:T(8,128)S(1)}, u32[]{:S(2)}, u32[]{:S(2)}) %collective-permute-start.8) | collective-permute-done | bytes 213024 | tf_op jit(solution)/shard_map/ppermute | solution.py:383
  35.7 0.5 %shard_map.66.heads_ref = bf16[32,1024]{1,0:T(8,128)(2,1)S(1)} custom-call(s32[1]{0:T(128)} %bitcast.me_ref, f32[4,64,128]{2,1,0:T(8,128)S(1)} %shard_map.64.refs_2_.refs_0_, f32[4,96,128]{2,1,0:T(8,128)S(1)} %shard_map.65.refs_1_, f32[104,512]{1,0:T(8,128)S(1)} %get-tuple-element.50.refs_2_, f32[104,512]{1,0:T(8,128)S(1)} %collective-permute-done.8.refs_3_, ...), custom_call_target="tpu_custom_call" | custom-call | flops 1 | bytes 1 | tf_op jit(solution)/shard_map/pallas_call | solution.py:304
  36.3 0.7 %shard_map.67.refs_0_ = f32[2,32,896]{2,1,0:T(8,128)S(1)} custom-call(s32[1]{0:T(128)} %bitcast.me_ref, bf16[32,1024]{1,0:T(8,128)(2,1)S(1)} %shard_map.66.heads_ref, bf16[1024,7168]{1,0:T(8,128)(2,1)S(1)} %bitcast.3), custom_call_target="tpu_custom_call" | custom-call | flops 5000000000 | bytes 1 | tf_op jit(solution)/shard_map/pallas_call | solution.py:325
  37.1 0.7 %shard_map.68.own_ref = f32[2,32,896]{2,1,0:T(8,128)S(1)} custom-call(s32[1]{0:T(128)} %bitcast.me_ref, bf16[32,1024]{1,0:T(8,128)(2,1)S(1)} %shard_map.66.heads_ref, bf16[1024,7168]{1,0:T(8,128)(2,1)S(1)} %bitcast.3, f32[2,32,896]{2,1,0:T(8,128)S(1)} %shard_map.67.refs_0_), custom_call_target="tpu_custom_call" | custom-call | flops 5000000000 | bytes 1 | tf_op jit(solution)/shard_map/pallas_call | solution.py:325
  37.8 0.7 %collective-permute-done.9.got_ref = f32[2,32,896]{2,1,0:T(8,128)S(1)} collective-permute-done((f32[2,32,896]{2,1,0:T(8,128)S(1)}, f32[2,32,896]{2,1,0:T(8,128)S(1)}, u32[]{:S(2)}, u32[]{:S(2)}) %collective-permute-start.9) | collective-permute-done | bytes 229408 | tf_op jit(solution)/shard_map/ppermute | solution.py:383
  38.6 1.6 %collective-permute-start.11 = (f32[32,896]{1,0:T(8,128)S(1)}, f32[32,896]{1,0:T(8,128)S(1)}, u32[]{:S(2)}, u32[]{:S(2)}) collective-permute-start(f32[32,896]{1,0:T(8,128)S(1)} %get-tuple-element.53.refs_0_), channel_id=1, source_target_pairs={{0,6},{1,7},{2,4},{3,5},{4,2},{5,3},{6,0},{7,1},{8,14},{9,15},{10,... | collective-permute-start | bytes 344072 | tf_op jit(solution)/shard_map/ppermute | solution.py:383
  40.1 0.7 %shard_map.70.refs_0_ = f32[2,32,896]{2,1,0:T(8,128)S(1)} custom-call(s32[1]{0:T(128)} %bitcast.me_ref, bf16[32,1024]{1,0:T(8,128)(2,1)S(1)} %shard_map.66.heads_ref, bf16[1024,7168]{1,0:T(8,128)(2,1)S(1)} %bitcast.3, f32[32,896]{1,0:T(8,128)S(1)} %get-tuple-element.53.refs_0_), custom_call_target="tpu_custom_call" | custom-call | flops 5000000000 | bytes 1 | tf_op jit(solution)/shard_map/pallas_call | solution.py:325
  40.9 0.7 %shard_map.71.own_ref = f32[2,32,896]{2,1,0:T(8,128)S(1)} custom-call(s32[1]{0:T(128)} %bitcast.me_ref, bf16[32,1024]{1,0:T(8,128)(2,1)S(1)} %shard_map.66.heads_ref, bf16[1024,7168]{1,0:T(8,128)(2,1)S(1)} %bitcast.3, f32[2,32,896]{2,1,0:T(8,128)S(1)} %shard_map.70.refs_0_), custom_call_target="tpu_custom_call" | custom-call | flops 5000000000 | bytes 1 | tf_op jit(solution)/shard_map/pallas_call | solution.py:325
  41.6 1.5 %collective-permute-start.12 = (f32[32,896]{1,0:T(8,128)S(1)}, f32[32,896]{1,0:T(8,128)S(1)}, u32[]{:S(2)}, u32[]{:S(2)}) collective-permute-start(f32[32,896]{1,0:T(8,128)S(1)} %get-tuple-element.55), channel_id=1, source_target_pairs={{0,2},{1,5},{2,0},{3,7},{4,6},{5,1},{6,4},{7,3},{8,10},{9,13},{10,... | collective-permute-start | bytes 344072 | tf_op jit(solution)/shard_map/ppermute | solution.py:383
  43.2 0.6 %collective-permute-start.13 = (f32[32,896]{1,0:T(8,128)S(1)}, f32[32,896]{1,0:T(8,128)S(1)}, u32[]{:S(2)}, u32[]{:S(2)}) collective-permute-start(f32[32,896]{1,0:T(8,128)S(1)} %get-tuple-element.56), channel_id=1, source_target_pairs={{0,4},{1,3},{2,6},{3,1},{4,0},{5,7},{6,2},{7,5},{8,12},{9,11},{10,... | collective-permute-start | bytes 344072 | tf_op jit(solution)/shard_map/ppermute | solution.py:383
  43.8 3.8 %collective-permute-done.12.refs_2_ = f32[32,896]{1,0:T(8,128)S(1)} collective-permute-done((f32[32,896]{1,0:T(8,128)S(1)}, f32[32,896]{1,0:T(8,128)S(1)}, u32[]{:S(2)}, u32[]{:S(2)}) %collective-permute-start.12) | collective-permute-done | bytes 114720 | tf_op jit(solution)/shard_map/ppermute | solution.py:383
  47.6 0.4 collective-permute-done.13.refs_3_
  48.1 0.7 %shard_map.73 = bf16[8,4,896]{2,1,0:T(4,128)(2,1)} custom-call(f32[32,896]{1,0:T(8,128)S(1)} %get-tuple-element.54.refs_0_, f32[32,896]{1,0:T(8,128)S(1)} %collective-permute-done.11.refs_1_, f32[32,896]{1,0:T(8,128)S(1)} %collective-permute-done.12.refs_2_, f32[32,896]{1,0:T(8,128)S(1)} %collective-permute-done.13.refs_3_), custom_call_target="tpu_custom_call" | custom-call | flops 1 | bytes 1 | tf_op jit(solution)/shard_map/pallas_call | solution.py:363
  (26 shorter events, 1.0 us)
Async XLA Ops:
  4.1 4.5 %collective-permute-start = (f32[264,512]{1,0:T(8,128)S(1)}, f32[264,512]{1,0:T(8,128)S(1)}, u32[]{:S(2)}, u32[]{:S(2)}) collective-permute-start(f32[264,512]{1,0:T(8,128)S(1)} %get-tuple-element.32), channel_id=1, source_target_pairs={{0,1},{1,0},{2,3},{3,2},{4,5},{5,4},{6,7},{7,6},{8,9},{9,8},{10,11... | collective-permute-start | bytes 1622024 | tf_op jit(solution)/shard_map/ppermute | solution.py:383
  8.4 7.1 %collective-permute-start.2 = (f32[392,512]{1,0:T(8,128)S(1)}, f32[392,512]{1,0:T(8,128)S(1)}, u32[]{:S(2)}, u32[]{:S(2)}) collective-permute-start(f32[392,512]{1,0:T(8,128)S(1)} %get-tuple-element.38), channel_id=1, source_target_pairs={{0,1},{1,0},{2,3},{3,2},{4,5},{5,4},{6,7},{7,6},{8,9},{9,8},{10,11... | collective-permute-start | bytes 2408456 | tf_op jit(solution)/shard_map/ppermute | solution.py:383
  8.9 8.6 %collective-permute-start.1 = (f32[136,512]{1,0:T(8,128)S(1)}, f32[136,512]{1,0:T(8,128)S(1)}, u32[]{:S(2)}, u32[]{:S(2)}) collective-permute-start(f32[136,512]{1,0:T(8,128)S(1)} %get-tuple-element.37), channel_id=1, source_target_pairs={{0,2},{1,5},{2,0},{3,7},{4,6},{5,1},{6,4},{7,3},{8,10},{9,13},{10,... | collective-permute-start | bytes 835592 | tf_op jit(solution)/shard_map/ppermute | solution.py:383
  15.5 2.4 %collective-permute-start.4 = (f32[392,512]{1,0:T(8,128)S(1)}, f32[392,512]{1,0:T(8,128)S(1)}, u32[]{:S(2)}, u32[]{:S(2)}) collective-permute-start(f32[392,512]{1,0:T(8,128)S(1)} %get-tuple-element.45), channel_id=1, source_target_pairs={{0,1},{1,0},{2,3},{3,2},{4,5},{5,4},{6,7},{7,6},{8,9},{9,8},{10,11... | collective-permute-start | bytes 2408456 | tf_op jit(solution)/shard_map/ppermute | solution.py:383
  15.9 10.9 %collective-permute-start.6 = (f32[200,512]{1,0:T(8,128)S(1)}, f32[200,512]{1,0:T(8,128)S(1)}, u32[]{:S(2)}, u32[]{:S(2)}) collective-permute-start(f32[200,512]{1,0:T(8,128)S(1)} %get-tuple-element.48), channel_id=1, source_target_pairs={{0,4},{1,3},{2,6},{3,1},{4,0},{5,7},{6,2},{7,5},{8,12},{9,11},{10,... | collective-permute-start | bytes 1228808 | tf_op jit(solution)/shard_map/ppermute | solution.py:383
  17.5 18.7 %slice-start = ((s8[14680064]{0:T(1024)(128)(4,1)}), s8[4194304]{0:T(1024)(128)(4,1)S(1)}, s32[]{:S(2)}) async-start(s8[14680064]{0:T(1024)(128)(4,1)} %bitcast.2), calls=%async_computation | async-start | bytes 8388608
  17.5 18.7 %slice-start.1 = ((s8[14680064]{0:T(1024)(128)(4,1)}), s8[4194304]{0:T(1024)(128)(4,1)S(1)}, s32[]{:S(2)}) async-start(s8[14680064]{0:T(1024)(128)(4,1)} %bitcast.2), calls=%async_computation.1 | async-start | bytes 8388608
  18.2 11.2 %collective-permute-start.5 = (f32[200,512]{1,0:T(8,128)S(1)}, f32[200,512]{1,0:T(8,128)S(1)}, u32[]{:S(2)}, u32[]{:S(2)}) collective-permute-start(f32[200,512]{1,0:T(8,128)S(1)} %get-tuple-element.47), channel_id=1, source_target_pairs={{0,2},{1,5},{2,0},{3,7},{4,6},{5,1},{6,4},{7,3},{8,10},{9,13},{10,... | collective-permute-start | bytes 1228808 | tf_op jit(solution)/shard_map/ppermute | solution.py:383
  19.2 12.1 %collective-permute-start.3 = (f32[72,512]{1,0:T(8,128)S(1)}, f32[72,512]{1,0:T(8,128)S(1)}, u32[]{:S(2)}, u32[]{:S(2)}) collective-permute-start(f32[72,512]{1,0:T(8,128)S(1)} %get-tuple-element.44), channel_id=1, source_target_pairs={{0,4},{1,3},{2,6},{3,1},{4,0},{5,7},{6,2},{7,5},{8,12},{9,11},{10,... | collective-permute-start | bytes 442376 | tf_op jit(solution)/shard_map/ppermute | solution.py:383
  27.1 5.9 %collective-permute-start.7 = (f32[104,512]{1,0:T(8,128)S(1)}, f32[104,512]{1,0:T(8,128)S(1)}, u32[]{:S(2)}, u32[]{:S(2)}) collective-permute-start(f32[104,512]{1,0:T(8,128)S(1)} %get-tuple-element.51), channel_id=1, source_target_pairs={{0,2},{1,5},{2,0},{3,7},{4,6},{5,1},{6,4},{7,3},{8,10},{9,13},{10,... | collective-permute-start | bytes 638984 | tf_op jit(solution)/shard_map/ppermute | solution.py:383
  29.4 6.8 %slice-start.2 = ((s8[14680064]{0:T(1024)(128)(4,1)}), s8[4194304]{0:T(1024)(128)(4,1)S(1)}, s32[]{:S(2)}) async-start(s8[14680064]{0:T(1024)(128)(4,1)} %bitcast.2), calls=%async_computation.2 | async-start | bytes 8388608
  29.4 6.8 %slice-start.3 = ((s8[14680064]{0:T(1024)(128)(4,1)}), s8[2097152]{0:T(1024)(128)(4,1)S(1)}, s32[]{:S(2)}) async-start(s8[14680064]{0:T(1024)(128)(4,1)} %bitcast.2), calls=%async_computation.3 | async-start | bytes 4194304
  29.8 5.9 %copy-start = (bf16[8,512,128]{2,1,0:T(8,128)(2,1)S(1)}, bf16[8,512,128]{2,1,0:T(8,128)(2,1)}, u32[]{:S(2)}) copy-start(bf16[8,512,128]{2,1,0:T(8,128)(2,1)} %refs_4_.1) | copy-start | bytes 3145732
  29.8 5.9 %collective-permute-start.8 = (f32[104,512]{1,0:T(8,128)S(1)}, f32[104,512]{1,0:T(8,128)S(1)}, u32[]{:S(2)}, u32[]{:S(2)}) collective-permute-start(f32[104,512]{1,0:T(8,128)S(1)} %get-tuple-element.52), channel_id=1, source_target_pairs={{0,4},{1,3},{2,6},{3,1},{4,0},{5,7},{6,2},{7,5},{8,12},{9,11},{10,... | collective-permute-start | bytes 638984 | tf_op jit(solution)/shard_map/ppermute | solution.py:383
  37.0 1.6 %collective-permute-start.9 = (f32[2,32,896]{2,1,0:T(8,128)S(1)}, f32[2,32,896]{2,1,0:T(8,128)S(1)}, u32[]{:S(2)}, u32[]{:S(2)}) collective-permute-start(f32[2,32,896]{2,1,0:T(8,128)S(1)} %shard_map.67.refs_0_), channel_id=1, source_target_pairs={{0,1},{1,0},{2,3},{3,2},{4,5},{5,4},{6,7},{7,6},{8,9},{9,8},{10,11... | collective-permute-start | bytes 688136 | tf_op jit(solution)/shard_map/ppermute | solution.py:383
  38.6 9.1 %collective-permute-start.11 = (f32[32,896]{1,0:T(8,128)S(1)}, f32[32,896]{1,0:T(8,128)S(1)}, u32[]{:S(2)}, u32[]{:S(2)}) collective-permute-start(f32[32,896]{1,0:T(8,128)S(1)} %get-tuple-element.53.refs_0_), channel_id=1, source_target_pairs={{0,6},{1,7},{2,4},{3,5},{4,2},{5,3},{6,0},{7,1},{8,14},{9,15},{10,... | collective-permute-start | bytes 344072 | tf_op jit(solution)/shard_map/ppermute | solution.py:383
  40.8 2.4 %collective-permute-start.10 = (f32[2,32,896]{2,1,0:T(8,128)S(1)}, f32[2,32,896]{2,1,0:T(8,128)S(1)}, u32[]{:S(2)}, u32[]{:S(2)}) collective-permute-start(f32[2,32,896]{2,1,0:T(8,128)S(1)} %shard_map.70.refs_0_), channel_id=1, source_target_pairs={{0,1},{1,0},{2,3},{3,2},{4,5},{5,4},{6,7},{7,6},{8,9},{9,8},{10,11... | collective-permute-start | bytes 688136 | tf_op jit(solution)/shard_map/ppermute | solution.py:383
  41.6 6.0 %collective-permute-start.12 = (f32[32,896]{1,0:T(8,128)S(1)}, f32[32,896]{1,0:T(8,128)S(1)}, u32[]{:S(2)}, u32[]{:S(2)}) collective-permute-start(f32[32,896]{1,0:T(8,128)S(1)} %get-tuple-element.55), channel_id=1, source_target_pairs={{0,2},{1,5},{2,0},{3,7},{4,6},{5,1},{6,4},{7,3},{8,10},{9,13},{10,... | collective-permute-start | bytes 344072 | tf_op jit(solution)/shard_map/ppermute | solution.py:383
  43.2 4.9 %collective-permute-start.13 = (f32[32,896]{1,0:T(8,128)S(1)}, f32[32,896]{1,0:T(8,128)S(1)}, u32[]{:S(2)}, u32[]{:S(2)}) collective-permute-start(f32[32,896]{1,0:T(8,128)S(1)} %get-tuple-element.56), channel_id=1, source_target_pairs={{0,4},{1,3},{2,6},{3,1},{4,0},{5,7},{6,2},{7,5},{8,12},{9,11},{10,... | collective-permute-start | bytes 344072 | tf_op jit(solution)/shard_map/ppermute | solution.py:383

commit v4 on v1

--- a/solution.py
+++ b/solution.py
@@ -49,7 +49,7 @@
     nq, heads, lat = q_hbm.shape[1:]
     rows = nq * heads
     tokens = cache_hbm.shape[2]
-    kvr = keep.shape[1]
+    kvr = acc_buf.shape[2]
     me = me_ref[0]
     length_copy = pltpu.make_async_copy(lengths_hbm, lengths, length_sem)
     length_copy.start()
@@ -76,7 +76,7 @@
     token = lax.broadcasted_iota(jnp.int32, (BLOCK, tokens), 1)
     lane = lax.broadcasted_iota(jnp.int32, (BLOCK, 128), 1)
     for out in (keep, send):
-        out[out.shape[0] - OWN :, :] = jnp.zeros((OWN, kvr), jnp.float32)
+        out[out.shape[0] - OWN :, :] = jnp.zeros((OWN, 128), jnp.float32)
     length_copy.wait()
 
     def score_piece(i, start):
@@ -126,11 +126,13 @@
                 for j in range(nq):
                     source = pl.multiple_of(j * heads + group(me, q, mate, turn) * OWN, OWN)
                     to = ((q * count + i) * nq + j) * OWN
-                    out[to : to + OWN, :] = acc_buf[i % 2, pl.ds(source, OWN), :]
+                    for k in range(kvr // 128):
+                        at = k * 4 * count * nq * OWN + to
+                        out[at : at + OWN, :] = acc_buf[i % 2, pl.ds(source, OWN), k * 128 : (k + 1) * 128]
         for part in range(rows // 128):
             for out in (keep, send):
-                at = out.shape[0] - OWN + i
-                out[at : at + 1, part * 128 : (part + 1) * 128] = tails[i, part]
+                at = out.shape[0] - OWN + i * (rows // 128) + part
+                out[at : at + 1, :] = tails[i, part]
 
     def pieces(stage, i):
         if not 0 <= i < count:
@@ -156,7 +158,7 @@
     batch, nq, heads, lat = queries.shape
     tokens = cache.shape[2]
     rows = nq * heads
-    out_rows = count * rows // 2 + OWN
+    out_rows = kvr // 128 * count * rows // 2 + OWN
     scratch = [
         pltpu.VMEM((2, rows, tokens), jnp.float32),
         pltpu.VMEM((2, rows, tokens), jnp.bfloat16),
@@ -171,7 +173,7 @@
             pltpu.VMEM((count, lat, tokens), jnp.bfloat16),
             pltpu.SemaphoreType.DMA((count, PIECES + 1)),
         ]
-    out_shape = [jax.ShapeDtypeStruct((out_rows, kvr), jnp.float32)] * 2
+    out_shape = [jax.ShapeDtypeStruct((out_rows, 128), jnp.float32)] * 2
     if following:
         out_shape += [
             jax.ShapeDtypeStruct((following, nq, heads, lat), jnp.bfloat16),
@@ -189,8 +191,7 @@
 
 
 def merged(refs, shares):
-    lanes = shares.shape[1]
-    logs = [ref[ref.shape[0] - OWN :, :lanes] for ref in refs]
+    logs = [ref[ref.shape[0] - OWN :, :] for ref in refs]
     largest = functools.reduce(jnp.maximum, logs)
     parts = [jnp.exp(log - largest) for log in logs]
     total = sum(parts[1:], parts[0])
@@ -199,40 +200,43 @@
     return largest + jnp.log(total)
 
 
-def merged_rows(refs, shares, me, heads, batch, q, b, j, turn):
-    at = pl.ds(pl.multiple_of(j * heads + group(me, q, 0, turn) * OWN, OWN), OWN)
-    source = ((q * batch + b) * (shares.shape[1] // heads) + j) * OWN
-    rows = slice(source, source + OWN)
-    terms_of = [shares[k, at, b : b + 1] * ref[rows, :] for k, ref in enumerate(refs)]
-    return sum(terms_of[1:], terms_of[0])
-
-
-def combine_kernel(places, pieces, batch, heads, turn, me_ref, keep_ref, got_ref, *refs):
+def merged_rows(refs, shares, me, sizes, places, q, b, j, turn):
+    batch, nq, heads = sizes
+    line, within = divmod(b * nq * heads + j * heads, 128)
+    at = pl.ds(pl.multiple_of(within + group(me, q, 0, turn) * OWN, OWN), OWN)
+    columns = [shares[k, at, line : line + 1] for k in range(len(refs))]
+    height = places * batch * nq * OWN
+    source = ((q * batch + b) * nq + j) * OWN
+    for start in range(source, refs[0].shape[0] - OWN, height):
+        terms_of = [column * ref[start : start + OWN, :] for column, ref in zip(columns, refs)]
+        yield sum(terms_of[1:], terms_of[0])
+
+
+def combine_kernel(places, pieces, sizes, turn, me_ref, keep_ref, got_ref, *refs):
     *outs, shares = refs[len(refs) - pieces - 1 :]
     lse = merged((keep_ref, got_ref), shares)
-    lanes = shares.shape[1]
-    size = batch * (lanes // heads) * OWN
+    batch, nq, _ = sizes
+    size = batch * nq * OWN
     for q in range(places):
         side, at = divmod(q, places // pieces)
         for b in range(batch):
-            for j in range(lanes // heads):
-                to = at * size + (b * (lanes // heads) + j) * OWN
-                outs[side][to : to + OWN, :] = merged_rows(
-                    (keep_ref, got_ref), shares, me_ref[0], heads, batch, q, b, j, turn
-                )
+            for j in range(nq):
+                blocks = merged_rows((keep_ref, got_ref), shares, me_ref[0], sizes, places, q, b, j, turn)
+                for k, block in enumerate(blocks):
+                    to = (k * (places // pieces) + at) * size + (b * nq + j) * OWN
+                    outs[side][to : to + OWN, :] = block
     for out in outs:
-        out[out.shape[0] - OWN :, :] = jnp.zeros((OWN, out.shape[1]), jnp.float32)
-        out[out.shape[0] - OWN :, :lanes] = lse
-
-
-def combine(me, keep, got, places, pieces, batch, heads, lanes, turn, after, length):
+        out[out.shape[0] - OWN :, :] = lse
+
+
+def combine(me, keep, got, places, pieces, sizes, turn, after, length):
     out_rows = (keep.shape[0] - OWN) // pieces + OWN
     return pl.pallas_call(
-        functools.partial(combine_kernel, places, pieces, batch, heads, turn),
+        functools.partial(combine_kernel, places, pieces, sizes, turn),
         in_specs=[SM, VM, VM] + [ANY] * len(after),
         out_specs=[VM] * pieces,
-        out_shape=[jax.ShapeDtypeStruct((out_rows, keep.shape[1]), jnp.float32)] * pieces,
-        scratch_shapes=[pltpu.VMEM((2, lanes, OWN), jnp.float32)],
+        out_shape=[jax.ShapeDtypeStruct((out_rows, 128), jnp.float32)] * pieces,
+        scratch_shapes=[pltpu.VMEM((2, 128, OWN), jnp.float32)],
         compiler_params=pltpu.CompilerParams(vmem_limit_bytes=16 * MIB),
         cost_estimate=declared(length),
     )(me, keep, got, *after)
@@ -253,39 +257,42 @@
     )(*after)
 
 
-def attend_rows(batch, heads, me, refs, shares, attended):
+def attend_rows(sizes, me, refs, shares, attended):
     merged(refs, shares)
-    positions = shares.shape[1] // heads
+    batch, nq, _ = sizes
     for b in range(batch):
-        for j in range(positions):
-            to = (b * positions + j) * OWN
-            rows = merged_rows(refs, shares, me, heads, batch, 0, b, j, 0)
-            for k in range(attended.shape[0]):
-                attended[k, to : to + OWN, :] = rows[:, k * 128 : (k + 1) * 128]
-
-
-def last_merge_kernel(batch, heads, count, me_ref, *refs):
+        for j in range(nq):
+            to = (b * nq + j) * OWN
+            for k, block in enumerate(merged_rows(refs, shares, me, sizes, 1, 0, b, j, 0)):
+                attended[k, to : to + OWN, :] = block
+
+
+def attended_shape(array, sizes):
+    rows = sizes[0] * sizes[1] * OWN
+    return ((array.shape[0] - OWN) // rows, rows, 128)
+
+
+def last_merge_kernel(sizes, count, me_ref, *refs):
     out_ref, shares = refs[-2:]
-    attend_rows(batch, heads, me_ref[0], refs[:count], shares, out_ref)
-
-
-def last_merge(me, arrays, batch, heads, lanes, after, length):
-    rows, kvr = arrays[0].shape
-    return pl.pallas_call(
-        functools.partial(last_merge_kernel, batch, heads, len(arrays)),
+    attend_rows(sizes, me_ref[0], refs[:count], shares, out_ref)
+
+
+def last_merge(me, arrays, sizes, after, length):
+    return pl.pallas_call(
+        functools.partial(last_merge_kernel, sizes, len(arrays)),
         in_specs=[SM] + [VM] * len(arrays) + [ANY] * len(after),
         out_specs=VM,
-        out_shape=jax.ShapeDtypeStruct((kvr // 128, rows - OWN, 128), jnp.float32),
-        scratch_shapes=[pltpu.VMEM((len(arrays), lanes, OWN), jnp.float32)],
+        out_shape=jax.ShapeDtypeStruct(attended_shape(arrays[0], sizes), jnp.float32),
+        scratch_shapes=[pltpu.VMEM((len(arrays), 128, OWN), jnp.float32)],
         compiler_params=pltpu.CompilerParams(vmem_limit_bytes=16 * MIB),
         cost_estimate=declared(length),
     )(me, *arrays, *after)
 
 
-def heads_kernel(batch, heads, count, me_ref, *refs):
+def heads_kernel(sizes, count, me_ref, *refs):
     early, refs = refs[: -count - 4], refs[-count - 4 :]
     arrays, (up_ref, out_ref, shares, attended) = refs[:count], refs[count:]
-    attend_rows(batch, heads, me_ref[0], arrays, shares, attended)
+    attend_rows(sizes, me_ref[0], arrays, shares, attended)
     width = up_ref.shape[2]
     for i in range(OWN):
         own = [
@@ -297,16 +304,15 @@
         out_ref[:, i * width : (i + 1) * width] = head_out.astype(jnp.bfloat16)
 
 
-def heads_out(me, early, arrays, batch, value_up, heads, lanes):
-    rows, kvr = arrays[0].shape
-    shape = (kvr // 128, rows - OWN, 128)
+def heads_out(me, early, arrays, sizes, value_up):
+    shape = attended_shape(arrays[0], sizes)
     places = sum(array.shape[1] for array in early) // OWN + shape[1] // OWN
     return pl.pallas_call(
-        functools.partial(heads_kernel, batch, heads, len(arrays)),
+        functools.partial(heads_kernel, sizes, len(arrays)),
         in_specs=[SM] + [VM] * (len(early) + len(arrays) + 1),
         out_specs=VM,
         out_shape=jax.ShapeDtypeStruct((places, OWN * value_up.shape[2]), jnp.bfloat16),
-        scratch_shapes=[pltpu.VMEM((len(arrays), lanes, OWN), jnp.float32), pltpu.VMEM(shape, jnp.float32)],
+        scratch_shapes=[pltpu.VMEM((len(arrays), 128, OWN), jnp.float32), pltpu.VMEM(shape, jnp.float32)],
         compiler_params=pltpu.CompilerParams(vmem_limit_bytes=16 * MIB),
         cost_estimate=declared(0),
     )(me, *early, *arrays, value_up)
@@ -373,7 +379,6 @@
 def local(n, queries, latent_cache, context_lengths, value_up, output_projection_rows):
     batch, nq, heads, _ = queries.shape
     kvr = value_up.shape[1]
-    lanes = nq * heads
     me = lax.axis_index("seq").astype(jnp.int32).reshape(1)
     queries = pltpu.with_memory_space_constraint(queries, pltpu.HBM)
     cache = pltpu.with_memory_space_constraint(jnp.swapaxes(latent_cache, 1, 2), pltpu.HBM)
@@ -394,7 +399,7 @@
     after, ready = (), ()
     for entry in ORDER.split():
         kind, p, length = entry[0], int(entry[1]), int(entry[3:])
-        turn = p & 1
+        turn, sizes = p & 1, (PARTS[p], nq, heads)
         if kind == "N":
             after = (order(after, length),)
         elif kind == "A":
@@ -405,7 +410,7 @@
             keep[p], send[p], ready = outs[0], outs[1:2], outs[2:]
             after = (keep[p],)
         elif kind == "M":
-            early[p] = last_merge(me, arrived(p), PARTS[p], heads, lanes, after, length)
+            early[p] = last_merge(me, arrived(p), sizes, after, length)
             after = (early[p],)
         else:
             step = "CS".index(kind)
@@ -416,9 +421,7 @@
                 swap(send[p][0], step, turn),
                 4 >> step,
                 pieces,
-                PARTS[p],
-                heads,
-                lanes,
+                sizes,
                 turn,
                 after,
                 length,
@@ -426,7 +429,7 @@
             after = (keep[p],)
 
     last = len(PARTS) - 1
-    flat = heads_out(me, [early[p] for p in range(last)], arrived(last), PARTS[last], value_up, heads, lanes)
+    flat = heads_out(me, [early[p] for p in range(last)], arrived(last), (PARTS[last], nq, heads), value_up)
     width = output_projection_rows.shape[1] // n
     sums = {}
     after = ()

time: 47.5 us -> 46.5 us (0.979)
  waiting for transfers between devices: 13.6 us -> 12.3 us
    ppermute x17, waiting for transfers between devices: 13.6 us -> 12.3 us  [swap(): return lax.ppermute(array, 'seq', pairs_of(n, step, turn))]
  transfers between devices with their start and end apart: 17 -> 17, of which waited for: 9 -> 8; matrix products, arithmetic and copies ran while one was open for 0% -> 0% of each run, Pallas kernels for 29% -> 30%
where the time goes in v4:
time: 46.5 us; the launch traced here: 46.4 us
  Pallas kernels  19.6 us (42%)
  starting transfers between devices  14.2 us (31%)
  waiting for transfers between devices  12.3 us (26%)
    ppermute x17, starting transfers between devices, swap(): return lax.ppermute(array, 'seq', pairs_of(n, step, turn))  14.2 us
    ppermute x17, waiting for transfers between devices, swap(): return lax.ppermute(array, 'seq', pairs_of(n, step, turn))  12.3 us
    pallas_call x4, Pallas kernels, attention(): pl.pallas_call(functools.partial(attention_kernel, first, count, turn, le...  12 us
    pallas_call x4, Pallas kernels, terms(): pl.pallas_call(functools.partial(terms_kernel, mate, places), in_specs=[S...  2.85 us
    pallas_call x8, Pallas kernels, combine(): pl.pallas_call(functools.partial(combine_kernel, places, pieces, sizes, t...  2.7 us
  transfers between devices with their start and end apart: 17, of which 8 were waited for; matrix products, arithmetic and copies ran while one was open for 0% of the time, Pallas kernels for 30%

profile of v4, /device:TPU:0, one launch (start us, length us, event | category | flops | bytes accessed | tf_op | source)
XLA Modules:
  0.0 46.4 jit_solution(4644729966581978080)
XLA Ops:
  0.0 3.7 %shard_map.55 = (f32[1032,128]{1,0:T(8,128)S(1)}, f32[1032,128]{1,0:T(8,128)S(1)}, bf16[2,4,64,576]{3,2,1,0:T(8,128)(2,1)S(1)}, bf16[2,576,1024]{2,1,0:T(8,128)(2,1)S(1)}) custom-call(s32[1]{0:T(128)} %bitcast.me_ref, s32[8]{0:T(128)} %lengths_hbm.7, bf16[8,4,64,576]{3,2,1,0:T(8,128)(2,1)} %q_hbm.7, bf16[8,576,1024]{2,1,0:T(8,128)(2,1)} %bitcast.4), custom_call_target="tpu_custom_call" | custom-call | flops 1000000000 | bytes 1 | tf_op jit(solution)/shard_map/pallas_call | solution.py:182
  3.8 0.5 %collective-permute-start = (f32[1032,128]{1,0:T(8,128)S(1)}, f32[1032,128]{1,0:T(8,128)S(1)}, u32[]{:S(2)}, u32[]{:S(2)}) collective-permute-start(f32[1032,128]{1,0:T(8,128)S(1)} %get-tuple-element.40), channel_id=1, source_target_pairs={{0,1},{1,0},{2,3},{3,2},{4,5},{5,4},{6,7},{7,6},{8,9},{9,8},{10,11... | collective-permute-start | bytes 1585160 | tf_op jit(solution)/shard_map/ppermute | solution.py:388
  4.3 2.8 %shard_map.56 = (f32[1032,128]{1,0:T(8,128)S(1)}, f32[1032,128]{1,0:T(8,128)S(1)}, bf16[2,4,64,576]{3,2,1,0:T(8,128)(2,1)S(1)}, bf16[2,576,1024]{2,1,0:T(8,128)(2,1)S(1)}) custom-call(s32[1]{0:T(128)} %bitcast.me_ref, s32[8]{0:T(128)} %lengths_hbm.7, bf16[8,4,64,576]{3,2,1,0:T(8,128)(2,1)} %q_hbm.7, bf16[8,576,1024]{2,1,0:T(8,128)(2,1)} %bitcast.5, ...), custom_call_target="tpu_custom_call" | custom-call | flops 1000000000 | bytes 1 | tf_op jit(solution)/shard_map/pallas_call | solution.py:182
  7.5 3.0 %collective-permute-start.1 = (f32[520,128]{1,0:T(8,128)S(1)}, f32[520,128]{1,0:T(8,128)S(1)}, u32[]{:S(2)}, u32[]{:S(2)}) collective-permute-start(f32[520,128]{1,0:T(8,128)S(1)} %get-tuple-element.45), channel_id=1, source_target_pairs={{0,2},{1,5},{2,0},{3,7},{4,6},{5,1},{6,4},{7,3},{8,10},{9,13},{10,... | collective-permute-start | bytes 798728 | tf_op jit(solution)/shard_map/ppermute | solution.py:388
  10.5 2.8 %shard_map.58 = (f32[1032,128]{1,0:T(8,128)S(1)}, f32[1032,128]{1,0:T(8,128)S(1)}, bf16[2,4,64,576]{3,2,1,0:T(8,128)(2,1)S(1)}, bf16[2,576,1024]{2,1,0:T(8,128)(2,1)S(1)}) custom-call(s32[1]{0:T(128)} %bitcast.me_ref, s32[8]{0:T(128)} %lengths_hbm.7, bf16[8,4,64,576]{3,2,1,0:T(8,128)(2,1)} %q_hbm.7, bf16[8,576,1024]{2,1,0:T(8,128)(2,1)} %bitcast.6, ...), custom_call_target="tpu_custom_call" | custom-call | flops 1000000000 | bytes 1 | tf_op jit(solution)/shard_map/pallas_call | solution.py:182
  13.4 0.4 shard_map.59
  13.8 1.6 %collective-permute-start.8 = (f32[520,128]{1,0:T(8,128)S(1)}, f32[520,128]{1,0:T(8,128)S(1)}, u32[]{:S(2)}, u32[]{:S(2)}) collective-permute-start(f32[520,128]{1,0:T(8,128)S(1)} %get-tuple-element.62), channel_id=1, source_target_pairs={{0,4},{1,3},{2,6},{3,1},{4,0},{5,7},{6,2},{7,5},{8,12},{9,11},{10,... | collective-permute-start | bytes 798728 | tf_op jit(solution)/shard_map/ppermute | solution.py:388
  15.4 2.7 %shard_map.60 = (f32[1032,128]{1,0:T(8,128)S(1)}, f32[1032,128]{1,0:T(8,128)S(1)}) custom-call(s32[1]{0:T(128)} %bitcast.me_ref, s32[8]{0:T(128)} %lengths_hbm.7, bf16[8,4,64,576]{3,2,1,0:T(8,128)(2,1)} %q_hbm.7, bf16[8,576,1024]{2,1,0:T(8,128)(2,1)} %bitcast.7, bf16[2,4,64,576]{3,2,1,0:T(8,128)(2,1)S(1)} %get-tuple-element.50.refs_0_, ...), custom_call_target="tpu_custom_call" | custom-call | flops 1000000000 | bytes 1 | tf_op jit(solution)/shard_map/pallas_call | solution.py:182
  18.1 0.4 shard_map.61
  18.5 0.7 %collective-permute-start.7 = (f32[520,128]{1,0:T(8,128)S(1)}, f32[520,128]{1,0:T(8,128)S(1)}, u32[]{:S(2)}, u32[]{:S(2)}) collective-permute-start(f32[520,128]{1,0:T(8,128)S(1)} %get-tuple-element.61), channel_id=1, source_target_pairs={{0,2},{1,5},{2,0},{3,7},{4,6},{5,1},{6,4},{7,3},{8,10},{9,13},{10,... | collective-permute-start | bytes 798728 | tf_op jit(solution)/shard_map/ppermute | solution.py:388
  19.6 0.5 collective-permute-done.5.got_ref
  20.4 1.1 %collective-permute-start.6 = (f32[520,128]{1,0:T(8,128)S(1)}, f32[520,128]{1,0:T(8,128)S(1)}, u32[]{:S(2)}, u32[]{:S(2)}) collective-permute-start(f32[520,128]{1,0:T(8,128)S(1)} %get-tuple-element.60), channel_id=1, source_target_pairs={{0,4},{1,3},{2,6},{3,1},{4,0},{5,7},{6,2},{7,5},{8,12},{9,11},{10,... | collective-permute-start | bytes 798728 | tf_op jit(solution)/shard_map/ppermute | solution.py:388
  21.6 0.9 %collective-permute-start.4 = (f32[264,128]{1,0:T(8,128)S(1)}, f32[264,128]{1,0:T(8,128)S(1)}, u32[]{:S(2)}, u32[]{:S(2)}) collective-permute-start(f32[264,128]{1,0:T(8,128)S(1)} %get-tuple-element.57), channel_id=1, source_target_pairs={{0,4},{1,3},{2,6},{3,1},{4,0},{5,7},{6,2},{7,5},{8,12},{9,11},{10,... | collective-permute-start | bytes 405512 | tf_op jit(solution)/shard_map/ppermute | solution.py:388
  22.8 1.0 %collective-permute-start.9 = (f32[264,128]{1,0:T(8,128)S(1)}, f32[264,128]{1,0:T(8,128)S(1)}, u32[]{:S(2)}, u32[]{:S(2)}) collective-permute-start(f32[264,128]{1,0:T(8,128)S(1)} %get-tuple-element.66), channel_id=1, source_target_pairs={{0,2},{1,5},{2,0},{3,7},{4,6},{5,1},{6,4},{7,3},{8,10},{9,13},{10,... | collective-permute-start | bytes 405512 | tf_op jit(solution)/shard_map/ppermute | solution.py:388
  23.8 3.0 %collective-permute-done.7.got_ref = f32[520,128]{1,0:T(8,128)S(1)} collective-permute-done((f32[520,128]{1,0:T(8,128)S(1)}, f32[520,128]{1,0:T(8,128)S(1)}, u32[]{:S(2)}, u32[]{:S(2)}) %collective-permute-start.7) | collective-permute-done | bytes 266272 | tf_op jit(solution)/shard_map/ppermute | solution.py:388
  27.1 0.5 %collective-permute-start.10 = (f32[264,128]{1,0:T(8,128)S(1)}, f32[264,128]{1,0:T(8,128)S(1)}, u32[]{:S(2)}, u32[]{:S(2)}) collective-permute-start(f32[264,128]{1,0:T(8,128)S(1)} %get-tuple-element.67), channel_id=1, source_target_pairs={{0,4},{1,3},{2,6},{3,1},{4,0},{5,7},{6,2},{7,5},{8,12},{9,11},{10,... | collective-permute-start | bytes 405512 | tf_op jit(solution)/shard_map/ppermute | solution.py:388
  27.6 1.2 %collective-permute-done.6.got_ref = f32[520,128]{1,0:T(8,128)S(1)} collective-permute-done((f32[520,128]{1,0:T(8,128)S(1)}, f32[520,128]{1,0:T(8,128)S(1)}, u32[]{:S(2)}, u32[]{:S(2)}) %collective-permute-start.6) | collective-permute-done | bytes 266272 | tf_op jit(solution)/shard_map/ppermute | solution.py:388
  29.1 0.7 %collective-permute-start.11 = (f32[264,128]{1,0:T(8,128)S(1)}, f32[264,128]{1,0:T(8,128)S(1)}, u32[]{:S(2)}, u32[]{:S(2)}) collective-permute-start(f32[264,128]{1,0:T(8,128)S(1)} %get-tuple-element.68), channel_id=1, source_target_pairs={{0,2},{1,5},{2,0},{3,7},{4,6},{5,1},{6,4},{7,3},{8,10},{9,13},{10,... | collective-permute-start | bytes 405512 | tf_op jit(solution)/shard_map/ppermute | solution.py:388
  29.9 0.4 collective-permute-done.4.refs_1_
  30.8 1.5 %collective-permute-done.10.refs_1_ = f32[264,128]{1,0:T(8,128)S(1)} collective-permute-done((f32[264,128]{1,0:T(8,128)S(1)}, f32[264,128]{1,0:T(8,128)S(1)}, u32[]{:S(2)}, u32[]{:S(2)}) %collective-permute-start.10) | collective-permute-done | bytes 135200 | tf_op jit(solution)/shard_map/ppermute | solution.py:388
  32.6 1.6 %collective-permute-done.11.refs_4_ = f32[264,128]{1,0:T(8,128)S(1)} collective-permute-done((f32[264,128]{1,0:T(8,128)S(1)}, f32[264,128]{1,0:T(8,128)S(1)}, u32[]{:S(2)}, u32[]{:S(2)}) %collective-permute-start.11) | collective-permute-done | bytes 135200 | tf_op jit(solution)/shard_map/ppermute | solution.py:388
  34.2 0.5 %shard_map.70.heads_ref = bf16[32,1024]{1,0:T(8,128)(2,1)S(1)} custom-call(s32[1]{0:T(128)} %bitcast.me_ref, f32[4,64,128]{2,1,0:T(8,128)S(1)} %shard_map.67.refs_2_.refs_0_, f32[4,64,128]{2,1,0:T(8,128)S(1)} %shard_map.68.refs_2_.refs_1_, f32[4,64,128]{2,1,0:T(8,128)S(1)} %shard_map.69.refs_2_, f32[264,128]{1,0:T(8,128)S(1)} %get-tuple-element.65.refs_2_.refs_3_, ...), custom_call_target="tpu_custom_call" | custom-call | flops 1 | bytes 1 | tf_op jit(solution)/shard_map/pallas_call | solution.py:310
  34.8 0.7 %shard_map.71.refs_0_ = f32[2,32,896]{2,1,0:T(8,128)S(1)} custom-call(s32[1]{0:T(128)} %bitcast.me_ref, bf16[32,1024]{1,0:T(8,128)(2,1)S(1)} %shard_map.70.heads_ref, bf16[1024,7168]{1,0:T(8,128)(2,1)S(1)} %bitcast.3), custom_call_target="tpu_custom_call" | custom-call | flops 5000000000 | bytes 1 | tf_op jit(solution)/shard_map/pallas_call | solution.py:331
  35.6 0.7 %shard_map.72.own_ref = f32[2,32,896]{2,1,0:T(8,128)S(1)} custom-call(s32[1]{0:T(128)} %bitcast.me_ref, bf16[32,1024]{1,0:T(8,128)(2,1)S(1)} %shard_map.70.heads_ref, bf16[1024,7168]{1,0:T(8,128)(2,1)S(1)} %bitcast.3, f32[2,32,896]{2,1,0:T(8,128)S(1)} %shard_map.71.refs_0_), custom_call_target="tpu_custom_call" | custom-call | flops 5000000000 | bytes 1 | tf_op jit(solution)/shard_map/pallas_call | solution.py:331
  36.3 0.7 %collective-permute-done.12.got_ref = f32[2,32,896]{2,1,0:T(8,128)S(1)} collective-permute-done((f32[2,32,896]{2,1,0:T(8,128)S(1)}, f32[2,32,896]{2,1,0:T(8,128)S(1)}, u32[]{:S(2)}, u32[]{:S(2)}) %collective-permute-start.12) | collective-permute-done | bytes 229408 | tf_op jit(solution)/shard_map/ppermute | solution.py:388
  37.1 1.3 %collective-permute-start.14 = (f32[32,896]{1,0:T(8,128)S(1)}, f32[32,896]{1,0:T(8,128)S(1)}, u32[]{:S(2)}, u32[]{:S(2)}) collective-permute-start(f32[32,896]{1,0:T(8,128)S(1)} %get-tuple-element.69.refs_0_), channel_id=1, source_target_pairs={{0,6},{1,7},{2,4},{3,5},{4,2},{5,3},{6,0},{7,1},{8,14},{9,15},{10,... | collective-permute-start | bytes 344072 | tf_op jit(solution)/shard_map/ppermute | solution.py:388
  38.4 0.7 %shard_map.74.refs_0_ = f32[2,32,896]{2,1,0:T(8,128)S(1)} custom-call(s32[1]{0:T(128)} %bitcast.me_ref, bf16[32,1024]{1,0:T(8,128)(2,1)S(1)} %shard_map.70.heads_ref, bf16[1024,7168]{1,0:T(8,128)(2,1)S(1)} %bitcast.3, f32[32,896]{1,0:T(8,128)S(1)} %get-tuple-element.69.refs_0_), custom_call_target="tpu_custom_call" | custom-call | flops 5000000000 | bytes 1 | tf_op jit(solution)/shard_map/pallas_call | solution.py:331
  39.1 0.7 %shard_map.75.own_ref = f32[2,32,896]{2,1,0:T(8,128)S(1)} custom-call(s32[1]{0:T(128)} %bitcast.me_ref, bf16[32,1024]{1,0:T(8,128)(2,1)S(1)} %shard_map.70.heads_ref, bf16[1024,7168]{1,0:T(8,128)(2,1)S(1)} %bitcast.3, f32[2,32,896]{2,1,0:T(8,128)S(1)} %shard_map.74.refs_0_), custom_call_target="tpu_custom_call" | custom-call | flops 5000000000 | bytes 1 | tf_op jit(solution)/shard_map/pallas_call | solution.py:331
  39.9 0.9 %collective-permute-start.15 = (f32[32,896]{1,0:T(8,128)S(1)}, f32[32,896]{1,0:T(8,128)S(1)}, u32[]{:S(2)}, u32[]{:S(2)}) collective-permute-start(f32[32,896]{1,0:T(8,128)S(1)} %get-tuple-element.71), channel_id=1, source_target_pairs={{0,2},{1,5},{2,0},{3,7},{4,6},{5,1},{6,4},{7,3},{8,10},{9,13},{10,... | collective-permute-start | bytes 344072 | tf_op jit(solution)/shard_map/ppermute | solution.py:388
  40.8 1.5 %collective-permute-start.16 = (f32[32,896]{1,0:T(8,128)S(1)}, f32[32,896]{1,0:T(8,128)S(1)}, u32[]{:S(2)}, u32[]{:S(2)}) collective-permute-start(f32[32,896]{1,0:T(8,128)S(1)} %get-tuple-element.72), channel_id=1, source_target_pairs={{0,4},{1,3},{2,6},{3,1},{4,0},{5,7},{6,2},{7,5},{8,12},{9,11},{10,... | collective-permute-start | bytes 344072 | tf_op jit(solution)/shard_map/ppermute | solution.py:388
  42.3 3.3 %collective-permute-done.15.refs_2_ = f32[32,896]{1,0:T(8,128)S(1)} collective-permute-done((f32[32,896]{1,0:T(8,128)S(1)}, f32[32,896]{1,0:T(8,128)S(1)}, u32[]{:S(2)}, u32[]{:S(2)}) %collective-permute-start.15) | collective-permute-done | bytes 114720 | tf_op jit(solution)/shard_map/ppermute | solution.py:388
  45.7 0.7 %shard_map.77 = bf16[8,4,896]{2,1,0:T(4,128)(2,1)} custom-call(f32[32,896]{1,0:T(8,128)S(1)} %get-tuple-element.70.refs_0_, f32[32,896]{1,0:T(8,128)S(1)} %collective-permute-done.14.refs_1_, f32[32,896]{1,0:T(8,128)S(1)} %collective-permute-done.15.refs_2_, f32[32,896]{1,0:T(8,128)S(1)} %collective-permute-done.16.refs_3_), custom_call_target="tpu_custom_call" | custom-call | flops 1 | bytes 1 | tf_op jit(solution)/shard_map/pallas_call | solution.py:369
  (36 shorter events, 3.3 us)
Async XLA Ops:
  3.8 3.4 %collective-permute-start = (f32[1032,128]{1,0:T(8,128)S(1)}, f32[1032,128]{1,0:T(8,128)S(1)}, u32[]{:S(2)}, u32[]{:S(2)}) collective-permute-start(f32[1032,128]{1,0:T(8,128)S(1)} %get-tuple-element.40), channel_id=1, source_target_pairs={{0,1},{1,0},{2,3},{3,2},{4,5},{5,4},{6,7},{7,6},{8,9},{9,8},{10,11... | collective-permute-start | bytes 1585160 | tf_op jit(solution)/shard_map/ppermute | solution.py:388
  7.1 6.3 %collective-permute-start.3 = (f32[1032,128]{1,0:T(8,128)S(1)}, f32[1032,128]{1,0:T(8,128)S(1)}, u32[]{:S(2)}, u32[]{:S(2)}) collective-permute-start(f32[1032,128]{1,0:T(8,128)S(1)} %get-tuple-element.52), channel_id=1, source_target_pairs={{0,1},{1,0},{2,3},{3,2},{4,5},{5,4},{6,7},{7,6},{8,9},{9,8},{10,11... | collective-permute-start | bytes 1585160 | tf_op jit(solution)/shard_map/ppermute | solution.py:388
  7.5 11.7 %collective-permute-start.1 = (f32[520,128]{1,0:T(8,128)S(1)}, f32[520,128]{1,0:T(8,128)S(1)}, u32[]{:S(2)}, u32[]{:S(2)}) collective-permute-start(f32[520,128]{1,0:T(8,128)S(1)} %get-tuple-element.45), channel_id=1, source_target_pairs={{0,2},{1,5},{2,0},{3,7},{4,6},{5,1},{6,4},{7,3},{8,10},{9,13},{10,... | collective-permute-start | bytes 798728 | tf_op jit(solution)/shard_map/ppermute | solution.py:388
  13.3 4.8 %collective-permute-start.2 = (f32[1032,128]{1,0:T(8,128)S(1)}, f32[1032,128]{1,0:T(8,128)S(1)}, u32[]{:S(2)}, u32[]{:S(2)}) collective-permute-start(f32[1032,128]{1,0:T(8,128)S(1)} %get-tuple-element.49), channel_id=1, source_target_pairs={{0,1},{1,0},{2,3},{3,2},{4,5},{5,4},{6,7},{7,6},{8,9},{9,8},{10,11... | collective-permute-start | bytes 1585160 | tf_op jit(solution)/shard_map/ppermute | solution.py:388
  13.8 8.7 %collective-permute-start.8 = (f32[520,128]{1,0:T(8,128)S(1)}, f32[520,128]{1,0:T(8,128)S(1)}, u32[]{:S(2)}, u32[]{:S(2)}) collective-permute-start(f32[520,128]{1,0:T(8,128)S(1)} %get-tuple-element.62), channel_id=1, source_target_pairs={{0,4},{1,3},{2,6},{3,1},{4,0},{5,7},{6,2},{7,5},{8,12},{9,11},{10,... | collective-permute-start | bytes 798728 | tf_op jit(solution)/shard_map/ppermute | solution.py:388
  18.1 2.0 %collective-permute-start.5 = (f32[1032,128]{1,0:T(8,128)S(1)}, f32[1032,128]{1,0:T(8,128)S(1)}, u32[]{:S(2)}, u32[]{:S(2)}) collective-permute-start(f32[1032,128]{1,0:T(8,128)S(1)} %get-tuple-element.58), channel_id=1, source_target_pairs={{0,1},{1,0},{2,3},{3,2},{4,5},{5,4},{6,7},{7,6},{8,9},{9,8},{10,11... | collective-permute-start | bytes 1585160 | tf_op jit(solution)/shard_map/ppermute | solution.py:388
  18.5 8.3 %collective-permute-start.7 = (f32[520,128]{1,0:T(8,128)S(1)}, f32[520,128]{1,0:T(8,128)S(1)}, u32[]{:S(2)}, u32[]{:S(2)}) collective-permute-start(f32[520,128]{1,0:T(8,128)S(1)} %get-tuple-element.61), channel_id=1, source_target_pairs={{0,2},{1,5},{2,0},{3,7},{4,6},{5,1},{6,4},{7,3},{8,10},{9,13},{10,... | collective-permute-start | bytes 798728 | tf_op jit(solution)/shard_map/ppermute | solution.py:388
  19.3 15.5 %slice-start = ((s8[14680064]{0:T(1024)(128)(4,1)}), s8[4194304]{0:T(1024)(128)(4,1)S(1)}, s32[]{:S(2)}) async-start(s8[14680064]{0:T(1024)(128)(4,1)} %bitcast.2), calls=%async_computation | async-start | bytes 8388608
  19.3 15.5 %slice-start.1 = ((s8[14680064]{0:T(1024)(128)(4,1)}), s8[4194304]{0:T(1024)(128)(4,1)S(1)}, s32[]{:S(2)}) async-start(s8[14680064]{0:T(1024)(128)(4,1)} %bitcast.2), calls=%async_computation.1 | async-start | bytes 8388608
  20.4 8.4 %collective-permute-start.6 = (f32[520,128]{1,0:T(8,128)S(1)}, f32[520,128]{1,0:T(8,128)S(1)}, u32[]{:S(2)}, u32[]{:S(2)}) collective-permute-start(f32[520,128]{1,0:T(8,128)S(1)} %get-tuple-element.60), channel_id=1, source_target_pairs={{0,4},{1,3},{2,6},{3,1},{4,0},{5,7},{6,2},{7,5},{8,12},{9,11},{10,... | collective-permute-start | bytes 798728 | tf_op jit(solution)/shard_map/ppermute | solution.py:388
  21.6 8.7 %collective-permute-start.4 = (f32[264,128]{1,0:T(8,128)S(1)}, f32[264,128]{1,0:T(8,128)S(1)}, u32[]{:S(2)}, u32[]{:S(2)}) collective-permute-start(f32[264,128]{1,0:T(8,128)S(1)} %get-tuple-element.57), channel_id=1, source_target_pairs={{0,4},{1,3},{2,6},{3,1},{4,0},{5,7},{6,2},{7,5},{8,12},{9,11},{10,... | collective-permute-start | bytes 405512 | tf_op jit(solution)/shard_map/ppermute | solution.py:388
  22.8 7.7 %collective-permute-start.9 = (f32[264,128]{1,0:T(8,128)S(1)}, f32[264,128]{1,0:T(8,128)S(1)}, u32[]{:S(2)}, u32[]{:S(2)}) collective-permute-start(f32[264,128]{1,0:T(8,128)S(1)} %get-tuple-element.66), channel_id=1, source_target_pairs={{0,2},{1,5},{2,0},{3,7},{4,6},{5,1},{6,4},{7,3},{8,10},{9,13},{10,... | collective-permute-start | bytes 405512 | tf_op jit(solution)/shard_map/ppermute | solution.py:388
  27.1 5.2 %collective-permute-start.10 = (f32[264,128]{1,0:T(8,128)S(1)}, f32[264,128]{1,0:T(8,128)S(1)}, u32[]{:S(2)}, u32[]{:S(2)}) collective-permute-start(f32[264,128]{1,0:T(8,128)S(1)} %get-tuple-element.67), channel_id=1, source_target_pairs={{0,4},{1,3},{2,6},{3,1},{4,0},{5,7},{6,2},{7,5},{8,12},{9,11},{10,... | collective-permute-start | bytes 405512 | tf_op jit(solution)/shard_map/ppermute | solution.py:388
  28.8 6.0 %slice-start.2 = ((s8[14680064]{0:T(1024)(128)(4,1)}), s8[4194304]{0:T(1024)(128)(4,1)S(1)}, s32[]{:S(2)}) async-start(s8[14680064]{0:T(1024)(128)(4,1)} %bitcast.2), calls=%async_computation.2 | async-start | bytes 8388608
  28.8 6.0 %slice-start.3 = ((s8[14680064]{0:T(1024)(128)(4,1)}), s8[2097152]{0:T(1024)(128)(4,1)S(1)}, s32[]{:S(2)}) async-start(s8[14680064]{0:T(1024)(128)(4,1)} %bitcast.2), calls=%async_computation.3 | async-start | bytes 4194304
  29.1 5.1 %collective-permute-start.11 = (f32[264,128]{1,0:T(8,128)S(1)}, f32[264,128]{1,0:T(8,128)S(1)}, u32[]{:S(2)}, u32[]{:S(2)}) collective-permute-start(f32[264,128]{1,0:T(8,128)S(1)} %get-tuple-element.68), channel_id=1, source_target_pairs={{0,2},{1,5},{2,0},{3,7},{4,6},{5,1},{6,4},{7,3},{8,10},{9,13},{10,... | collective-permute-start | bytes 405512 | tf_op jit(solution)/shard_map/ppermute | solution.py:388
  30.3 4.0 %copy-start = (bf16[8,512,128]{2,1,0:T(8,128)(2,1)S(1)}, bf16[8,512,128]{2,1,0:T(8,128)(2,1)}, u32[]{:S(2)}) copy-start(bf16[8,512,128]{2,1,0:T(8,128)(2,1)} %refs_5_.1) | copy-start | bytes 3145732
  35.5 1.6 %collective-permute-start.12 = (f32[2,32,896]{2,1,0:T(8,128)S(1)}, f32[2,32,896]{2,1,0:T(8,128)S(1)}, u32[]{:S(2)}, u32[]{:S(2)}) collective-permute-start(f32[2,32,896]{2,1,0:T(8,128)S(1)} %shard_map.71.refs_0_), channel_id=1, source_target_pairs={{0,1},{1,0},{2,3},{3,2},{4,5},{5,4},{6,7},{7,6},{8,9},{9,8},{10,11... | collective-permute-start | bytes 688136 | tf_op jit(solution)/shard_map/ppermute | solution.py:388
  37.1 8.6 %collective-permute-start.14 = (f32[32,896]{1,0:T(8,128)S(1)}, f32[32,896]{1,0:T(8,128)S(1)}, u32[]{:S(2)}, u32[]{:S(2)}) collective-permute-start(f32[32,896]{1,0:T(8,128)S(1)} %get-tuple-element.69.refs_0_), channel_id=1, source_target_pairs={{0,6},{1,7},{2,4},{3,5},{4,2},{5,3},{6,0},{7,1},{8,14},{9,15},{10,... | collective-permute-start | bytes 344072 | tf_op jit(solution)/shard_map/ppermute | solution.py:388
  39.1 1.7 %collective-permute-start.13 = (f32[2,32,896]{2,1,0:T(8,128)S(1)}, f32[2,32,896]{2,1,0:T(8,128)S(1)}, u32[]{:S(2)}, u32[]{:S(2)}) collective-permute-start(f32[2,32,896]{2,1,0:T(8,128)S(1)} %shard_map.74.refs_0_), channel_id=1, source_target_pairs={{0,1},{1,0},{2,3},{3,2},{4,5},{5,4},{6,7},{7,6},{8,9},{9,8},{10,11... | collective-permute-start | bytes 688136 | tf_op jit(solution)/shard_map/ppermute | solution.py:388
  39.9 5.8 %collective-permute-start.15 = (f32[32,896]{1,0:T(8,128)S(1)}, f32[32,896]{1,0:T(8,128)S(1)}, u32[]{:S(2)}, u32[]{:S(2)}) collective-permute-start(f32[32,896]{1,0:T(8,128)S(1)} %get-tuple-element.71), channel_id=1, source_target_pairs={{0,2},{1,5},{2,0},{3,7},{4,6},{5,1},{6,4},{7,3},{8,10},{9,13},{10,... | collective-permute-start | bytes 344072 | tf_op jit(solution)/shard_map/ppermute | solution.py:388
  40.8 4.9 %collective-permute-start.16 = (f32[32,896]{1,0:T(8,128)S(1)}, f32[32,896]{1,0:T(8,128)S(1)}, u32[]{:S(2)}, u32[]{:S(2)}) collective-permute-start(f32[32,896]{1,0:T(8,128)S(1)} %get-tuple-element.72), channel_id=1, source_target_pairs={{0,4},{1,3},{2,6},{3,1},{4,0},{5,7},{6,2},{7,5},{8,12},{9,11},{10,... | collective-permute-start | bytes 344072 | tf_op jit(solution)/shard_map/ppermute | solution.py:388

commit v5 on v4

--- a/solution.py
+++ b/solution.py
@@ -11,7 +11,7 @@
 score_scale = 0.07216878364870323
 empty_mark = -1e30
 MIB = 1024 * 1024
-PARTS = (2, 2, 2, 2)
+PARTS = (3, 2, 2, 1)
 LAST = (50, 50, 0)
 DIRECT = ()
 ORDER = "A0:10 A1:10 C0:50 A2:10 C1:50 A3:10 C2:50 S0:50 C3:0 S1:0 S2:0 S3:50 M0:5 M1:5 M2:5"

time: 46.5 us -> 47.5 us (1.022)
  starting transfers between devices: 14.2 us -> 15 us
    ppermute x17, starting transfers between devices: 14.2 us -> 15 us  [swap(): return lax.ppermute(array, 'seq', pairs_of(n, step, turn))]
  transfers between devices with their start and end apart: 17 -> 17, of which waited for: 8 -> 8; matrix products, arithmetic and copies ran while one was open for 0% -> 0% of each run, Pallas kernels for 30% -> 28%
where the time goes in v5:
time: 47.5 us; the launch traced here: 47.3 us
  Pallas kernels  19.9 us (42%)
  starting transfers between devices  15 us (32%)
  waiting for transfers between devices  12.1 us (25%)
    ppermute x17, starting transfers between devices, swap(): return lax.ppermute(array, 'seq', pairs_of(n, step, turn))  15 us
    pallas_call x4, Pallas kernels, attention(): pl.pallas_call(functools.partial(attention_kernel, first, count, turn, le...  12.3 us
    ppermute x17, waiting for transfers between devices, swap(): return lax.ppermute(array, 'seq', pairs_of(n, step, turn))  12.1 us
    pallas_call x4, Pallas kernels, terms(): pl.pallas_call(functools.partial(terms_kernel, mate, places), in_specs=[S...  2.84 us
    pallas_call x8, Pallas kernels, combine(): pl.pallas_call(functools.partial(combine_kernel, places, pieces, sizes, t...  2.69 us
  transfers between devices with their start and end apart: 17, of which 8 were waited for; matrix products, arithmetic and copies ran while one was open for 0% of the time, Pallas kernels for 28%

profile of v5, /device:TPU:0, one launch (start us, length us, event | category | flops | bytes accessed | tf_op | source)
XLA Modules:
  0.0 47.3 jit_solution(14666129376538880295)
XLA Ops:
  0.0 4.9 %shard_map.55 = (f32[1544,128]{1,0:T(8,128)S(1)}, f32[1544,128]{1,0:T(8,128)S(1)}, bf16[2,4,64,576]{3,2,1,0:T(8,128)(2,1)S(1)}, bf16[2,576,1024]{2,1,0:T(8,128)(2,1)S(1)}) custom-call(s32[1]{0:T(128)} %bitcast.me_ref, s32[8]{0:T(128)} %lengths_hbm.7, bf16[8,4,64,576]{3,2,1,0:T(8,128)(2,1)} %q_hbm.7, bf16[8,576,1024]{2,1,0:T(8,128)(2,1)} %bitcast.4), custom_call_target="tpu_custom_call" | custom-call | flops 1000000000 | bytes 1 | tf_op jit(solution)/shard_map/pallas_call | solution.py:182
  4.9 0.5 %collective-permute-start = (f32[1544,128]{1,0:T(8,128)S(1)}, f32[1544,128]{1,0:T(8,128)S(1)}, u32[]{:S(2)}, u32[]{:S(2)}) collective-permute-start(f32[1544,128]{1,0:T(8,128)S(1)} %get-tuple-element.40), channel_id=1, source_target_pairs={{0,1},{1,0},{2,3},{3,2},{4,5},{5,4},{6,7},{7,6},{8,9},{9,8},{10,11... | collective-permute-start | bytes 2371592 | tf_op jit(solution)/shard_map/ppermute | solution.py:388
  5.5 2.8 %shard_map.56 = (f32[1032,128]{1,0:T(8,128)S(1)}, f32[1032,128]{1,0:T(8,128)S(1)}, bf16[2,4,64,576]{3,2,1,0:T(8,128)(2,1)S(1)}, bf16[2,576,1024]{2,1,0:T(8,128)(2,1)S(1)}) custom-call(s32[1]{0:T(128)} %bitcast.me_ref, s32[8]{0:T(128)} %lengths_hbm.7, bf16[8,4,64,576]{3,2,1,0:T(8,128)(2,1)} %q_hbm.7, bf16[8,576,1024]{2,1,0:T(8,128)(2,1)} %bitcast.5, ...), custom_call_target="tpu_custom_call" | custom-call | flops 1000000000 | bytes 1 | tf_op jit(solution)/shard_map/pallas_call | solution.py:182
  8.4 0.4 shard_map.57
  8.8 3.0 %collective-permute-start.1 = (f32[776,128]{1,0:T(8,128)S(1)}, f32[776,128]{1,0:T(8,128)S(1)}, u32[]{:S(2)}, u32[]{:S(2)}) collective-permute-start(f32[776,128]{1,0:T(8,128)S(1)} %get-tuple-element.45), channel_id=1, source_target_pairs={{0,2},{1,5},{2,0},{3,7},{4,6},{5,1},{6,4},{7,3},{8,10},{9,13},{10,... | collective-permute-start | bytes 1191944 | tf_op jit(solution)/shard_map/ppermute | solution.py:388
  11.8 2.7 %shard_map.58 = (f32[1032,128]{1,0:T(8,128)S(1)}, f32[1032,128]{1,0:T(8,128)S(1)}, bf16[1,4,64,576]{3,2,1,0:T(8,128)(2,1)S(1)}, bf16[1,576,1024]{2,1,0:T(8,128)(2,1)S(1)}) custom-call(s32[1]{0:T(128)} %bitcast.me_ref, s32[8]{0:T(128)} %lengths_hbm.7, bf16[8,4,64,576]{3,2,1,0:T(8,128)(2,1)} %q_hbm.7, bf16[8,576,1024]{2,1,0:T(8,128)(2,1)} %bitcast.6, ...), custom_call_target="tpu_custom_call" | custom-call | flops 1000000000 | bytes 1 | tf_op jit(solution)/shard_map/pallas_call | solution.py:182
  15.0 1.9 %shard_map.60 = (f32[520,128]{1,0:T(8,128)S(1)}, f32[520,128]{1,0:T(8,128)S(1)}) custom-call(s32[1]{0:T(128)} %bitcast.me_ref, s32[8]{0:T(128)} %lengths_hbm.7, bf16[8,4,64,576]{3,2,1,0:T(8,128)(2,1)} %q_hbm.7, bf16[8,576,1024]{2,1,0:T(8,128)(2,1)} %bitcast.7, bf16[1,4,64,576]{3,2,1,0:T(8,128)(2,1)S(1)} %get-tuple-element.50.refs_0_, ...), custom_call_target="tpu_custom_call" | custom-call | flops 1000000000 | bytes 1 | tf_op jit(solution)/shard_map/pallas_call | solution.py:182
  16.9 0.6 %collective-permute-start.5 = (f32[520,128]{1,0:T(8,128)S(1)}, f32[520,128]{1,0:T(8,128)S(1)}, u32[]{:S(2)}, u32[]{:S(2)}) collective-permute-start(f32[520,128]{1,0:T(8,128)S(1)} %get-tuple-element.58), channel_id=1, source_target_pairs={{0,1},{1,0},{2,3},{3,2},{4,5},{5,4},{6,7},{7,6},{8,9},{9,8},{10,11... | collective-permute-start | bytes 798728 | tf_op jit(solution)/shard_map/ppermute | solution.py:388
  17.4 1.5 %collective-permute-start.8 = (f32[520,128]{1,0:T(8,128)S(1)}, f32[520,128]{1,0:T(8,128)S(1)}, u32[]{:S(2)}, u32[]{:S(2)}) collective-permute-start(f32[520,128]{1,0:T(8,128)S(1)} %get-tuple-element.62), channel_id=1, source_target_pairs={{0,4},{1,3},{2,6},{3,1},{4,0},{5,7},{6,2},{7,5},{8,12},{9,11},{10,... | collective-permute-start | bytes 798728 | tf_op jit(solution)/shard_map/ppermute | solution.py:388
  19.3 0.6 %collective-permute-start.7 = (f32[520,128]{1,0:T(8,128)S(1)}, f32[520,128]{1,0:T(8,128)S(1)}, u32[]{:S(2)}, u32[]{:S(2)}) collective-permute-start(f32[520,128]{1,0:T(8,128)S(1)} %get-tuple-element.61), channel_id=1, source_target_pairs={{0,2},{1,5},{2,0},{3,7},{4,6},{5,1},{6,4},{7,3},{8,10},{9,13},{10,... | collective-permute-start | bytes 798728 | tf_op jit(solution)/shard_map/ppermute | solution.py:388
  20.6 0.9 %collective-permute-start.6 = (f32[264,128]{1,0:T(8,128)S(1)}, f32[264,128]{1,0:T(8,128)S(1)}, u32[]{:S(2)}, u32[]{:S(2)}) collective-permute-start(f32[264,128]{1,0:T(8,128)S(1)} %get-tuple-element.60), channel_id=1, source_target_pairs={{0,4},{1,3},{2,6},{3,1},{4,0},{5,7},{6,2},{7,5},{8,12},{9,11},{10,... | collective-permute-start | bytes 405512 | tf_op jit(solution)/shard_map/ppermute | solution.py:388
  21.5 1.2 %collective-permute-start.4 = (f32[392,128]{1,0:T(8,128)S(1)}, f32[392,128]{1,0:T(8,128)S(1)}, u32[]{:S(2)}, u32[]{:S(2)}) collective-permute-start(f32[392,128]{1,0:T(8,128)S(1)} %get-tuple-element.57), channel_id=1, source_target_pairs={{0,4},{1,3},{2,6},{3,1},{4,0},{5,7},{6,2},{7,5},{8,12},{9,11},{10,... | collective-permute-start | bytes 602120 | tf_op jit(solution)/shard_map/ppermute | solution.py:388
  22.7 3.6 %collective-permute-done.8.got_ref = f32[520,128]{1,0:T(8,128)S(1)} collective-permute-done((f32[520,128]{1,0:T(8,128)S(1)}, f32[520,128]{1,0:T(8,128)S(1)}, u32[]{:S(2)}, u32[]{:S(2)}) %collective-permute-start.8) | collective-permute-done | bytes 266272 | tf_op jit(solution)/shard_map/ppermute | solution.py:388
  26.6 0.9 %collective-permute-start.9 = (f32[264,128]{1,0:T(8,128)S(1)}, f32[264,128]{1,0:T(8,128)S(1)}, u32[]{:S(2)}, u32[]{:S(2)}) collective-permute-start(f32[264,128]{1,0:T(8,128)S(1)} %get-tuple-element.66), channel_id=1, source_target_pairs={{0,2},{1,5},{2,0},{3,7},{4,6},{5,1},{6,4},{7,3},{8,10},{9,13},{10,... | collective-permute-start | bytes 405512 | tf_op jit(solution)/shard_map/ppermute | solution.py:388
  27.5 1.2 %collective-permute-done.7.got_ref = f32[520,128]{1,0:T(8,128)S(1)} collective-permute-done((f32[520,128]{1,0:T(8,128)S(1)}, f32[520,128]{1,0:T(8,128)S(1)}, u32[]{:S(2)}, u32[]{:S(2)}) %collective-permute-start.7) | collective-permute-done | bytes 266272 | tf_op jit(solution)/shard_map/ppermute | solution.py:388
  29.0 0.6 %collective-permute-start.10 = (f32[264,128]{1,0:T(8,128)S(1)}, f32[264,128]{1,0:T(8,128)S(1)}, u32[]{:S(2)}, u32[]{:S(2)}) collective-permute-start(f32[264,128]{1,0:T(8,128)S(1)} %get-tuple-element.67), channel_id=1, source_target_pairs={{0,4},{1,3},{2,6},{3,1},{4,0},{5,7},{6,2},{7,5},{8,12},{9,11},{10,... | collective-permute-start | bytes 405512 | tf_op jit(solution)/shard_map/ppermute | solution.py:388
  29.9 1.3 %collective-permute-start.11 = (f32[136,128]{1,0:T(8,128)S(1)}, f32[136,128]{1,0:T(8,128)S(1)}, u32[]{:S(2)}, u32[]{:S(2)}) collective-permute-start(f32[136,128]{1,0:T(8,128)S(1)} %get-tuple-element.68), channel_id=1, source_target_pairs={{0,2},{1,5},{2,0},{3,7},{4,6},{5,1},{6,4},{7,3},{8,10},{9,13},{10,... | collective-permute-start | bytes 208904 | tf_op jit(solution)/shard_map/ppermute | solution.py:388
  31.2 1.2 %collective-permute-done.4.refs_1_ = f32[392,128]{1,0:T(8,128)S(1)} collective-permute-done((f32[392,128]{1,0:T(8,128)S(1)}, f32[392,128]{1,0:T(8,128)S(1)}, u32[]{:S(2)}, u32[]{:S(2)}) %collective-permute-start.4) | collective-permute-done | bytes 200736 | tf_op jit(solution)/shard_map/ppermute | solution.py:388
  32.7 0.4 collective-permute-done.9.refs_1_
  33.3 0.8 %collective-permute-done.10.refs_1_ = f32[264,128]{1,0:T(8,128)S(1)} collective-permute-done((f32[264,128]{1,0:T(8,128)S(1)}, f32[264,128]{1,0:T(8,128)S(1)}, u32[]{:S(2)}, u32[]{:S(2)}) %collective-permute-start.10) | collective-permute-done | bytes 135200 | tf_op jit(solution)/shard_map/ppermute | solution.py:388
  34.4 0.5 %shard_map.70.heads_ref = bf16[32,1024]{1,0:T(8,128)(2,1)S(1)} custom-call(s32[1]{0:T(128)} %bitcast.me_ref, f32[4,96,128]{2,1,0:T(8,128)S(1)} %shard_map.67.refs_2_.refs_0_, f32[4,64,128]{2,1,0:T(8,128)S(1)} %shard_map.68.refs_2_.refs_1_, f32[4,64,128]{2,1,0:T(8,128)S(1)} %shard_map.69.refs_2_, f32[136,128]{1,0:T(8,128)S(1)} %get-tuple-element.65.refs_2_.refs_3_, ...), custom_call_target="tpu_custom_call" | custom-call | flops 1 | bytes 1 | tf_op jit(solution)/shard_map/pallas_call | solution.py:310
  35.0 0.7 %shard_map.71.refs_0_ = f32[2,32,896]{2,1,0:T(8,128)S(1)} custom-call(s32[1]{0:T(128)} %bitcast.me_ref, bf16[32,1024]{1,0:T(8,128)(2,1)S(1)} %shard_map.70.heads_ref, bf16[1024,7168]{1,0:T(8,128)(2,1)S(1)} %bitcast.3), custom_call_target="tpu_custom_call" | custom-call | flops 5000000000 | bytes 1 | tf_op jit(solution)/shard_map/pallas_call | solution.py:331
  35.8 0.7 %shard_map.72.own_ref = f32[2,32,896]{2,1,0:T(8,128)S(1)} custom-call(s32[1]{0:T(128)} %bitcast.me_ref, bf16[32,1024]{1,0:T(8,128)(2,1)S(1)} %shard_map.70.heads_ref, bf16[1024,7168]{1,0:T(8,128)(2,1)S(1)} %bitcast.3, f32[2,32,896]{2,1,0:T(8,128)S(1)} %shard_map.71.refs_0_), custom_call_target="tpu_custom_call" | custom-call | flops 5000000000 | bytes 1 | tf_op jit(solution)/shard_map/pallas_call | solution.py:331
  36.5 0.8 %collective-permute-done.12.got_ref = f32[2,32,896]{2,1,0:T(8,128)S(1)} collective-permute-done((f32[2,32,896]{2,1,0:T(8,128)S(1)}, f32[2,32,896]{2,1,0:T(8,128)S(1)}, u32[]{:S(2)}, u32[]{:S(2)}) %collective-permute-start.12) | collective-permute-done | bytes 229408 | tf_op jit(solution)/shard_map/ppermute | solution.py:388
  37.3 1.4 %collective-permute-start.14 = (f32[32,896]{1,0:T(8,128)S(1)}, f32[32,896]{1,0:T(8,128)S(1)}, u32[]{:S(2)}, u32[]{:S(2)}) collective-permute-start(f32[32,896]{1,0:T(8,128)S(1)} %get-tuple-element.69.refs_0_), channel_id=1, source_target_pairs={{0,6},{1,7},{2,4},{3,5},{4,2},{5,3},{6,0},{7,1},{8,14},{9,15},{10,... | collective-permute-start | bytes 344072 | tf_op jit(solution)/shard_map/ppermute | solution.py:388
  38.7 0.7 %shard_map.74.refs_0_ = f32[2,32,896]{2,1,0:T(8,128)S(1)} custom-call(s32[1]{0:T(128)} %bitcast.me_ref, bf16[32,1024]{1,0:T(8,128)(2,1)S(1)} %shard_map.70.heads_ref, bf16[1024,7168]{1,0:T(8,128)(2,1)S(1)} %bitcast.3, f32[32,896]{1,0:T(8,128)S(1)} %get-tuple-element.69.refs_0_), custom_call_target="tpu_custom_call" | custom-call | flops 5000000000 | bytes 1 | tf_op jit(solution)/shard_map/pallas_call | solution.py:331
  39.5 0.7 %shard_map.75.own_ref = f32[2,32,896]{2,1,0:T(8,128)S(1)} custom-call(s32[1]{0:T(128)} %bitcast.me_ref, bf16[32,1024]{1,0:T(8,128)(2,1)S(1)} %shard_map.70.heads_ref, bf16[1024,7168]{1,0:T(8,128)(2,1)S(1)} %bitcast.3, f32[2,32,896]{2,1,0:T(8,128)S(1)} %shard_map.74.refs_0_), custom_call_target="tpu_custom_call" | custom-call | flops 5000000000 | bytes 1 | tf_op jit(solution)/shard_map/pallas_call | solution.py:331
  40.2 1.6 %collective-permute-start.15 = (f32[32,896]{1,0:T(8,128)S(1)}, f32[32,896]{1,0:T(8,128)S(1)}, u32[]{:S(2)}, u32[]{:S(2)}) collective-permute-start(f32[32,896]{1,0:T(8,128)S(1)} %get-tuple-element.71), channel_id=1, source_target_pairs={{0,2},{1,5},{2,0},{3,7},{4,6},{5,1},{6,4},{7,3},{8,10},{9,13},{10,... | collective-permute-start | bytes 344072 | tf_op jit(solution)/shard_map/ppermute | solution.py:388
  41.8 0.7 %collective-permute-start.16 = (f32[32,896]{1,0:T(8,128)S(1)}, f32[32,896]{1,0:T(8,128)S(1)}, u32[]{:S(2)}, u32[]{:S(2)}) collective-permute-start(f32[32,896]{1,0:T(8,128)S(1)} %get-tuple-element.72), channel_id=1, source_target_pairs={{0,4},{1,3},{2,6},{3,1},{4,0},{5,7},{6,2},{7,5},{8,12},{9,11},{10,... | collective-permute-start | bytes 344072 | tf_op jit(solution)/shard_map/ppermute | solution.py:388
  42.5 3.3 %collective-permute-done.15.refs_2_ = f32[32,896]{1,0:T(8,128)S(1)} collective-permute-done((f32[32,896]{1,0:T(8,128)S(1)}, f32[32,896]{1,0:T(8,128)S(1)}, u32[]{:S(2)}, u32[]{:S(2)}) %collective-permute-start.15) | collective-permute-done | bytes 114720 | tf_op jit(solution)/shard_map/ppermute | solution.py:388
  45.9 0.8 %collective-permute-done.16.refs_3_ = f32[32,896]{1,0:T(8,128)S(1)} collective-permute-done((f32[32,896]{1,0:T(8,128)S(1)}, f32[32,896]{1,0:T(8,128)S(1)}, u32[]{:S(2)}, u32[]{:S(2)}) %collective-permute-start.16) | collective-permute-done | bytes 114720 | tf_op jit(solution)/shard_map/ppermute | solution.py:388
  46.7 0.7 %shard_map.77 = bf16[8,4,896]{2,1,0:T(4,128)(2,1)} custom-call(f32[32,896]{1,0:T(8,128)S(1)} %get-tuple-element.70.refs_0_, f32[32,896]{1,0:T(8,128)S(1)} %collective-permute-done.14.refs_1_, f32[32,896]{1,0:T(8,128)S(1)} %collective-permute-done.15.refs_2_, f32[32,896]{1,0:T(8,128)S(1)} %collective-permute-done.16.refs_3_), custom_call_target="tpu_custom_call" | custom-call | flops 1 | bytes 1 | tf_op jit(solution)/shard_map/pallas_call | solution.py:369
  (36 shorter events, 3.5 us)
Async XLA Ops:
  4.9 3.4 %collective-permute-start = (f32[1544,128]{1,0:T(8,128)S(1)}, f32[1544,128]{1,0:T(8,128)S(1)}, u32[]{:S(2)}, u32[]{:S(2)}) collective-permute-start(f32[1544,128]{1,0:T(8,128)S(1)} %get-tuple-element.40), channel_id=1, source_target_pairs={{0,1},{1,0},{2,3},{3,2},{4,5},{5,4},{6,7},{7,6},{8,9},{9,8},{10,11... | collective-permute-start | bytes 2371592 | tf_op jit(solution)/shard_map/ppermute | solution.py:388
  8.2 6.4 %collective-permute-start.3 = (f32[1032,128]{1,0:T(8,128)S(1)}, f32[1032,128]{1,0:T(8,128)S(1)}, u32[]{:S(2)}, u32[]{:S(2)}) collective-permute-start(f32[1032,128]{1,0:T(8,128)S(1)} %get-tuple-element.52), channel_id=1, source_target_pairs={{0,1},{1,0},{2,3},{3,2},{4,5},{5,4},{6,7},{7,6},{8,9},{9,8},{10,11... | collective-permute-start | bytes 1585160 | tf_op jit(solution)/shard_map/ppermute | solution.py:388
  8.8 11.1 %collective-permute-start.1 = (f32[776,128]{1,0:T(8,128)S(1)}, f32[776,128]{1,0:T(8,128)S(1)}, u32[]{:S(2)}, u32[]{:S(2)}) collective-permute-start(f32[776,128]{1,0:T(8,128)S(1)} %get-tuple-element.45), channel_id=1, source_target_pairs={{0,2},{1,5},{2,0},{3,7},{4,6},{5,1},{6,4},{7,3},{8,10},{9,13},{10,... | collective-permute-start | bytes 1191944 | tf_op jit(solution)/shard_map/ppermute | solution.py:388
  14.5 4.4 %collective-permute-start.2 = (f32[1032,128]{1,0:T(8,128)S(1)}, f32[1032,128]{1,0:T(8,128)S(1)}, u32[]{:S(2)}, u32[]{:S(2)}) collective-permute-start(f32[1032,128]{1,0:T(8,128)S(1)} %get-tuple-element.49), channel_id=1, source_target_pairs={{0,1},{1,0},{2,3},{3,2},{4,5},{5,4},{6,7},{7,6},{8,9},{9,8},{10,11... | collective-permute-start | bytes 1585160 | tf_op jit(solution)/shard_map/ppermute | solution.py:388
  16.9 3.4 %collective-permute-start.5 = (f32[520,128]{1,0:T(8,128)S(1)}, f32[520,128]{1,0:T(8,128)S(1)}, u32[]{:S(2)}, u32[]{:S(2)}) collective-permute-start(f32[520,128]{1,0:T(8,128)S(1)} %get-tuple-element.58), channel_id=1, source_target_pairs={{0,1},{1,0},{2,3},{3,2},{4,5},{5,4},{6,7},{7,6},{8,9},{9,8},{10,11... | collective-permute-start | bytes 798728 | tf_op jit(solution)/shard_map/ppermute | solution.py:388
  17.4 8.9 %collective-permute-start.8 = (f32[520,128]{1,0:T(8,128)S(1)}, f32[520,128]{1,0:T(8,128)S(1)}, u32[]{:S(2)}, u32[]{:S(2)}) collective-permute-start(f32[520,128]{1,0:T(8,128)S(1)} %get-tuple-element.62), channel_id=1, source_target_pairs={{0,4},{1,3},{2,6},{3,1},{4,0},{5,7},{6,2},{7,5},{8,12},{9,11},{10,... | collective-permute-start | bytes 798728 | tf_op jit(solution)/shard_map/ppermute | solution.py:388
  19.3 9.4 %collective-permute-start.7 = (f32[520,128]{1,0:T(8,128)S(1)}, f32[520,128]{1,0:T(8,128)S(1)}, u32[]{:S(2)}, u32[]{:S(2)}) collective-permute-start(f32[520,128]{1,0:T(8,128)S(1)} %get-tuple-element.61), channel_id=1, source_target_pairs={{0,2},{1,5},{2,0},{3,7},{4,6},{5,1},{6,4},{7,3},{8,10},{9,13},{10,... | collective-permute-start | bytes 798728 | tf_op jit(solution)/shard_map/ppermute | solution.py:388
  19.9 15.0 %slice-start = ((s8[14680064]{0:T(1024)(128)(4,1)}), s8[4194304]{0:T(1024)(128)(4,1)S(1)}, s32[]{:S(2)}) async-start(s8[14680064]{0:T(1024)(128)(4,1)} %bitcast.2), calls=%async_computation | async-start | bytes 8388608
  19.9 15.0 %slice-start.1 = ((s8[14680064]{0:T(1024)(128)(4,1)}), s8[4194304]{0:T(1024)(128)(4,1)S(1)}, s32[]{:S(2)}) async-start(s8[14680064]{0:T(1024)(128)(4,1)} %bitcast.2), calls=%async_computation.1 | async-start | bytes 8388608
  20.6 9.0 %collective-permute-start.6 = (f32[264,128]{1,0:T(8,128)S(1)}, f32[264,128]{1,0:T(8,128)S(1)}, u32[]{:S(2)}, u32[]{:S(2)}) collective-permute-start(f32[264,128]{1,0:T(8,128)S(1)} %get-tuple-element.60), channel_id=1, source_target_pairs={{0,4},{1,3},{2,6},{3,1},{4,0},{5,7},{6,2},{7,5},{8,12},{9,11},{10,... | collective-permute-start | bytes 405512 | tf_op jit(solution)/shard_map/ppermute | solution.py:388
  21.5 10.9 %collective-permute-start.4 = (f32[392,128]{1,0:T(8,128)S(1)}, f32[392,128]{1,0:T(8,128)S(1)}, u32[]{:S(2)}, u32[]{:S(2)}) collective-permute-start(f32[392,128]{1,0:T(8,128)S(1)} %get-tuple-element.57), channel_id=1, source_target_pairs={{0,4},{1,3},{2,6},{3,1},{4,0},{5,7},{6,2},{7,5},{8,12},{9,11},{10,... | collective-permute-start | bytes 602120 | tf_op jit(solution)/shard_map/ppermute | solution.py:388
  26.6 6.4 %collective-permute-start.9 = (f32[264,128]{1,0:T(8,128)S(1)}, f32[264,128]{1,0:T(8,128)S(1)}, u32[]{:S(2)}, u32[]{:S(2)}) collective-permute-start(f32[264,128]{1,0:T(8,128)S(1)} %get-tuple-element.66), channel_id=1, source_target_pairs={{0,2},{1,5},{2,0},{3,7},{4,6},{5,1},{6,4},{7,3},{8,10},{9,13},{10,... | collective-permute-start | bytes 405512 | tf_op jit(solution)/shard_map/ppermute | solution.py:388
  29.0 5.1 %collective-permute-start.10 = (f32[264,128]{1,0:T(8,128)S(1)}, f32[264,128]{1,0:T(8,128)S(1)}, u32[]{:S(2)}, u32[]{:S(2)}) collective-permute-start(f32[264,128]{1,0:T(8,128)S(1)} %get-tuple-element.67), channel_id=1, source_target_pairs={{0,4},{1,3},{2,6},{3,1},{4,0},{5,7},{6,2},{7,5},{8,12},{9,11},{10,... | collective-permute-start | bytes 405512 | tf_op jit(solution)/shard_map/ppermute | solution.py:388
  29.6 5.3 %slice-start.2 = ((s8[14680064]{0:T(1024)(128)(4,1)}), s8[4194304]{0:T(1024)(128)(4,1)S(1)}, s32[]{:S(2)}) async-start(s8[14680064]{0:T(1024)(128)(4,1)} %bitcast.2), calls=%async_computation.2 | async-start | bytes 8388608
  29.6 5.4 %slice-start.3 = ((s8[14680064]{0:T(1024)(128)(4,1)}), s8[2097152]{0:T(1024)(128)(4,1)S(1)}, s32[]{:S(2)}) async-start(s8[14680064]{0:T(1024)(128)(4,1)} %bitcast.2), calls=%async_computation.3 | async-start | bytes 4194304
  29.9 4.5 %collective-permute-start.11 = (f32[136,128]{1,0:T(8,128)S(1)}, f32[136,128]{1,0:T(8,128)S(1)}, u32[]{:S(2)}, u32[]{:S(2)}) collective-permute-start(f32[136,128]{1,0:T(8,128)S(1)} %get-tuple-element.68), channel_id=1, source_target_pairs={{0,2},{1,5},{2,0},{3,7},{4,6},{5,1},{6,4},{7,3},{8,10},{9,13},{10,... | collective-permute-start | bytes 208904 | tf_op jit(solution)/shard_map/ppermute | solution.py:388
  32.4 2.0 %copy-start = (bf16[8,512,128]{2,1,0:T(8,128)(2,1)S(1)}, bf16[8,512,128]{2,1,0:T(8,128)(2,1)}, u32[]{:S(2)}) copy-start(bf16[8,512,128]{2,1,0:T(8,128)(2,1)} %refs_5_.1) | copy-start | bytes 3145732
  35.7 1.6 %collective-permute-start.12 = (f32[2,32,896]{2,1,0:T(8,128)S(1)}, f32[2,32,896]{2,1,0:T(8,128)S(1)}, u32[]{:S(2)}, u32[]{:S(2)}) collective-permute-start(f32[2,32,896]{2,1,0:T(8,128)S(1)} %shard_map.71.refs_0_), channel_id=1, source_target_pairs={{0,1},{1,0},{2,3},{3,2},{4,5},{5,4},{6,7},{7,6},{8,9},{9,8},{10,11... | collective-permute-start | bytes 688136 | tf_op jit(solution)/shard_map/ppermute | solution.py:388
  37.3 8.6 %collective-permute-start.14 = (f32[32,896]{1,0:T(8,128)S(1)}, f32[32,896]{1,0:T(8,128)S(1)}, u32[]{:S(2)}, u32[]{:S(2)}) collective-permute-start(f32[32,896]{1,0:T(8,128)S(1)} %get-tuple-element.69.refs_0_), channel_id=1, source_target_pairs={{0,6},{1,7},{2,4},{3,5},{4,2},{5,3},{6,0},{7,1},{8,14},{9,15},{10,... | collective-permute-start | bytes 344072 | tf_op jit(solution)/shard_map/ppermute | solution.py:388
  39.4 2.4 %collective-permute-start.13 = (f32[2,32,896]{2,1,0:T(8,128)S(1)}, f32[2,32,896]{2,1,0:T(8,128)S(1)}, u32[]{:S(2)}, u32[]{:S(2)}) collective-permute-start(f32[2,32,896]{2,1,0:T(8,128)S(1)} %shard_map.74.refs_0_), channel_id=1, source_target_pairs={{0,1},{1,0},{2,3},{3,2},{4,5},{5,4},{6,7},{7,6},{8,9},{9,8},{10,11... | collective-permute-start | bytes 688136 | tf_op jit(solution)/shard_map/ppermute | solution.py:388
  40.2 5.7 %collective-permute-start.15 = (f32[32,896]{1,0:T(8,128)S(1)}, f32[32,896]{1,0:T(8,128)S(1)}, u32[]{:S(2)}, u32[]{:S(2)}) collective-permute-start(f32[32,896]{1,0:T(8,128)S(1)} %get-tuple-element.71), channel_id=1, source_target_pairs={{0,2},{1,5},{2,0},{3,7},{4,6},{5,1},{6,4},{7,3},{8,10},{9,13},{10,... | collective-permute-start | bytes 344072 | tf_op jit(solution)/shard_map/ppermute | solution.py:388
  41.8 4.9 %collective-permute-start.16 = (f32[32,896]{1,0:T(8,128)S(1)}, f32[32,896]{1,0:T(8,128)S(1)}, u32[]{:S(2)}, u32[]{:S(2)}) collective-permute-start(f32[32,896]{1,0:T(8,128)S(1)} %get-tuple-element.72), channel_id=1, source_target_pairs={{0,4},{1,3},{2,6},{3,1},{4,0},{5,7},{6,2},{7,5},{8,12},{9,11},{10,... | collective-permute-start | bytes 344072 | tf_op jit(solution)/shard_map/ppermute | solution.py:388

commit v6 on v4

--- a/solution.py
+++ b/solution.py
@@ -14,7 +14,7 @@
 PARTS = (2, 2, 2, 2)
 LAST = (50, 50, 0)
 DIRECT = ()
-ORDER = "A0:10 A1:10 C0:50 A2:10 C1:50 A3:10 C2:50 S0:50 C3:0 S1:0 S2:0 S3:50 M0:5 M1:5 M2:5"
+ORDER = "A0:10 A1:10 C0:50 A2:10 C1:50 A3:10 C2:50 S0:50 C3:50 S1:20 S2:20 S3:50 M0:5 M1:5 M2:5"
 BLOCK = 32
 PIECES = 4
 TILE = 256

time: 46.5 us -> 49 us (1.054)
  waiting for transfers between devices: 12.3 us -> 13.6 us
  starting transfers between devices: 14.2 us -> 15.4 us
    ppermute x17, waiting for transfers between devices: 12.3 us -> 13.6 us  [swap(): return lax.ppermute(array, 'seq', pairs_of(n, step, turn))]
    ppermute x17, starting transfers between devices: 14.2 us -> 15.4 us  [swap(): return lax.ppermute(array, 'seq', pairs_of(n, step, turn))]
  transfers between devices with their start and end apart: 17 -> 17, of which waited for: 8 -> 6; matrix products, arithmetic and copies ran while one was open for 0% -> 0% of each run, Pallas kernels for 30% -> 28%
where the time goes in v6:
time: 49 us; the launch traced here: 48.8 us
  Pallas kernels  19.6 us (40%)
  starting transfers between devices  15.4 us (31%)
  waiting for transfers between devices  13.6 us (28%)
    ppermute x17, starting transfers between devices, swap(): return lax.ppermute(array, 'seq', pairs_of(n, step, turn))  15.4 us
    ppermute x17, waiting for transfers between devices, swap(): return lax.ppermute(array, 'seq', pairs_of(n, step, turn))  13.6 us
    pallas_call x4, Pallas kernels, attention(): pl.pallas_call(functools.partial(attention_kernel, first, count, turn, le...  12 us
    pallas_call x4, Pallas kernels, terms(): pl.pallas_call(functools.partial(terms_kernel, mate, places), in_specs=[S...  2.84 us
    pallas_call x8, Pallas kernels, combine(): pl.pallas_call(functools.partial(combine_kernel, places, pieces, sizes, t...  2.72 us
  transfers between devices with their start and end apart: 17, of which 6 were waited for; matrix products, arithmetic and copies ran while one was open for 0% of the time, Pallas kernels for 28%

profile of v6, /device:TPU:0, one launch (start us, length us, event | category | flops | bytes accessed | tf_op | source)
XLA Modules:
  0.0 48.8 jit_solution(4032014071207609661)
XLA Ops:
  0.0 3.7 %shard_map.55 = (f32[1032,128]{1,0:T(8,128)S(1)}, f32[1032,128]{1,0:T(8,128)S(1)}, bf16[2,4,64,576]{3,2,1,0:T(8,128)(2,1)S(1)}, bf16[2,576,1024]{2,1,0:T(8,128)(2,1)S(1)}) custom-call(s32[1]{0:T(128)} %bitcast.me_ref, s32[8]{0:T(128)} %lengths_hbm.7, bf16[8,4,64,576]{3,2,1,0:T(8,128)(2,1)} %q_hbm.7, bf16[8,576,1024]{2,1,0:T(8,128)(2,1)} %bitcast.4), custom_call_target="tpu_custom_call" | custom-call | flops 1000000000 | bytes 1 | tf_op jit(solution)/shard_map/pallas_call | solution.py:182
  3.8 0.5 %collective-permute-start = (f32[1032,128]{1,0:T(8,128)S(1)}, f32[1032,128]{1,0:T(8,128)S(1)}, u32[]{:S(2)}, u32[]{:S(2)}) collective-permute-start(f32[1032,128]{1,0:T(8,128)S(1)} %get-tuple-element.40), channel_id=1, source_target_pairs={{0,1},{1,0},{2,3},{3,2},{4,5},{5,4},{6,7},{7,6},{8,9},{9,8},{10,11... | collective-permute-start | bytes 1585160 | tf_op jit(solution)/shard_map/ppermute | solution.py:388
  4.3 2.8 %shard_map.56 = (f32[1032,128]{1,0:T(8,128)S(1)}, f32[1032,128]{1,0:T(8,128)S(1)}, bf16[2,4,64,576]{3,2,1,0:T(8,128)(2,1)S(1)}, bf16[2,576,1024]{2,1,0:T(8,128)(2,1)S(1)}) custom-call(s32[1]{0:T(128)} %bitcast.me_ref, s32[8]{0:T(128)} %lengths_hbm.7, bf16[8,4,64,576]{3,2,1,0:T(8,128)(2,1)} %q_hbm.7, bf16[8,576,1024]{2,1,0:T(8,128)(2,1)} %bitcast.5, ...), custom_call_target="tpu_custom_call" | custom-call | flops 1000000000 | bytes 1 | tf_op jit(solution)/shard_map/pallas_call | solution.py:182
  7.2 0.4 shard_map.57
  7.5 3.0 %collective-permute-start.1 = (f32[520,128]{1,0:T(8,128)S(1)}, f32[520,128]{1,0:T(8,128)S(1)}, u32[]{:S(2)}, u32[]{:S(2)}) collective-permute-start(f32[520,128]{1,0:T(8,128)S(1)} %get-tuple-element.45), channel_id=1, source_target_pairs={{0,2},{1,5},{2,0},{3,7},{4,6},{5,1},{6,4},{7,3},{8,10},{9,13},{10,... | collective-permute-start | bytes 798728 | tf_op jit(solution)/shard_map/ppermute | solution.py:388
  10.5 2.8 %shard_map.58 = (f32[1032,128]{1,0:T(8,128)S(1)}, f32[1032,128]{1,0:T(8,128)S(1)}, bf16[2,4,64,576]{3,2,1,0:T(8,128)(2,1)S(1)}, bf16[2,576,1024]{2,1,0:T(8,128)(2,1)S(1)}) custom-call(s32[1]{0:T(128)} %bitcast.me_ref, s32[8]{0:T(128)} %lengths_hbm.7, bf16[8,4,64,576]{3,2,1,0:T(8,128)(2,1)} %q_hbm.7, bf16[8,576,1024]{2,1,0:T(8,128)(2,1)} %bitcast.6, ...), custom_call_target="tpu_custom_call" | custom-call | flops 1000000000 | bytes 1 | tf_op jit(solution)/shard_map/pallas_call | solution.py:182
  13.4 0.4 shard_map.59
  13.8 1.6 %collective-permute-start.8 = (f32[520,128]{1,0:T(8,128)S(1)}, f32[520,128]{1,0:T(8,128)S(1)}, u32[]{:S(2)}, u32[]{:S(2)}) collective-permute-start(f32[520,128]{1,0:T(8,128)S(1)} %get-tuple-element.62), channel_id=1, source_target_pairs={{0,4},{1,3},{2,6},{3,1},{4,0},{5,7},{6,2},{7,5},{8,12},{9,11},{10,... | collective-permute-start | bytes 798728 | tf_op jit(solution)/shard_map/ppermute | solution.py:388
  15.4 2.7 %shard_map.60 = (f32[1032,128]{1,0:T(8,128)S(1)}, f32[1032,128]{1,0:T(8,128)S(1)}) custom-call(s32[1]{0:T(128)} %bitcast.me_ref, s32[8]{0:T(128)} %lengths_hbm.7, bf16[8,4,64,576]{3,2,1,0:T(8,128)(2,1)} %q_hbm.7, bf16[8,576,1024]{2,1,0:T(8,128)(2,1)} %bitcast.7, bf16[2,4,64,576]{3,2,1,0:T(8,128)(2,1)S(1)} %get-tuple-element.50.refs_0_, ...), custom_call_target="tpu_custom_call" | custom-call | flops 1000000000 | bytes 1 | tf_op jit(solution)/shard_map/pallas_call | solution.py:182
  18.1 0.4 shard_map.61
  18.9 0.8 %collective-permute-start.4 = (f32[264,128]{1,0:T(8,128)S(1)}, f32[264,128]{1,0:T(8,128)S(1)}, u32[]{:S(2)}, u32[]{:S(2)}) collective-permute-start(f32[264,128]{1,0:T(8,128)S(1)} %get-tuple-element.57), channel_id=1, source_target_pairs={{0,4},{1,3},{2,6},{3,1},{4,0},{5,7},{6,2},{7,5},{8,12},{9,11},{10,... | collective-permute-start | bytes 405512 | tf_op jit(solution)/shard_map/ppermute | solution.py:388
  19.6 1.5 %collective-permute-start.7 = (f32[520,128]{1,0:T(8,128)S(1)}, f32[520,128]{1,0:T(8,128)S(1)}, u32[]{:S(2)}, u32[]{:S(2)}) collective-permute-start(f32[520,128]{1,0:T(8,128)S(1)} %get-tuple-element.61), channel_id=1, source_target_pairs={{0,2},{1,5},{2,0},{3,7},{4,6},{5,1},{6,4},{7,3},{8,10},{9,13},{10,... | collective-permute-start | bytes 798728 | tf_op jit(solution)/shard_map/ppermute | solution.py:388
  21.1 0.4 shard_map.63
  21.5 0.6 %collective-permute-start.6 = (f32[520,128]{1,0:T(8,128)S(1)}, f32[520,128]{1,0:T(8,128)S(1)}, u32[]{:S(2)}, u32[]{:S(2)}) collective-permute-start(f32[520,128]{1,0:T(8,128)S(1)} %get-tuple-element.60), channel_id=1, source_target_pairs={{0,4},{1,3},{2,6},{3,1},{4,0},{5,7},{6,2},{7,5},{8,12},{9,11},{10,... | collective-permute-start | bytes 798728 | tf_op jit(solution)/shard_map/ppermute | solution.py:388
  22.4 1.4 %collective-permute-start.9 = (f32[264,128]{1,0:T(8,128)S(1)}, f32[264,128]{1,0:T(8,128)S(1)}, u32[]{:S(2)}, u32[]{:S(2)}) collective-permute-start(f32[264,128]{1,0:T(8,128)S(1)} %get-tuple-element.66), channel_id=1, source_target_pairs={{0,2},{1,5},{2,0},{3,7},{4,6},{5,1},{6,4},{7,3},{8,10},{9,13},{10,... | collective-permute-start | bytes 405512 | tf_op jit(solution)/shard_map/ppermute | solution.py:388
  23.8 5.1 %collective-permute-done.7.got_ref = f32[520,128]{1,0:T(8,128)S(1)} collective-permute-done((f32[520,128]{1,0:T(8,128)S(1)}, f32[520,128]{1,0:T(8,128)S(1)}, u32[]{:S(2)}, u32[]{:S(2)}) %collective-permute-start.7) | collective-permute-done | bytes 266272 | tf_op jit(solution)/shard_map/ppermute | solution.py:388
  29.2 1.3 %collective-permute-start.10 = (f32[264,128]{1,0:T(8,128)S(1)}, f32[264,128]{1,0:T(8,128)S(1)}, u32[]{:S(2)}, u32[]{:S(2)}) collective-permute-start(f32[264,128]{1,0:T(8,128)S(1)} %get-tuple-element.67), channel_id=1, source_target_pairs={{0,4},{1,3},{2,6},{3,1},{4,0},{5,7},{6,2},{7,5},{8,12},{9,11},{10,... | collective-permute-start | bytes 405512 | tf_op jit(solution)/shard_map/ppermute | solution.py:388
  30.5 0.3 collective-permute-done.6.got_ref
  31.2 0.6 %collective-permute-start.11 = (f32[264,128]{1,0:T(8,128)S(1)}, f32[264,128]{1,0:T(8,128)S(1)}, u32[]{:S(2)}, u32[]{:S(2)}) collective-permute-start(f32[264,128]{1,0:T(8,128)S(1)} %get-tuple-element.68), channel_id=1, source_target_pairs={{0,2},{1,5},{2,0},{3,7},{4,6},{5,1},{6,4},{7,3},{8,10},{9,13},{10,... | collective-permute-start | bytes 405512 | tf_op jit(solution)/shard_map/ppermute | solution.py:388
  32.4 3.0 %collective-permute-done.10.refs_1_ = f32[264,128]{1,0:T(8,128)S(1)} collective-permute-done((f32[264,128]{1,0:T(8,128)S(1)}, f32[264,128]{1,0:T(8,128)S(1)}, u32[]{:S(2)}, u32[]{:S(2)}) %collective-permute-start.10) | collective-permute-done | bytes 135200 | tf_op jit(solution)/shard_map/ppermute | solution.py:388
  35.6 0.6 %collective-permute-done.11.refs_4_ = f32[264,128]{1,0:T(8,128)S(1)} collective-permute-done((f32[264,128]{1,0:T(8,128)S(1)}, f32[264,128]{1,0:T(8,128)S(1)}, u32[]{:S(2)}, u32[]{:S(2)}) %collective-permute-start.11) | collective-permute-done | bytes 135200 | tf_op jit(solution)/shard_map/ppermute | solution.py:388
  36.2 0.5 %shard_map.70.heads_ref = bf16[32,1024]{1,0:T(8,128)(2,1)S(1)} custom-call(s32[1]{0:T(128)} %bitcast.me_ref, f32[4,64,128]{2,1,0:T(8,128)S(1)} %shard_map.67.refs_2_.refs_0_, f32[4,64,128]{2,1,0:T(8,128)S(1)} %shard_map.68.refs_2_.refs_1_, f32[4,64,128]{2,1,0:T(8,128)S(1)} %shard_map.69.refs_2_, f32[264,128]{1,0:T(8,128)S(1)} %get-tuple-element.65.refs_2_.refs_3_, ...), custom_call_target="tpu_custom_call" | custom-call | flops 1 | bytes 1 | tf_op jit(solution)/shard_map/pallas_call | solution.py:310
  36.8 0.7 %shard_map.71.refs_0_ = f32[2,32,896]{2,1,0:T(8,128)S(1)} custom-call(s32[1]{0:T(128)} %bitcast.me_ref, bf16[32,1024]{1,0:T(8,128)(2,1)S(1)} %shard_map.70.heads_ref, bf16[1024,7168]{1,0:T(8,128)(2,1)S(1)} %bitcast.3), custom_call_target="tpu_custom_call" | custom-call | flops 5000000000 | bytes 1 | tf_op jit(solution)/shard_map/pallas_call | solution.py:331
  37.6 0.7 %shard_map.72.own_ref = f32[2,32,896]{2,1,0:T(8,128)S(1)} custom-call(s32[1]{0:T(128)} %bitcast.me_ref, bf16[32,1024]{1,0:T(8,128)(2,1)S(1)} %shard_map.70.heads_ref, bf16[1024,7168]{1,0:T(8,128)(2,1)S(1)} %bitcast.3, f32[2,32,896]{2,1,0:T(8,128)S(1)} %shard_map.71.refs_0_), custom_call_target="tpu_custom_call" | custom-call | flops 5000000000 | bytes 1 | tf_op jit(solution)/shard_map/pallas_call | solution.py:331
  38.4 0.7 %collective-permute-done.12.got_ref = f32[2,32,896]{2,1,0:T(8,128)S(1)} collective-permute-done((f32[2,32,896]{2,1,0:T(8,128)S(1)}, f32[2,32,896]{2,1,0:T(8,128)S(1)}, u32[]{:S(2)}, u32[]{:S(2)}) %collective-permute-start.12) | collective-permute-done | bytes 229408 | tf_op jit(solution)/shard_map/ppermute | solution.py:388
  39.1 1.5 %collective-permute-start.14 = (f32[32,896]{1,0:T(8,128)S(1)}, f32[32,896]{1,0:T(8,128)S(1)}, u32[]{:S(2)}, u32[]{:S(2)}) collective-permute-start(f32[32,896]{1,0:T(8,128)S(1)} %get-tuple-element.69.refs_0_), channel_id=1, source_target_pairs={{0,6},{1,7},{2,4},{3,5},{4,2},{5,3},{6,0},{7,1},{8,14},{9,15},{10,... | collective-permute-start | bytes 344072 | tf_op jit(solution)/shard_map/ppermute | solution.py:388
  40.6 0.7 %shard_map.74.refs_0_ = f32[2,32,896]{2,1,0:T(8,128)S(1)} custom-call(s32[1]{0:T(128)} %bitcast.me_ref, bf16[32,1024]{1,0:T(8,128)(2,1)S(1)} %shard_map.70.heads_ref, bf16[1024,7168]{1,0:T(8,128)(2,1)S(1)} %bitcast.3, f32[32,896]{1,0:T(8,128)S(1)} %get-tuple-element.69.refs_0_), custom_call_target="tpu_custom_call" | custom-call | flops 5000000000 | bytes 1 | tf_op jit(solution)/shard_map/pallas_call | solution.py:331
  41.4 0.7 %shard_map.75.own_ref = f32[2,32,896]{2,1,0:T(8,128)S(1)} custom-call(s32[1]{0:T(128)} %bitcast.me_ref, bf16[32,1024]{1,0:T(8,128)(2,1)S(1)} %shard_map.70.heads_ref, bf16[1024,7168]{1,0:T(8,128)(2,1)S(1)} %bitcast.3, f32[2,32,896]{2,1,0:T(8,128)S(1)} %shard_map.74.refs_0_), custom_call_target="tpu_custom_call" | custom-call | flops 5000000000 | bytes 1 | tf_op jit(solution)/shard_map/pallas_call | solution.py:331
  42.1 0.8 %collective-permute-start.15 = (f32[32,896]{1,0:T(8,128)S(1)}, f32[32,896]{1,0:T(8,128)S(1)}, u32[]{:S(2)}, u32[]{:S(2)}) collective-permute-start(f32[32,896]{1,0:T(8,128)S(1)} %get-tuple-element.71), channel_id=1, source_target_pairs={{0,2},{1,5},{2,0},{3,7},{4,6},{5,1},{6,4},{7,3},{8,10},{9,13},{10,... | collective-permute-start | bytes 344072 | tf_op jit(solution)/shard_map/ppermute | solution.py:388
  42.9 1.4 %collective-permute-start.16 = (f32[32,896]{1,0:T(8,128)S(1)}, f32[32,896]{1,0:T(8,128)S(1)}, u32[]{:S(2)}, u32[]{:S(2)}) collective-permute-start(f32[32,896]{1,0:T(8,128)S(1)} %get-tuple-element.72), channel_id=1, source_target_pairs={{0,4},{1,3},{2,6},{3,1},{4,0},{5,7},{6,2},{7,5},{8,12},{9,11},{10,... | collective-permute-start | bytes 344072 | tf_op jit(solution)/shard_map/ppermute | solution.py:388
  44.4 3.8 %collective-permute-done.15.refs_2_ = f32[32,896]{1,0:T(8,128)S(1)} collective-permute-done((f32[32,896]{1,0:T(8,128)S(1)}, f32[32,896]{1,0:T(8,128)S(1)}, u32[]{:S(2)}, u32[]{:S(2)}) %collective-permute-start.15) | collective-permute-done | bytes 114720 | tf_op jit(solution)/shard_map/ppermute | solution.py:388
  48.2 0.7 %shard_map.77 = bf16[8,4,896]{2,1,0:T(4,128)(2,1)} custom-call(f32[32,896]{1,0:T(8,128)S(1)} %get-tuple-element.70.refs_0_, f32[32,896]{1,0:T(8,128)S(1)} %collective-permute-done.14.refs_1_, f32[32,896]{1,0:T(8,128)S(1)} %collective-permute-done.15.refs_2_, f32[32,896]{1,0:T(8,128)S(1)} %collective-permute-done.16.refs_3_), custom_call_target="tpu_custom_call" | custom-call | flops 1 | bytes 1 | tf_op jit(solution)/shard_map/pallas_call | solution.py:369
  (36 shorter events, 2.6 us)
Async XLA Ops:
  3.8 3.4 %collective-permute-start = (f32[1032,128]{1,0:T(8,128)S(1)}, f32[1032,128]{1,0:T(8,128)S(1)}, u32[]{:S(2)}, u32[]{:S(2)}) collective-permute-start(f32[1032,128]{1,0:T(8,128)S(1)} %get-tuple-element.40), channel_id=1, source_target_pairs={{0,1},{1,0},{2,3},{3,2},{4,5},{5,4},{6,7},{7,6},{8,9},{9,8},{10,11... | collective-permute-start | bytes 1585160 | tf_op jit(solution)/shard_map/ppermute | solution.py:388
  7.1 6.3 %collective-permute-start.3 = (f32[1032,128]{1,0:T(8,128)S(1)}, f32[1032,128]{1,0:T(8,128)S(1)}, u32[]{:S(2)}, u32[]{:S(2)}) collective-permute-start(f32[1032,128]{1,0:T(8,128)S(1)} %get-tuple-element.52), channel_id=1, source_target_pairs={{0,1},{1,0},{2,3},{3,2},{4,5},{5,4},{6,7},{7,6},{8,9},{9,8},{10,11... | collective-permute-start | bytes 1585160 | tf_op jit(solution)/shard_map/ppermute | solution.py:388
  7.5 11.0 %collective-permute-start.1 = (f32[520,128]{1,0:T(8,128)S(1)}, f32[520,128]{1,0:T(8,128)S(1)}, u32[]{:S(2)}, u32[]{:S(2)}) collective-permute-start(f32[520,128]{1,0:T(8,128)S(1)} %get-tuple-element.45), channel_id=1, source_target_pairs={{0,2},{1,5},{2,0},{3,7},{4,6},{5,1},{6,4},{7,3},{8,10},{9,13},{10,... | collective-permute-start | bytes 798728 | tf_op jit(solution)/shard_map/ppermute | solution.py:388
  13.3 4.8 %collective-permute-start.2 = (f32[1032,128]{1,0:T(8,128)S(1)}, f32[1032,128]{1,0:T(8,128)S(1)}, u32[]{:S(2)}, u32[]{:S(2)}) collective-permute-start(f32[1032,128]{1,0:T(8,128)S(1)} %get-tuple-element.49), channel_id=1, source_target_pairs={{0,1},{1,0},{2,3},{3,2},{4,5},{5,4},{6,7},{7,6},{8,9},{9,8},{10,11... | collective-permute-start | bytes 1585160 | tf_op jit(solution)/shard_map/ppermute | solution.py:388
  13.8 8.3 %collective-permute-start.8 = (f32[520,128]{1,0:T(8,128)S(1)}, f32[520,128]{1,0:T(8,128)S(1)}, u32[]{:S(2)}, u32[]{:S(2)}) collective-permute-start(f32[520,128]{1,0:T(8,128)S(1)} %get-tuple-element.62), channel_id=1, source_target_pairs={{0,4},{1,3},{2,6},{3,1},{4,0},{5,7},{6,2},{7,5},{8,12},{9,11},{10,... | collective-permute-start | bytes 798728 | tf_op jit(solution)/shard_map/ppermute | solution.py:388
  18.1 3.1 %collective-permute-start.5 = (f32[1032,128]{1,0:T(8,128)S(1)}, f32[1032,128]{1,0:T(8,128)S(1)}, u32[]{:S(2)}, u32[]{:S(2)}) collective-permute-start(f32[1032,128]{1,0:T(8,128)S(1)} %get-tuple-element.58), channel_id=1, source_target_pairs={{0,1},{1,0},{2,3},{3,2},{4,5},{5,4},{6,7},{7,6},{8,9},{9,8},{10,11... | collective-permute-start | bytes 1585160 | tf_op jit(solution)/shard_map/ppermute | solution.py:388
  18.9 13.0 %collective-permute-start.4 = (f32[264,128]{1,0:T(8,128)S(1)}, f32[264,128]{1,0:T(8,128)S(1)}, u32[]{:S(2)}, u32[]{:S(2)}) collective-permute-start(f32[264,128]{1,0:T(8,128)S(1)} %get-tuple-element.57), channel_id=1, source_target_pairs={{0,4},{1,3},{2,6},{3,1},{4,0},{5,7},{6,2},{7,5},{8,12},{9,11},{10,... | collective-permute-start | bytes 405512 | tf_op jit(solution)/shard_map/ppermute | solution.py:388
  19.6 9.3 %collective-permute-start.7 = (f32[520,128]{1,0:T(8,128)S(1)}, f32[520,128]{1,0:T(8,128)S(1)}, u32[]{:S(2)}, u32[]{:S(2)}) collective-permute-start(f32[520,128]{1,0:T(8,128)S(1)} %get-tuple-element.61), channel_id=1, source_target_pairs={{0,2},{1,5},{2,0},{3,7},{4,6},{5,1},{6,4},{7,3},{8,10},{9,13},{10,... | collective-permute-start | bytes 798728 | tf_op jit(solution)/shard_map/ppermute | solution.py:388
  21.5 9.3 %collective-permute-start.6 = (f32[520,128]{1,0:T(8,128)S(1)}, f32[520,128]{1,0:T(8,128)S(1)}, u32[]{:S(2)}, u32[]{:S(2)}) collective-permute-start(f32[520,128]{1,0:T(8,128)S(1)} %get-tuple-element.60), channel_id=1, source_target_pairs={{0,4},{1,3},{2,6},{3,1},{4,0},{5,7},{6,2},{7,5},{8,12},{9,11},{10,... | collective-permute-start | bytes 798728 | tf_op jit(solution)/shard_map/ppermute | solution.py:388
  22.4 9.7 %collective-permute-start.9 = (f32[264,128]{1,0:T(8,128)S(1)}, f32[264,128]{1,0:T(8,128)S(1)}, u32[]{:S(2)}, u32[]{:S(2)}) collective-permute-start(f32[264,128]{1,0:T(8,128)S(1)} %get-tuple-element.66), channel_id=1, source_target_pairs={{0,2},{1,5},{2,0},{3,7},{4,6},{5,1},{6,4},{7,3},{8,10},{9,13},{10,... | collective-permute-start | bytes 405512 | tf_op jit(solution)/shard_map/ppermute | solution.py:388
  28.9 7.9 %slice-start = ((s8[14680064]{0:T(1024)(128)(4,1)}), s8[4194304]{0:T(1024)(128)(4,1)S(1)}, s32[]{:S(2)}) async-start(s8[14680064]{0:T(1024)(128)(4,1)} %bitcast.2), calls=%async_computation | async-start | bytes 8388608
  29.2 6.1 %collective-permute-start.10 = (f32[264,128]{1,0:T(8,128)S(1)}, f32[264,128]{1,0:T(8,128)S(1)}, u32[]{:S(2)}, u32[]{:S(2)}) collective-permute-start(f32[264,128]{1,0:T(8,128)S(1)} %get-tuple-element.67), channel_id=1, source_target_pairs={{0,4},{1,3},{2,6},{3,1},{4,0},{5,7},{6,2},{7,5},{8,12},{9,11},{10,... | collective-permute-start | bytes 405512 | tf_op jit(solution)/shard_map/ppermute | solution.py:388
  30.8 6.0 %slice-start.1 = ((s8[14680064]{0:T(1024)(128)(4,1)}), s8[4194304]{0:T(1024)(128)(4,1)S(1)}, s32[]{:S(2)}) async-start(s8[14680064]{0:T(1024)(128)(4,1)} %bitcast.2), calls=%async_computation.1 | async-start | bytes 8388608
  30.8 6.0 %slice-start.2 = ((s8[14680064]{0:T(1024)(128)(4,1)}), s8[4194304]{0:T(1024)(128)(4,1)S(1)}, s32[]{:S(2)}) async-start(s8[14680064]{0:T(1024)(128)(4,1)} %bitcast.2), calls=%async_computation.2 | async-start | bytes 8388608
  30.9 6.0 %slice-start.3 = ((s8[14680064]{0:T(1024)(128)(4,1)}), s8[2097152]{0:T(1024)(128)(4,1)S(1)}, s32[]{:S(2)}) async-start(s8[14680064]{0:T(1024)(128)(4,1)} %bitcast.2), calls=%async_computation.3 | async-start | bytes 4194304
  31.2 5.1 %collective-permute-start.11 = (f32[264,128]{1,0:T(8,128)S(1)}, f32[264,128]{1,0:T(8,128)S(1)}, u32[]{:S(2)}, u32[]{:S(2)}) collective-permute-start(f32[264,128]{1,0:T(8,128)S(1)} %get-tuple-element.68), channel_id=1, source_target_pairs={{0,2},{1,5},{2,0},{3,7},{4,6},{5,1},{6,4},{7,3},{8,10},{9,13},{10,... | collective-permute-start | bytes 405512 | tf_op jit(solution)/shard_map/ppermute | solution.py:388
  31.8 4.4 %copy-start = (bf16[8,512,128]{2,1,0:T(8,128)(2,1)S(1)}, bf16[8,512,128]{2,1,0:T(8,128)(2,1)}, u32[]{:S(2)}) copy-start(bf16[8,512,128]{2,1,0:T(8,128)(2,1)} %refs_5_.1) | copy-start | bytes 3145732
  37.5 1.6 %collective-permute-start.12 = (f32[2,32,896]{2,1,0:T(8,128)S(1)}, f32[2,32,896]{2,1,0:T(8,128)S(1)}, u32[]{:S(2)}, u32[]{:S(2)}) collective-permute-start(f32[2,32,896]{2,1,0:T(8,128)S(1)} %shard_map.71.refs_0_), channel_id=1, source_target_pairs={{0,1},{1,0},{2,3},{3,2},{4,5},{5,4},{6,7},{7,6},{8,9},{9,8},{10,11... | collective-permute-start | bytes 688136 | tf_op jit(solution)/shard_map/ppermute | solution.py:388
  39.1 9.0 %collective-permute-start.14 = (f32[32,896]{1,0:T(8,128)S(1)}, f32[32,896]{1,0:T(8,128)S(1)}, u32[]{:S(2)}, u32[]{:S(2)}) collective-permute-start(f32[32,896]{1,0:T(8,128)S(1)} %get-tuple-element.69.refs_0_), channel_id=1, source_target_pairs={{0,6},{1,7},{2,4},{3,5},{4,2},{5,3},{6,0},{7,1},{8,14},{9,15},{10,... | collective-permute-start | bytes 344072 | tf_op jit(solution)/shard_map/ppermute | solution.py:388
  41.3 1.6 %collective-permute-start.13 = (f32[2,32,896]{2,1,0:T(8,128)S(1)}, f32[2,32,896]{2,1,0:T(8,128)S(1)}, u32[]{:S(2)}, u32[]{:S(2)}) collective-permute-start(f32[2,32,896]{2,1,0:T(8,128)S(1)} %shard_map.74.refs_0_), channel_id=1, source_target_pairs={{0,1},{1,0},{2,3},{3,2},{4,5},{5,4},{6,7},{7,6},{8,9},{9,8},{10,11... | collective-permute-start | bytes 688136 | tf_op jit(solution)/shard_map/ppermute | solution.py:388
  42.1 6.0 %collective-permute-start.15 = (f32[32,896]{1,0:T(8,128)S(1)}, f32[32,896]{1,0:T(8,128)S(1)}, u32[]{:S(2)}, u32[]{:S(2)}) collective-permute-start(f32[32,896]{1,0:T(8,128)S(1)} %get-tuple-element.71), channel_id=1, source_target_pairs={{0,2},{1,5},{2,0},{3,7},{4,6},{5,1},{6,4},{7,3},{8,10},{9,13},{10,... | collective-permute-start | bytes 344072 | tf_op jit(solution)/shard_map/ppermute | solution.py:388
  42.9 5.2 %collective-permute-start.16 = (f32[32,896]{1,0:T(8,128)S(1)}, f32[32,896]{1,0:T(8,128)S(1)}, u32[]{:S(2)}, u32[]{:S(2)}) collective-permute-start(f32[32,896]{1,0:T(8,128)S(1)} %get-tuple-element.72), channel_id=1, source_target_pairs={{0,4},{1,3},{2,6},{3,1},{4,0},{5,7},{6,2},{7,5},{8,12},{9,11},{10,... | collective-permute-start | bytes 344072 | tf_op jit(solution)/shard_map/ppermute | solution.py:388
